TPU v7x, 256 devices: a whole 4x4x8 slice. The times are simulated.
256 devices in a mesh: gx: 16 (over z_hi, y), gy: 16 (over z_lo, x, core).
Axes of the slice: x: 4, y: 4, z: 8 (z_hi: 4, z_lo: 2; z = z_hi * 2 + z_lo), core: 2. Of those that a mesh axis runs over, the one named last changes fastest.
Arguments:
- prior_kelvin_state: float32 [512, 512, 128], P('gx', 'gy'), may hold values from 0 to 6
- substance_identifier: int32 [512, 512, 128], P('gx', 'gy'), may hold values from 0 to 3
- chip_touch_indicator: int32 [512, 512, 128], P('gx', 'gy'), may hold values from 0 to 1
- substance_reference_diffusivity: float32 [4], replicated, may hold values from 1 to 8
- substance_diffusivity_gradient: float32 [4], replicated, may hold values from -0.5 to 0.5
- substance_storage_coefficient: float32 [4], replicated, may hold values from 0.5 to 2
- clearance_point_indices: int32 [262144], P(('gx', 'gy')), may hold values from 0 to 262143, as said below
- clearance_face_pressure: float32 [262144], P(('gx', 'gy')), may hold values from 0.5 to 2
Outputs:
- temperature: float32 [512, 512, 128], P('gx', 'gy')
- clearance_abrasion_growth: float32 [262144], P(('gx', 'gy'))
Inputs may be any that keep to these rules, and one draw needn't show every extreme that they name: `clearance_point_indices`: each surface cell i * 512 + j is named by exactly one flank site.
All inputs are finite; a program needn't handle non-finite values.
Results may differ from a plain program's by a relative error of at most 0.0001.
Values sent between devices are 32-bit elements; how exact they have to be, the bound alone decides.
No kernel may reach another device: no remote copies, remote signals or barrier semaphores. Data moves between devices by JAX's collectives and lax.ppermute only.
A program may use at most 64 MiB of HBM per device.

v0:
```python
import jax
import jax.numpy as jnp
from jax import lax
from jax.experimental import pallas as pl
from jax.experimental.pallas import tpu as pltpu
from jax.sharding import PartitionSpec as P

clock_advance = 2.0
interface_warming_rate = 3.0
usui_rate = 3.0
usui_energy = 4.0
kelvin_shift_amount = 2.0

LOW = 3
HIGH = 4
NX = 32
NY = 32
NZ = 128
PX = NX + HIGH + LOW
PY = NY + 8
FIELDS = 4
TILE = 8
PAIRS = 20
VMEM_LIMIT = 48 * 1024 * 1024
f32 = jnp.float32


def shift_pairs(count):
    forward = [(i, i + 1) for i in range(count - 1)]
    backward = [(target, source) for source, target in forward]
    return forward, backward


def sublane(shape):
    return lax.broadcasted_iota(jnp.int32, shape, len(shape) - 2)


def lane(shape):
    return lax.broadcasted_iota(jnp.int32, shape, len(shape) - 1)


def pack_tile(low_sub, t_first, id_first, t_last, id_last, chip_last):
    to_low = jnp.where(low_sub < 4, t_first, pltpu.roll(id_first, 4, 0))
    to_high = jnp.where(
        low_sub >= 5,
        t_last,
        jnp.where(low_sub >= 2, pltpu.roll(id_last, 5, 0), pltpu.roll(chip_last, 2, 0)),
    )
    return to_low, to_high


def pack_kernel(t_ref, id_ref, chip_ref, xp_ref, xm_ref, low_ref, high_ref):
    sub = sublane((TILE, NZ))
    zero = jnp.zeros((TILE, NZ), f32)

    def chip_first(q):
        if q < NX:
            return chip_ref[q, 0:TILE, :].astype(f32)
        if q < NX + 3:
            return xp_ref[8 + q - NX, 0:TILE, :]
        if q in (37, 38):
            return xm_ref[6 + q - 37, 0:TILE, :]
        return zero

    def own(q, _):
        a, b = pack_tile(
            sub,
            t_ref[q, 0:TILE, :],
            id_ref[q, 0:TILE, :].astype(f32),
            t_ref[q, NY - TILE :, :],
            id_ref[q, NY - TILE :, :].astype(f32),
            chip_ref[q, NY - TILE :, :].astype(f32),
        )
        low_ref[q] = a
        high_ref[q] = b
        return 0

    lax.fori_loop(0, NX, own, 0, unroll=4)
    for k in range(HIGH):
        a, b = pack_tile(
            sub,
            xp_ref[k, 0:TILE, :],
            xp_ref[4 + k, 0:TILE, :],
            xp_ref[k, NY - TILE :, :],
            xp_ref[4 + k, NY - TILE :, :],
            xp_ref[8 + k, NY - TILE :, :] if k < 3 else zero,
        )
        low_ref[NX + k] = a
        high_ref[NX + k] = b
    for k in range(LOW):
        a, b = pack_tile(
            sub,
            xm_ref[k, 0:TILE, :],
            xm_ref[3 + k, 0:TILE, :],
            xm_ref[k, NY - TILE :, :],
            xm_ref[3 + k, NY - TILE :, :],
            xm_ref[5 + k, NY - TILE :, :] if k > 0 else zero,
        )
        low_ref[NX + HIGH + k] = a
        high_ref[NX + HIGH + k] = b
    for j in range(PAIRS):
        second = chip_first(j + PAIRS) if j + PAIRS < PX else zero
        low_ref[PX + j] = jnp.where(sub < 4, chip_first(j), pltpu.roll(second, 4, 0))


def krylov_kernel(
    ref_ref,
    grad_ref,
    store_ref,
    t_ref,
    id_ref,
    chip_ref,
    xp_ref,
    xm_ref,
    yp_ref,
    ym_ref,
    w0_ref,
    w1_ref,
    w2_ref,
    send_ref,
    tp,
    cp,
    capp,
    chp,
    ex,
    ey,
    ez,
    dinv,
):
    ix = lax.axis_index("gx")
    iy = lax.axis_index("gy")
    last_x = lax.axis_size("gx") - 1
    last_y = lax.axis_size("gy") - 1
    sub = sublane((TILE, NZ))
    one = jnp.ones((), f32)
    low_x = jnp.where(ix > 0, 1.0, 0.0).astype(f32)
    high_x = jnp.where(ix < last_x, 1.0, 0.0).astype(f32)
    low_y = jnp.where(iy > 0, 1.0, 0.0).astype(f32)
    high_y = jnp.where(iy < last_y, 1.0, 0.0).astype(f32)
    rows_halo = jnp.where(sub < 4, high_y, low_y)

    def pick(ident, table):
        low = jnp.where(ident == 1, table[1], table[0])
        high = jnp.where(ident == 3, table[3], table[2])
        return jnp.where(ident >= 2, high, low)

    def element(temp, ident):
        conduct = pick(ident, ref_ref) * (
            1.0 + pick(ident, grad_ref) * jnp.tanh(temp - kelvin_shift_amount)
        )
        return conduct, pick(ident, store_ref)

    rate = clock_advance * interface_warming_rate

    def halo_tile(q, chip_high):
        low = ym_ref[q]
        high = yp_ref[q]
        temp = jnp.where(sub < 4, high, low)
        ident = jnp.where(sub < 4, pltpu.roll(high, 4, 0), pltpu.roll(low, 3, 0))
        chip = jnp.where(sub < 4, chip_high, pltpu.roll(low, 6, 0))
        return temp, ident, chip

    def put_halo(q, chip_high, plane_in):
        temp, ident, chip = halo_tile(q, chip_high)
        conduct, store = element(temp, ident)
        tp[q, NY:, :] = temp
        cp[q, NY:, :] = conduct * (rows_halo * plane_in)
        capp[q, NY:, :] = store
        chp[q, NY:, :] = rate * chip

    def own_plane(q, _):
        temp = t_ref[q]
        conduct, store = element(temp, id_ref[q])
        tp[q, :NY, :] = temp
        cp[q, :NY, :] = conduct
        capp[q, :NY, :] = store
        chp[q, :NY, :] = rate * chip_ref[q].astype(f32)
        return 0

    lax.fori_loop(0, NX, own_plane, 0, unroll=2)

    def own_halo_first(q, _):
        put_halo(q, yp_ref[PX + q], one)
        return 0

    def own_halo_second(q, _):
        put_halo(q, pltpu.roll(yp_ref[PX + q - PAIRS], 4, 0), one)
        return 0

    lax.fori_loop(0, PAIRS, own_halo_first, 0, unroll=4)
    lax.fori_loop(PAIRS, NX, own_halo_second, 0, unroll=4)

    zero_plane = jnp.zeros((NY, NZ), f32)

    def side_plane(q, temp, ident, chip, plane_in):
        conduct, store = element(temp, ident)
        tp[q, :NY, :] = temp
        cp[q, :NY, :] = conduct * plane_in
        capp[q, :NY, :] = store
        chp[q, :NY, :] = rate * chip
        put_halo(q, pltpu.roll(yp_ref[PX + q - PAIRS], 4, 0), plane_in)

    for k in range(HIGH):
        side_plane(
            NX + k, xp_ref[k], xp_ref[4 + k], xp_ref[8 + k] if k < 3 else zero_plane, high_x
        )
    for k in range(LOW):
        side_plane(
            NX + HIGH + k,
            xm_ref[k],
            xm_ref[3 + k],
            xm_ref[5 + k] if k > 0 else zero_plane,
            low_x,
        )

    lanes = lane((PY, NZ))
    subs = sublane((PY, NZ))
    inner_z = jnp.where(lanes < NZ - 1, 1.0, 0.0).astype(f32)
    edge_z = jnp.where((lanes == 0) | (lanes == NZ - 1), 1.0, 0.0).astype(f32)
    rows_in = jnp.where(subs < NY, 1.0, jnp.where(subs < NY + 4, high_y, low_y)).astype(f32)
    lane_tile = lane((TILE, NZ))

    def up_y(v):
        return pltpu.roll(v, PY - 1, 0)

    def down_y(v):
        return pltpu.roll(v, 1, 0)

    def up_z(v):
        return pltpu.roll(v, NZ - 1, 1)

    def down_z(v):
        return pltpu.roll(v, 1, 1)

    def fold(v):
        return (v[0:8] + v[8:16]) + (v[16:24] + v[24:32])

    def surface(acc, plane, x):
        for t in range(NY // TILE):
            part = plane[TILE * t : TILE * (t + 1)]
            acc = jnp.where(
                lane_tile == x * 4 + t, jnp.broadcast_to(part[:, 0:1], (TILE, NZ)), acc
            )
        return acc

    def faces(q, nxt, ex_before, fx_before, plane_in):
        c0 = cp[q]
        t0 = tp[q]
        e_x = c0 + cp[nxt]
        f_x = e_x * (tp[nxt] - t0)
        e_y = c0 + up_y(c0)
        f_y = e_y * (up_y(t0) - t0)
        e_z = (c0 + up_z(c0)) * inner_z
        f_z = e_z * (up_z(t0) - t0)
        c_b = c0 * edge_z
        diag = (capp[q] + c_b) + (
            (e_x + ex_before) + ((e_y + down_y(e_y)) + (e_z + down_z(e_z)))
        )
        inverse = (rows_in * plane_in) / diag
        resid = (chp[q] - c_b * t0) + (
            (f_x - fx_before) + ((f_y - down_y(f_y)) + (f_z - down_z(f_z)))
        )
        first = resid * inverse
        ex[q] = e_x
        ey[q] = e_y
        ez[q] = e_z
        dinv[q] = inverse
        w0_ref[q] = first
        return e_x, f_x, resid, first

    zero_tile = jnp.zeros((TILE, NZ), f32)
    e_first = cp[36] + cp[37]
    carry = (e_first, e_first * (tp[37] - tp[36]))
    for q, nxt in ((37, 38), (38, 0)):
        carry = faces(q, nxt, carry[0], carry[1], low_x)[:2]

    def faces_own(q, state):
        e_b, f_b, m0, s_t, s_0 = state
        e_x, f_x, resid, first = faces(q, q + 1, e_b, f_b, one)
        m0 = m0 + fold(resid[:NY] * first[:NY])
        return e_x, f_x, m0, surface(s_t, tp[q, :NY, :], q), surface(s_0, first, q)

    e_b, f_b, m0, surf_t, surf_0 = lax.fori_loop(
        0, NX, faces_own, (carry[0], carry[1], zero_tile, zero_tile, zero_tile)
    )
    carry = (e_b, f_b)
    for q in (32, 33, 34):
        carry = faces(q, q + 1, carry[0], carry[1], high_x)[:2]

    def neighbours(src, q, nxt, g_before):
        v = src[q]
        e_x = ex[q]
        e_y = ey[q]
        e_z = ez[q]
        total = (e_x * src[nxt] + g_before) + (
            (e_y * up_y(v) + down_y(e_y * v)) + (e_z * up_z(v) + down_z(e_z * v))
        )
        return total, v, e_x * v

    def advance(src, dst, before, prologue, epilogue):
        carry = ex[before] * src[before]
        for q, nxt in prologue:
            total, _, carry = neighbours(src, q, nxt, carry)
            dst[q] = dinv[q] * total

        def step(q, state):
            g, ma, mb, surf = state
            total, v, g = neighbours(src, q, q + 1, g)
            new = dinv[q] * total
            dst[q] = new
            ma = ma + fold(total[:NY] * v[:NY])
            mb = mb + fold(total[:NY] * new[:NY])
            return g, ma, mb, surface(surf, new, q)

        carry, ma, mb, surf = lax.fori_loop(
            0, NX, step, (carry, zero_tile, zero_tile, zero_tile)
        )
        for q, nxt in epilogue:
            total, _, carry = neighbours(src, q, nxt, carry)
            dst[q] = dinv[q] * total
        return ma, mb, surf

    m1, m2, surf_1 = advance(w0_ref, w1_ref, 37, ((38, 0),), ((32, 33), (33, 34)))
    m3, m4, surf_2 = advance(w1_ref, w2_ref, 38, (), ((32, 33),))

    def last(q, acc):
        v = w2_ref[q]
        half = ex[q] * w2_ref[q + 1] + (ey[q] * up_y(v) + ez[q] * up_z(v))
        return acc + fold(half[:NY] * v[:NY])

    m5 = lax.fori_loop(0, NX, last, zero_tile)
    m5 = m5 + m5

    moments = zero_tile
    for k, m in enumerate((m0, m1, m2, m3, m4, m5)):
        moments = jnp.where(sub == k, jnp.sum(m, axis=0, keepdims=True), moments)
    for k in range(send_ref.shape[0]):
        for j, tile in enumerate((surf_t, surf_0, surf_1, surf_2, moments)):
            send_ref[k, TILE * j : TILE * (j + 1), :] = tile


def lookup_kernel(site_ref, table_ref, out_ref, row_s, lane_s):
    iy = lax.axis_index("gy")
    blocks = table_ref.shape[0]
    targets = site_ref.shape[0]
    width = NY * lax.axis_size("gy")
    group = 4

    def places(b, _):
        site = site_ref[b]
        row = site // width
        col = site - row * width
        here = (col // NY) == iy
        x = row % NX
        y = col % NY
        place = (row // NX) * TILE + y % TILE
        row_s[b] = jnp.where(here, place, -1)
        lane_s[b] = x * 4 + y // TILE
        return 0

    lax.fori_loop(0, targets, places, 0)

    zero = jnp.zeros((TILE, NZ), f32)

    def one_group(g, _):
        rows = [row_s[g * group + i] for i in range(group)]
        lanes = [lane_s[g * group + i] for i in range(group)]

        def one_block(a, acc):
            acc = list(acc)
            for s in range(TILE):
                r = a * TILE + s
                hit = [rows[i] == r for i in range(group)]
                for f in range(FIELDS):
                    line = jnp.broadcast_to(
                        table_ref[a, TILE * f + s : TILE * f + s + 1, :], (TILE, NZ)
                    )
                    for i in range(group):
                        got = jnp.take_along_axis(line, lanes[i], axis=1)
                        acc[f * group + i] = jnp.where(hit[i], got, acc[f * group + i])
            return tuple(acc)

        acc = lax.fori_loop(0, blocks, one_block, tuple([zero] * (FIELDS * group)))
        for i in range(group):
            for f in range(FIELDS):
                out_ref[g * group + i, TILE * f : TILE * (f + 1), :] = acc[f * group + i]
        return 0

    lax.fori_loop(0, targets // group, one_group, 0)

    def add(a, acc):
        return acc + table_ref[a, TILE * FIELDS :, :]

    total = lax.fori_loop(0, blocks, add, zero)
    for b in range(targets):
        out_ref[b, TILE * FIELDS :, :] = total


def cg_coefficients(m):
    a = [m[j] - m[j + 1] for j in range(5)]

    def quadratic(v, h):
        total = None
        for i in range(3):
            for j in range(3):
                if v[i] is None or v[j] is None:
                    continue
                term = v[i] * v[j] * h[i + j]
                total = term if total is None else total + term
        return total

    def add(u, v):
        return v if u is None else u if v is None else u + v

    def scale(s, v):
        return [None if e is None else s * e for e in v]

    one = jnp.ones_like(m[0])
    z = [one, None, None]
    p = [one, None, None]
    rz = m[0]
    x = [None, None, None]
    for step in range(3):
        alpha = rz / quadratic(p, a)
        x = [add(e, g) for e, g in zip(x, scale(alpha, p))]
        if step < 2:
            ap = scale(alpha, p)
            moved = [None] + ap[:2]
            z = [
                add(add(z[i], None if ap[i] is None else -ap[i]), moved[i]) for i in range(3)
            ]
            new = quadratic(z, m)
            p = [add(z[i], e) for i, e in enumerate(scale(new / rz, p))]
            rz = new
    return x


def final_kernel(got_ref, pressure_ref, t_ref, w0_ref, w1_ref, w2_ref, temp_ref, growth_ref):
    total = got_ref[0]
    for b in range(1, got_ref.shape[0]):
        total = total + got_ref[b]
    sums = jnp.sum(total[TILE * FIELDS :], axis=1, keepdims=True)
    m = [sums[k : k + 1] for k in range(6)]
    c = cg_coefficients(m)
    c_tile = [jnp.broadcast_to(e, (TILE, NZ)) for e in c]
    c_plane = [jnp.broadcast_to(e, (NY, NZ)) for e in c]
    flank = total[0:TILE]
    for k in range(3):
        flank = flank + c_tile[k] * total[TILE * (k + 1) : TILE * (k + 2)]
    soft = jnp.maximum(flank, 0.0) + jnp.log1p(jnp.exp(-jnp.abs(flank)))
    growth_ref[...] = usui_rate * pressure_ref[...] * jnp.exp(-usui_energy / (1.0 + soft))

    def plane(q, _):
        temp_ref[q] = (
            t_ref[q]
            + c_plane[0] * w0_ref[q]
            + c_plane[1] * w1_ref[q]
            + c_plane[2] * w2_ref[q]
        )
        return 0

    lax.fori_loop(0, NX, plane, 0, unroll=2)


def local(
    prior_kelvin_state,
    substance_identifier,
    chip_touch_indicator,
    substance_reference_diffusivity,
    substance_diffusivity_gradient,
    substance_storage_coefficient,
    clearance_point_indices,
    clearance_face_pressure,
):
    size_x = lax.axis_size("gx")
    size_y = lax.axis_size("gy")
    temp, ident, chip = prior_kelvin_state, substance_identifier, chip_touch_indicator
    vmem = pl.BlockSpec(memory_space=pltpu.VMEM)
    smem = pl.BlockSpec(memory_space=pltpu.SMEM)
    params = pltpu.CompilerParams(vmem_limit_bytes=VMEM_LIMIT)

    sites = lax.all_gather(clearance_point_indices, "gy")
    sites = sites.reshape(size_y, TILE, NZ)

    forward, backward = shift_pairs(size_x)
    to_low = jnp.concatenate(
        [temp[:HIGH], ident[:HIGH].astype(f32), chip[: HIGH - 1].astype(f32)], axis=0
    )
    to_high = jnp.concatenate(
        [temp[NX - LOW :], ident[NX - LOW :].astype(f32), chip[NX - LOW + 1 :].astype(f32)],
        axis=0,
    )
    xp = lax.ppermute(to_low, "gx", backward)
    xm = lax.ppermute(to_high, "gx", forward)

    low_rows, high_rows = pl.pallas_call(
        pack_kernel,
        name="pack_rows",
        in_specs=[vmem] * 5,
        out_specs=[vmem] * 2,
        out_shape=[
            jax.ShapeDtypeStruct((PX + PAIRS, TILE, NZ), f32),
            jax.ShapeDtypeStruct((PX, TILE, NZ), f32),
        ],
        compiler_params=params,
    )(temp, ident, chip, xp, xm)
    forward, backward = shift_pairs(size_y)
    yp = lax.ppermute(low_rows, "gy", backward)
    ym = lax.ppermute(high_rows, "gy", forward)

    padded = jax.ShapeDtypeStruct((PX, PY, NZ), f32)
    payload = TILE * (FIELDS + 1)
    w0, w1, w2, send = pl.pallas_call(
        krylov_kernel,
        name="krylov",
        in_specs=[smem] * 3 + [vmem] * 7,
        out_specs=[vmem] * 4,
        out_shape=[padded] * 3 + [jax.ShapeDtypeStruct((size_x, payload, NZ), f32)],
        scratch_shapes=[pltpu.VMEM((PX, PY, NZ), f32)] * 8,
        compiler_params=params,
    )(
        substance_reference_diffusivity,
        substance_diffusivity_gradient,
        substance_storage_coefficient,
        temp,
        ident,
        chip,
        xp,
        xm,
        yp,
        ym,
    )
    table = lax.all_to_all(send, "gx", 0, 0)
    found = pl.pallas_call(
        lookup_kernel,
        name="lookup",
        in_specs=[vmem] * 2,
        out_specs=vmem,
        out_shape=jax.ShapeDtypeStruct((size_y, payload, NZ), f32),
        scratch_shapes=[pltpu.VMEM((size_y, TILE, NZ), jnp.int32)] * 2,
        compiler_params=params,
    )(sites, table)
    got = lax.all_to_all(found, "gy", 0, 0)
    block = pl.BlockSpec((NX, NY, NZ), lambda i: (0, 0, 0))
    temperature, growth = pl.pallas_call(
        final_kernel,
        name="finish",
        grid=(1,),
        in_specs=[
            pl.BlockSpec((size_y, payload, NZ), lambda i: (0, 0, 0)),
            pl.BlockSpec((TILE, NZ), lambda i: (0, 0)),
            block,
            block,
            block,
            block,
        ],
        out_specs=[block, pl.BlockSpec((TILE, NZ), lambda i: (0, 0))],
        out_shape=[
            jax.ShapeDtypeStruct((NX, NY, NZ), f32),
            jax.ShapeDtypeStruct((TILE, NZ), f32),
        ],
        compiler_params=params,
    )(got, clearance_face_pressure.reshape(TILE, NZ), temp, w0, w1, w2)
    return temperature, growth.reshape(-1)


def solution(mesh):
    in_specs = (
        P("gx", "gy", None),
        P("gx", "gy", None),
        P("gx", "gy", None),
        P(),
        P(),
        P(),
        P(("gx", "gy")),
        P(("gx", "gy")),
    )
    out_specs = (P("gx", "gy", None), P(("gx", "gy")))
    return jax.shard_map(local, mesh=mesh, in_specs=in_specs, out_specs=out_specs, check_vma=False)
```

profile of v0, /device:TPU:1, one launch (start us, length us, event | category | flops | bytes accessed | tf_op | source)
XLA Modules:
  0.0 126.2 jit_solution(398160155508781844)
XLA Ops:
  0.6 0.8 slice_convert_fusion
  1.5 0.9 slice_convert_fusion.2
  2.4 1.3 %collective-permute-start = (f32[11,32,128]{2,1,0:T(8,128)S(1)}, f32[11,32,128]{2,1,0:T(8,128)S(1)}, u32[]{:S(2)}, u32[]{:S(2)}) collective-permute-start(f32[11,32,128]{2,1,0:T(8,128)S(1)} %pad_maximum_fusion), channel_id=1, source_target_pairs={{16,0},{32,16},{48,32},{64,48},{80,64},{96,80},{112,96},{128,112},... | collective-permute-start | bytes 540680 | tf_op jit(solution)/shard_map/ppermute | solution.py:493
  3.7 0.8 slice_convert_fusion.1
  4.5 0.8 slice_convert_fusion.3
  5.2 0.0 slice-done.1
  5.3 4.7 %collective-permute-start.1 = (f32[8,32,128]{2,1,0:T(8,128)S(1)}, f32[8,32,128]{2,1,0:T(8,128)S(1)}, u32[]{:S(2)}, u32[]{:S(2)}) collective-permute-start(f32[8,32,128]{2,1,0:T(8,128)S(1)} %pad_maximum_fusion.1), channel_id=1, source_target_pairs={{0,16},{16,32},{32,48},{48,64},{64,80},{80,96},{96,112},{112,128},... | collective-permute-start | bytes 393224 | tf_op jit(solution)/shard_map/ppermute | solution.py:494
  10.0 1.9 %collective-permute-done.1.xm_ref = f32[8,32,128]{2,1,0:T(8,128)S(1)} collective-permute-done((f32[8,32,128]{2,1,0:T(8,128)S(1)}, f32[8,32,128]{2,1,0:T(8,128)S(1)}, u32[]{:S(2)}, u32[]{:S(2)}) %collective-permute-start.1) | collective-permute-done | bytes 131104 | tf_op jit(solution)/shard_map/ppermute | solution.py:494
  11.9 0.0 collective-permute-done.xp_ref
  11.9 0.0 copy-done
  11.9 1.0 copy-done.1
  13.0 1.0 copy-done.2
  14.0 0.1 pack_rows.1
  14.1 0.0 copy-start.5
  14.1 0.0 copy-start.6
  14.1 0.0 copy-start.7
  14.1 5.7 %collective-permute-start.2 = (f32[59,8,128]{2,1,0:T(8,128)S(1)}, f32[59,8,128]{2,1,0:T(8,128)S(1)}, u32[]{:S(2)}, u32[]{:S(2)}) collective-permute-start(f32[59,8,128]{2,1,0:T(8,128)S(1)} %get-tuple-element.10), channel_id=1, source_target_pairs={{1,0},{2,1},{3,2},{4,3},{5,4},{6,5},{7,6},{8,7},{9,8},{10,9},{11,1... | collective-permute-start | bytes 725000 | tf_op jit(solution)/shard_map/ppermute | solution.py:508
  19.9 1.9 %collective-permute-start.3 = (f32[39,8,128]{2,1,0:T(8,128)S(1)}, f32[39,8,128]{2,1,0:T(8,128)S(1)}, u32[]{:S(2)}, u32[]{:S(2)}) collective-permute-start(f32[39,8,128]{2,1,0:T(8,128)S(1)} %get-tuple-element.11), channel_id=1, source_target_pairs={{0,1},{1,2},{2,3},{3,4},{4,5},{5,6},{6,7},{7,8},{8,9},{9,10},{10,1... | collective-permute-start | bytes 479240 | tf_op jit(solution)/shard_map/ppermute | solution.py:509
  21.8 2.2 %collective-permute-done.3.ym_ref = f32[39,8,128]{2,1,0:T(8,128)S(1)} collective-permute-done((f32[39,8,128]{2,1,0:T(8,128)S(1)}, f32[39,8,128]{2,1,0:T(8,128)S(1)}, u32[]{:S(2)}, u32[]{:S(2)}) %collective-permute-start.3) | collective-permute-done | bytes 159776 | tf_op jit(solution)/shard_map/ppermute | solution.py:509
  24.0 0.0 collective-permute-done.2.yp_ref
  24.0 0.0 copy-done.6
  24.0 21.4 %krylov.1 = (f32[39,40,128]{2,1,0:T(8,128)S(1)}, f32[39,40,128]{2,1,0:T(8,128)S(1)}, f32[39,40,128]{2,1,0:T(8,128)S(1)}, f32[16,40,128]{2,1,0:T(8,128)S(1)}) custom-call(f32[4]{0:T(128)S(1)} %copy-done.5, f32[4]{0:T(128)S(1)} %copy-done.6, f32[4]{0:T(128)S(1)} %copy-done.7, f32[32,32,128]{2,1,0:T(8,128)S(1)} %copy-done, s32[32,32,128]{2,1,0:T(8,128)S(1)} %copy-done.1, ...), custom_call_target="tpu_custom_call" | custom-call | tf_op jit(solution)/shard_map/krylov/pallas_call | solution.py:513
  45.4 0.0 copy-start.3
  45.4 0.7 copy-done.3
  46.1 17.3 %all-to-all-start = ((f32[16,40,128]{2,1,0:T(8,128)}), f32[16,40,128]{2,1,0:T(8,128)S(1)}, u32[]{:S(2)}, u32[]{:S(2)}) async-start(f32[16,40,128]{2,1,0:T(8,128)} %copy-done.3), calls=%async_computation | async-start | bytes 655360 | tf_op jit(solution)/shard_map/all_to_all | solution.py:533
  63.5 0.0 copy-done.8
  63.5 19.4 %all-gather = s32[16384]{0:T(1024)S(1)} all-gather(s32[1024]{0:T(1024)S(1)} %copy-done.8), channel_id=2, replica_groups=mesh['gx'=16,'gy'=16] {'gy'}, dimensions={0}, use_global_device_ids=true | all-gather | bytes 69632 | tf_op jit(solution)/shard_map/all_gather | solution.py:482
  82.9 0.0 all-to-all-done.table_ref
  82.9 27.7 %lookup.1 = f32[16,40,128]{2,1,0:T(8,128)S(1)} custom-call(s32[16,8,128]{2,1,0:T(8,128)S(1)} %bitcast.3, f32[16,40,128]{2,1,0:T(8,128)S(1)} %all-to-all-done.table_ref), custom_call_target="tpu_custom_call" | custom-call | tf_op jit(solution)/shard_map/lookup/pallas_call | solution.py:534
  110.6 13.6 %all_to_all.10.got_ref = f32[16,40,128]{2,1,0:T(8,128)S(1)} all-to-all(f32[16,40,128]{2,1,0:T(8,128)S(1)} %lookup.1), channel_id=1, replica_groups=mesh['gx'=16,'gy'=16] {'gy'}, dimensions={0} | all-to-all | bytes 655360 | tf_op jit(solution)/shard_map/all_to_all | solution.py:543
  124.2 0.7 copy-done.4
  124.9 1.3 %finish.1 = (f32[32,32,128]{2,1,0:T(8,128)}, f32[8,128]{1,0:T(8,128)}) custom-call(f32[16,40,128]{2,1,0:T(8,128)S(1)} %all_to_all.10.got_ref, f32[8,128]{1,0:T(8,128)S(1)} %bitcast.4, f32[32,32,128]{2,1,0:T(8,128)S(1)} %copy-done, f32[39,40,128]{2,1,0:T(8,128)S(1)} %get-tuple-element.13.w0_ref, f32[39,40,128]{2,1,0:T(8,128)S(1)} %get-tuple-element.14.w1_ref, ...), custom_call_target="tpu_custom_call" | custom-call | tf_op jit(solution)/shard_map/finish/pallas_call | solution.py:545
  (12 shorter events, 0.0 us)
Async XLA Ops:
  1.5 0.9 slice-start
  1.5 10.4 %copy-start = (f32[32,32,128]{2,1,0:T(8,128)S(1)}, f32[32,32,128]{2,1,0:T(8,128)}, u32[]{:S(2)}) copy-start(f32[32,32,128]{2,1,0:T(8,128)} %t_ref.5) | copy-start | bytes 1572868
  2.4 9.5 %collective-permute-start = (f32[11,32,128]{2,1,0:T(8,128)S(1)}, f32[11,32,128]{2,1,0:T(8,128)S(1)}, u32[]{:S(2)}, u32[]{:S(2)}) collective-permute-start(f32[11,32,128]{2,1,0:T(8,128)S(1)} %pad_maximum_fusion), channel_id=1, source_target_pairs={{16,0},{32,16},{48,32},{64,48},{80,64},{96,80},{112,96},{128,112},... | collective-permute-start | bytes 540680 | tf_op jit(solution)/shard_map/ppermute | solution.py:493
  4.5 0.8 slice-start.1
  5.3 6.6 %collective-permute-start.1 = (f32[8,32,128]{2,1,0:T(8,128)S(1)}, f32[8,32,128]{2,1,0:T(8,128)S(1)}, u32[]{:S(2)}, u32[]{:S(2)}) collective-permute-start(f32[8,32,128]{2,1,0:T(8,128)S(1)} %pad_maximum_fusion.1), channel_id=1, source_target_pairs={{0,16},{16,32},{32,48},{48,64},{64,80},{80,96},{96,112},{112,128},... | collective-permute-start | bytes 393224 | tf_op jit(solution)/shard_map/ppermute | solution.py:494
  11.9 1.0 copy-start.1
  13.0 1.0 copy-start.2
  14.1 9.9 %copy-start.5 = (f32[4]{0:T(128)S(1)}, f32[4]{0:T(128)}, u32[]{:S(2)}) copy-start(f32[4]{0:T(128)} %ref_ref.1) | copy-start | bytes 52
  14.1 9.9 %copy-start.6 = (f32[4]{0:T(128)S(1)}, f32[4]{0:T(128)}, u32[]{:S(2)}) copy-start(f32[4]{0:T(128)} %grad_ref.1) | copy-start | bytes 52
  14.1 9.9 %copy-start.7 = (f32[4]{0:T(128)S(1)}, f32[4]{0:T(128)}, u32[]{:S(2)}) copy-start(f32[4]{0:T(128)} %store_ref.1) | copy-start | bytes 52
  14.1 9.9 %collective-permute-start.2 = (f32[59,8,128]{2,1,0:T(8,128)S(1)}, f32[59,8,128]{2,1,0:T(8,128)S(1)}, u32[]{:S(2)}, u32[]{:S(2)}) collective-permute-start(f32[59,8,128]{2,1,0:T(8,128)S(1)} %get-tuple-element.10), channel_id=1, source_target_pairs={{1,0},{2,1},{3,2},{4,3},{5,4},{6,5},{7,6},{8,7},{9,8},{10,9},{11,1... | collective-permute-start | bytes 725000 | tf_op jit(solution)/shard_map/ppermute | solution.py:508
  19.9 4.1 %collective-permute-start.3 = (f32[39,8,128]{2,1,0:T(8,128)S(1)}, f32[39,8,128]{2,1,0:T(8,128)S(1)}, u32[]{:S(2)}, u32[]{:S(2)}) collective-permute-start(f32[39,8,128]{2,1,0:T(8,128)S(1)} %get-tuple-element.11), channel_id=1, source_target_pairs={{0,1},{1,2},{2,3},{3,4},{4,5},{5,6},{6,7},{7,8},{8,9},{9,10},{10,1... | collective-permute-start | bytes 479240 | tf_op jit(solution)/shard_map/ppermute | solution.py:509
  45.4 0.7 copy-start.3
  46.1 17.3 %copy-start.8 = (s32[1024]{0:T(1024)S(1)}, s32[1024]{0:T(1024)}, u32[]{:S(2)}) copy-start(s32[1024]{0:T(1024)} %param.14) | copy-start | bytes 12292
  46.1 36.7 %all-to-all-start = ((f32[16,40,128]{2,1,0:T(8,128)}), f32[16,40,128]{2,1,0:T(8,128)S(1)}, u32[]{:S(2)}, u32[]{:S(2)}) async-start(f32[16,40,128]{2,1,0:T(8,128)} %copy-done.3), calls=%async_computation | async-start | bytes 655360 | tf_op jit(solution)/shard_map/all_to_all | solution.py:533
  124.2 0.7 copy-start.4
where the time goes:
time: 127 us; the launch traced here: 126 us
  Pallas kernels  50.5 us (40%)
  blocking collectives  33 us (26%)
  starting transfers between devices  30.9 us (24%)
  waiting for transfers between devices  4.13 us (3%)
  local copies, waits for them, and re-layouts  3.56 us (3%)
  other arithmetic  3.31 us (3%)
    pallas_call x1, Pallas kernels, local(): pl.pallas_call(lookup_kernel, name='lookup', in_specs=[vmem] * 2, out_spe...  27.7 us
    pallas_call x1, Pallas kernels, local(): pl.pallas_call(krylov_kernel, name='krylov', in_specs=[smem] * 3 + [vmem]...  21.4 us
    all_gather x1, blocking collectives, local(): sites = lax.all_gather(clearance_point_indices, 'gy')  19.4 us
    all_to_all x1, starting transfers between devices, local(): table = lax.all_to_all(send, 'gx', 0, 0)  17.3 us
    all_to_all x1, blocking collectives, local(): got = lax.all_to_all(found, 'gy', 0, 0)  13.6 us
    ppermute x1, starting transfers between devices, local(): yp = lax.ppermute(low_rows, 'gy', backward)  5.74 us
    ppermute x1, starting transfers between devices, local(): xm = lax.ppermute(to_high, 'gx', forward)  4.67 us
    unnamed x18, local copies, waits for them, and re-layouts  3.52 us
  transfers between devices with their start and end apart: 5, of which 2 were waited for; matrix products, arithmetic and copies ran while one was open for 1% of the time, Pallas kernels for 0%

commit v1 on v0

v1 whole, which is shorter than its diff:
```python
import jax
import jax.numpy as jnp
from jax import lax
from jax.experimental import pallas as pl
from jax.experimental.pallas import tpu as pltpu
from jax.sharding import PartitionSpec as P

clock_advance = 2.0
interface_warming_rate = 3.0
usui_rate = 3.0
usui_energy = 4.0
kelvin_shift_amount = 2.0

LOW = 3
HIGH = 4
NX = 32
NY = 32
NZ = 128
PX = NX + HIGH + LOW
PY = NY + 8
FIELDS = 4
TILE = 8
PAIRS = 16
MIB = 1024 * 1024
f32 = jnp.float32
bf16 = jnp.bfloat16


def sublane(shape):
    return lax.broadcasted_iota(jnp.int32, shape, len(shape) - 2)


def lane(shape):
    return lax.broadcasted_iota(jnp.int32, shape, len(shape) - 1)


def pack_kernel(
    t_hbm,
    id_hbm,
    chip_hbm,
    x_low,
    x_high,
    y_low,
    y_high,
    low_low,
    low_high,
    high_low,
    high_high,
    t_a,
    t_b,
    i_a,
    i_b,
    c_a,
    c_b,
    t_p,
    t_m,
    i_p,
    i_m,
    c_p,
    c_m,
    sems,
):
    copies = []
    for k, (src, dst) in enumerate(
        (
            (t_hbm.at[pl.ds(0, HIGH)], t_p),
            (id_hbm.at[pl.ds(0, HIGH)], i_p),
            (chip_hbm.at[pl.ds(0, HIGH)], c_p),
            (t_hbm.at[pl.ds(NX - HIGH, HIGH)], t_m),
            (id_hbm.at[pl.ds(NX - HIGH, HIGH)], i_m),
            (chip_hbm.at[pl.ds(NX - HIGH, HIGH)], c_m),
            (t_hbm.at[:, pl.ds(0, TILE)], t_a),
            (id_hbm.at[:, pl.ds(0, TILE)], i_a),
            (chip_hbm.at[:, pl.ds(0, TILE)], c_a),
            (t_hbm.at[:, pl.ds(NY - TILE, TILE)], t_b),
            (id_hbm.at[:, pl.ds(NY - TILE, TILE)], i_b),
            (chip_hbm.at[:, pl.ds(NY - TILE, TILE)], c_b),
        )
    ):
        copies.append(pltpu.make_async_copy(src, dst, sems.at[k]))
        copies[-1].start()
    for copy in copies:
        copy.wait()

    sub = sublane((TILE, NZ))
    for k in range(HIGH):
        x_low[k] = t_p[k]
        x_low[4 + k] = i_p[k].astype(f32)
        if k < 3:
            x_low[8 + k] = c_p[k].astype(f32)
            x_high[k] = t_m[1 + k]
            x_high[3 + k] = i_m[1 + k].astype(f32)
        if k < 2:
            x_high[6 + k] = c_m[2 + k].astype(f32)

    def first_rows(q):
        return jnp.where(sub < 4, t_a[q], pltpu.roll(i_a[q].astype(f32), 4, 0))

    def last_rows(q):
        return jnp.where(
            sub >= 5,
            t_b[q],
            jnp.where(
                sub >= 2,
                pltpu.roll(i_b[q].astype(f32), 5, 0),
                pltpu.roll(c_b[q].astype(f32), 2, 0),
            ),
        )

    def own(q, _):
        y_low[q] = first_rows(q)
        y_high[q] = last_rows(q)
        return 0

    lax.fori_loop(0, NX, own, 0, unroll=8)

    def pair(j, _):
        y_low[NX + j] = jnp.where(
            sub < 4, c_a[j].astype(f32), pltpu.roll(c_a[j + PAIRS].astype(f32), 4, 0)
        )
        return 0

    lax.fori_loop(0, PAIRS, pair, 0, unroll=8)
    for k in range(HIGH):
        low_low[k] = first_rows(k)
        low_high[k] = last_rows(k)
        if k < 3:
            low_low[4 + k] = c_a[k].astype(f32)
            high_low[k] = first_rows(NX - 3 + k)
            high_high[k] = last_rows(NX - 3 + k)
        if k < 2:
            high_low[3 + k] = c_a[NX - 2 + k].astype(f32)


def pick(ident, table):
    low = jnp.where(ident == 1, table[1], table[0])
    high = jnp.where(ident == 3, table[3], table[2])
    return jnp.where(ident >= 2, high, low)


def element(temp, ident, ref_ref, grad_ref, store_ref):
    conduct = pick(ident, ref_ref) * (
        1.0 + pick(ident, grad_ref) * jnp.tanh(temp - kelvin_shift_amount)
    )
    return conduct, pick(ident, store_ref)


def own_kernel(ref_ref, grad_ref, store_ref, t_ref, id_ref, chip_ref, tp, cp, capp, chp):
    def own_plane(q, _):
        temp = t_ref[q]
        conduct, store = element(temp, id_ref[q], ref_ref, grad_ref, store_ref)
        tp[q, :NY, :] = temp
        cp[q, :NY, :] = conduct
        capp[q, :NY, :] = store
        chp[q, :NY, :] = clock_advance * interface_warming_rate * chip_ref[q].astype(f32)
        return 0

    lax.fori_loop(0, NX, own_plane, 0, unroll=4)


def krylov_kernel(
    ref_ref,
    grad_ref,
    store_ref,
    tp_in,
    cp_in,
    capp_in,
    chp_in,
    xp_ref,
    xm_ref,
    yp_ref,
    ym_ref,
    pp_ref,
    pm_ref,
    mp_ref,
    mm_ref,
    tp,
    cp,
    capp,
    chp,
    w0_ref,
    w1_ref,
    w2_ref,
    send_ref,
    ex,
    ey,
    ez,
    dinv,
):
    del tp_in, cp_in, capp_in, chp_in
    ix = lax.axis_index("gx")
    iy = lax.axis_index("gy")
    last_x = lax.axis_size("gx") - 1
    last_y = lax.axis_size("gy") - 1
    sub = sublane((TILE, NZ))
    one = jnp.ones((), f32)
    low_x = jnp.where(ix > 0, 1.0, 0.0).astype(f32)
    high_x = jnp.where(ix < last_x, 1.0, 0.0).astype(f32)
    low_y = jnp.where(iy > 0, 1.0, 0.0).astype(f32)
    high_y = jnp.where(iy < last_y, 1.0, 0.0).astype(f32)
    rows_halo = jnp.where(sub < 4, high_y, low_y)
    rate = clock_advance * interface_warming_rate

    def put_halo(q, high, low, chip_high, plane_in):
        temp = jnp.where(sub < 4, high, low)
        ident = jnp.where(sub < 4, pltpu.roll(high, 4, 0), pltpu.roll(low, 3, 0))
        chip = jnp.where(sub < 4, chip_high, pltpu.roll(low, 6, 0))
        conduct, store = element(temp, ident, ref_ref, grad_ref, store_ref)
        tp[q, NY:, :] = temp
        cp[q, NY:, :] = conduct * (rows_halo * plane_in)
        capp[q, NY:, :] = store
        chp[q, NY:, :] = rate * chip

    def own_halo(j, _):
        chips = yp_ref[NX + j]
        put_halo(j, yp_ref[j], ym_ref[j], chips, one)
        q = j + PAIRS
        put_halo(q, yp_ref[q], ym_ref[q], pltpu.roll(chips, 4, 0), one)
        return 0

    lax.fori_loop(0, PAIRS, own_halo, 0, unroll=4)

    zero_plane = jnp.zeros((NY, NZ), f32)
    zero_tile = jnp.zeros((TILE, NZ), f32)

    def side_plane(q, temp, ident, chip, high, low, chip_high, plane_in):
        conduct, store = element(temp, ident, ref_ref, grad_ref, store_ref)
        tp[q, :NY, :] = temp
        cp[q, :NY, :] = conduct * plane_in
        capp[q, :NY, :] = store
        chp[q, :NY, :] = rate * chip
        put_halo(q, high, low, chip_high, plane_in)

    for k in range(HIGH):
        side_plane(
            NX + k,
            xp_ref[k],
            xp_ref[4 + k],
            xp_ref[8 + k] if k < 3 else zero_plane,
            pp_ref[k],
            pm_ref[k],
            pp_ref[4 + k] if k < 3 else zero_tile,
            high_x,
        )
    for k in range(LOW):
        side_plane(
            NX + HIGH + k,
            xm_ref[k],
            xm_ref[3 + k],
            xm_ref[5 + k] if k > 0 else zero_plane,
            mp_ref[k],
            mm_ref[k],
            mp_ref[2 + k] if k > 0 else zero_tile,
            low_x,
        )

    lanes = lane((PY, NZ))
    subs = sublane((PY, NZ))
    inner_z = jnp.where(lanes < NZ - 1, 1.0, 0.0).astype(f32)
    edge_z = jnp.where((lanes == 0) | (lanes == NZ - 1), 1.0, 0.0).astype(f32)
    rows_in = jnp.where(subs < NY, 1.0, jnp.where(subs < NY + 4, high_y, low_y)).astype(f32)
    lane_tile = lane((TILE, NZ))

    def up_y(v):
        return pltpu.roll(v, PY - 1, 0)

    def down_y(v):
        return pltpu.roll(v, 1, 0)

    def up_z(v):
        return pltpu.roll(v, NZ - 1, 1)

    def down_z(v):
        return pltpu.roll(v, 1, 1)

    def fold(v):
        return (v[0:8] + v[8:16]) + (v[16:24] + v[24:32])

    def surface(acc, plane, x):
        for t in range(NY // TILE):
            part = plane[TILE * t : TILE * (t + 1)]
            acc = jnp.where(
                lane_tile == x * 4 + t, jnp.broadcast_to(part[:, 0:1], (TILE, NZ)), acc
            )
        return acc

    def faces(q, nxt, ex_before, fx_before, plane_in):
        c0 = cp[q]
        t0 = tp[q]
        e_x = c0 + cp[nxt]
        f_x = e_x * (tp[nxt] - t0)
        e_y = c0 + up_y(c0)
        f_y = e_y * (up_y(t0) - t0)
        e_z = (c0 + up_z(c0)) * inner_z
        f_z = e_z * (up_z(t0) - t0)
        c_b = c0 * edge_z
        diag = (capp[q] + c_b) + (
            (e_x + ex_before) + ((e_y + down_y(e_y)) + (e_z + down_z(e_z)))
        )
        inverse = (rows_in * plane_in) / diag
        resid = (chp[q] - c_b * t0) + (
            (f_x - fx_before) + ((f_y - down_y(f_y)) + (f_z - down_z(f_z)))
        )
        first = resid * inverse
        ex[q] = e_x
        ey[q] = e_y
        ez[q] = e_z
        dinv[q] = inverse
        w0_ref[q] = first
        return e_x, f_x, resid, first

    e_first = cp[36] + cp[37]
    carry = (e_first, e_first * (tp[37] - tp[36]))
    for q, nxt in ((37, 38), (38, 0)):
        carry = faces(q, nxt, carry[0], carry[1], low_x)[:2]

    def faces_own(q, state):
        e_b, f_b, m0, s_t, s_0 = state
        e_x, f_x, resid, first = faces(q, q + 1, e_b, f_b, one)
        m0 = m0 + fold(resid[:NY] * first[:NY])
        return e_x, f_x, m0, surface(s_t, tp[q, :NY, :], q), surface(s_0, first, q)

    e_b, f_b, m0, surf_t, surf_0 = lax.fori_loop(
        0, NX, faces_own, (carry[0], carry[1], zero_tile, zero_tile, zero_tile), unroll=8
    )
    carry = (e_b, f_b)
    for q in (32, 33, 34):
        carry = faces(q, q + 1, carry[0], carry[1], high_x)[:2]

    def neighbours(src, q, nxt, g_before):
        v = src[q]
        e_x = ex[q]
        e_y = ey[q]
        e_z = ez[q]
        total = (e_x * src[nxt] + g_before) + (
            (e_y * up_y(v) + down_y(e_y * v)) + (e_z * up_z(v) + down_z(e_z * v))
        )
        return total, v, e_x * v

    def advance(src, dst, before, prologue, epilogue):
        carry = ex[before] * src[before]
        for q, nxt in prologue:
            total, _, carry = neighbours(src, q, nxt, carry)
            dst[q] = dinv[q] * total

        def step(q, state):
            g, ma, mb, surf = state
            total, v, g = neighbours(src, q, q + 1, g)
            new = dinv[q] * total
            dst[q] = new
            ma = ma + fold(total[:NY] * v[:NY])
            mb = mb + fold(total[:NY] * new[:NY])
            return g, ma, mb, surface(surf, new, q)

        carry, ma, mb, surf = lax.fori_loop(
            0, NX, step, (carry, zero_tile, zero_tile, zero_tile), unroll=8
        )
        for q, nxt in epilogue:
            total, _, carry = neighbours(src, q, nxt, carry)
            dst[q] = dinv[q] * total
        return ma, mb, surf

    m1, m2, surf_1 = advance(w0_ref, w1_ref, 37, ((38, 0),), ((32, 33), (33, 34)))
    m3, m4, surf_2 = advance(w1_ref, w2_ref, 38, (), ((32, 33),))

    def last(q, acc):
        v = w2_ref[q]
        half = ex[q] * w2_ref[q + 1] + (ey[q] * up_y(v) + ez[q] * up_z(v))
        return acc + fold(half[:NY] * v[:NY])

    m5 = lax.fori_loop(0, NX, last, zero_tile, unroll=8)
    m5 = m5 + m5

    moments = zero_tile
    for k, m in enumerate((m0, m1, m2, m3, m4, m5)):
        moments = jnp.where(sub == k, jnp.sum(m, axis=0, keepdims=True), moments)
    for k in range(send_ref.shape[0]):
        for j, tile in enumerate((surf_t, surf_0, surf_1, surf_2, moments)):
            send_ref[k, TILE * j : TILE * (j + 1), :] = tile


def lookup_kernel(site_hbm, table_ref, out_ref, parts, site_ref, sem):
    copy = pltpu.make_async_copy(site_hbm.at[:, pl.ds(0, TILE)], site_ref, sem)
    copy.start()
    blocks = table_ref.shape[0]
    targets = site_ref.shape[0]
    iy = lax.axis_index("gy")
    width = NY * lax.axis_size("gy")
    sub = sublane((TILE, NZ))
    subs = sublane((NZ, NZ))
    zero = jnp.zeros((TILE, NZ), f32)
    fields = FIELDS - 1
    for f in range(fields):
        rest = jnp.concatenate(
            [table_ref[a, TILE * (f + 1) : TILE * (f + 2), :] for a in range(blocks)], axis=0
        ).T
        for k in range(2):
            part = rest.astype(bf16)
            parts[NZ * f : NZ * (f + 1), NZ * k : NZ * (k + 1)] = part
            rest = rest - part.astype(f32)

    total = table_ref[0, TILE * FIELDS :, :]
    for a in range(1, blocks):
        total = total + table_ref[a, TILE * FIELDS :, :]
    copy.wait()

    def one(b, _):
        site = site_ref[b]
        row = site // width
        col = site - row * width
        here = (col // NY) == iy
        y = col % NY
        row_of = jnp.where(here, (row // NX) * TILE + y % TILE, -1)
        lane_of = (row % NX) * (NY // TILE) + y // TILE
        hot = jnp.concatenate(
            [
                jnp.where(
                    subs == jnp.broadcast_to(row_of[s : s + 1], (NZ, NZ)), 1.0, 0.0
                ).astype(bf16)
                for s in range(TILE)
            ],
            axis=1,
        )
        hot = jnp.concatenate([hot, hot], axis=0)
        found = [zero] * FIELDS
        lines = [
            jnp.dot(parts[NZ * f : NZ * (f + 1)], hot, preferred_element_type=f32)
            for f in range(fields)
        ]
        for s in range(TILE):
            lanes = jnp.broadcast_to(lane_of[s : s + 1], (TILE, NZ))
            rows = jnp.broadcast_to(row_of[s : s + 1], (TILE, NZ)) - sub
            acc = [zero] * FIELDS
            for a in range(blocks):
                got = jnp.take_along_axis(table_ref[a, 0:TILE, :], lanes, axis=1)
                acc[0] = jnp.where(rows == a * TILE, got, acc[0])
            lanes = lanes - sub
            for t in range(NZ // TILE):
                hit = lanes == t * TILE
                for f in range(fields):
                    acc[f + 1] = jnp.where(
                        hit,
                        lines[f][TILE * t : TILE * (t + 1), NZ * s : NZ * (s + 1)],
                        acc[f + 1],
                    )
            for f in range(FIELDS):
                found[f] = jnp.where(sub == s, jnp.sum(acc[f], axis=0, keepdims=True), found[f])
        for f in range(FIELDS):
            out_ref[b, TILE * f : TILE * (f + 1), :] = found[f]
        out_ref[b, TILE * FIELDS :, :] = total
        return 0

    lax.fori_loop(0, targets, one, 0, unroll=2)


def cg_coefficients(m):
    a = [m[j] - m[j + 1] for j in range(5)]

    def quadratic(v, h):
        total = None
        for i in range(3):
            for j in range(3):
                if v[i] is None or v[j] is None:
                    continue
                term = v[i] * v[j] * h[i + j]
                total = term if total is None else total + term
        return total

    def add(u, v):
        return v if u is None else u if v is None else u + v

    def scale(s, v):
        return [None if e is None else s * e for e in v]

    one = jnp.ones_like(m[0])
    z = [one, None, None]
    p = [one, None, None]
    rz = m[0]
    x = [None, None, None]
    for step in range(3):
        alpha = rz / quadratic(p, a)
        x = [add(e, g) for e, g in zip(x, scale(alpha, p))]
        if step < 2:
            ap = scale(alpha, p)
            moved = [None] + ap[:2]
            z = [
                add(add(z[i], None if ap[i] is None else -ap[i]), moved[i]) for i in range(3)
            ]
            new = quadratic(z, m)
            p = [add(z[i], e) for i, e in enumerate(scale(new / rz, p))]
            rz = new
    return x


def final_kernel(
    got_ref, pressure_hbm, t_ref, w0_ref, w1_ref, w2_ref, temp_ref, growth_ref, pressure_ref, sem
):
    copy = pltpu.make_async_copy(pressure_hbm, pressure_ref, sem)
    copy.start()
    total = got_ref[0]
    for b in range(1, got_ref.shape[0]):
        total = total + got_ref[b]
    sums = jnp.sum(total[TILE * FIELDS :], axis=1, keepdims=True)
    m = [sums[k : k + 1] for k in range(6)]
    c = cg_coefficients(m)
    c_tile = [jnp.broadcast_to(e, (TILE, NZ)) for e in c]
    c_plane = [jnp.broadcast_to(e, (NY, NZ)) for e in c]
    flank = total[0:TILE]
    for k in range(3):
        flank = flank + c_tile[k] * total[TILE * (k + 1) : TILE * (k + 2)]
    soft = jnp.maximum(flank, 0.0) + jnp.log1p(jnp.exp(-jnp.abs(flank)))
    copy.wait()
    growth_ref[...] = usui_rate * pressure_ref[...] * jnp.exp(-usui_energy / (1.0 + soft))

    def plane(q, _):
        temp_ref[q] = (
            t_ref[q, :NY, :]
            + c_plane[0] * w0_ref[q, :NY, :]
            + c_plane[1] * w1_ref[q, :NY, :]
            + c_plane[2] * w2_ref[q, :NY, :]
        )
        return 0

    lax.fori_loop(0, NX, plane, 0, unroll=2)


def local(
    prior_kelvin_state,
    substance_identifier,
    chip_touch_indicator,
    substance_reference_diffusivity,
    substance_diffusivity_gradient,
    substance_storage_coefficient,
    clearance_point_indices,
    clearance_face_pressure,
):
    size_x = lax.axis_size("gx")
    size_y = lax.axis_size("gy")
    temp, ident, chip = prior_kelvin_state, substance_identifier, chip_touch_indicator
    vmem = pl.BlockSpec(memory_space=pltpu.VMEM)
    smem = pl.BlockSpec(memory_space=pltpu.SMEM)

    def params(mib):
        return pltpu.CompilerParams(vmem_limit_bytes=mib * MIB)


    sites = jnp.pad(clearance_point_indices.reshape(TILE, NZ), ((0, NZ - TILE), (0, 0)))
    sites = lax.all_gather(sites, "gy")

    anywhere = pl.BlockSpec(memory_space=pltpu.HBM)

    def arr(*shape, dtype=f32):
        return jax.ShapeDtypeStruct(shape, dtype)

    def buf(*shape, dtype=f32):
        return pltpu.VMEM(shape, dtype)

    def in_hbm(*arrays):
        return [pltpu.with_memory_space_constraint(a, pltpu.HBM) for a in arrays]

    i32 = jnp.int32
    packed = pl.pallas_call(
        pack_kernel,
        name="pack",
        in_specs=[anywhere] * 3,
        out_specs=[vmem] * 8,
        out_shape=[
            arr(11, NY, NZ),
            arr(8, NY, NZ),
            arr(NX + PAIRS, TILE, NZ),
            arr(NX, TILE, NZ),
            arr(7, TILE, NZ),
            arr(4, TILE, NZ),
            arr(5, TILE, NZ),
            arr(3, TILE, NZ),
        ],
        scratch_shapes=[
            buf(NX, TILE, NZ),
            buf(NX, TILE, NZ),
            buf(NX, TILE, NZ, dtype=i32),
            buf(NX, TILE, NZ, dtype=i32),
            buf(NX, TILE, NZ, dtype=i32),
            buf(NX, TILE, NZ, dtype=i32),
            buf(HIGH, NY, NZ),
            buf(HIGH, NY, NZ),
            buf(HIGH, NY, NZ, dtype=i32),
            buf(HIGH, NY, NZ, dtype=i32),
            buf(HIGH, NY, NZ, dtype=i32),
            buf(HIGH, NY, NZ, dtype=i32),
            pltpu.SemaphoreType.DMA((12,)),
        ],
        compiler_params=params(10),
    )(*in_hbm(temp, ident, chip))

    def shift(block, dx, dy):
        pairs = [
            (i * size_y + j, (i + dx) * size_y + j + dy)
            for i in range(size_x)
            for j in range(size_y)
            if 0 <= i + dx < size_x and 0 <= j + dy < size_y
        ]
        return lax.ppermute(block, ("gx", "gy"), pairs)

    moves = ((-1, 0), (1, 0), (0, -1), (0, 1), (-1, -1), (-1, 1), (1, -1), (1, 1))
    halos = [shift(block, dx, dy) for block, (dx, dy) in zip(packed, moves)]

    tables = (
        substance_reference_diffusivity,
        substance_diffusivity_gradient,
        substance_storage_coefficient,
    )
    padded = arr(PX, PY, NZ)
    own = pl.pallas_call(
        own_kernel,
        name="own_cells",
        in_specs=[smem] * 3 + [vmem] * 3,
        out_specs=[vmem] * 4,
        out_shape=[padded] * 4,
        compiler_params=params(12),
    )(*tables, temp, ident, chip)

    payload = TILE * (FIELDS + 1)
    start, _, _, _, w0, w1, w2, send = pl.pallas_call(
        krylov_kernel,
        name="krylov",
        in_specs=[smem] * 3 + [vmem] * 12,
        out_specs=[vmem] * 8,
        out_shape=[padded] * 7 + [arr(size_x, payload, NZ)],
        input_output_aliases={3: 0, 4: 1, 5: 2, 6: 3},
        scratch_shapes=[buf(PX, PY, NZ)] * 4,
        compiler_params=params(24),
    )(*tables, *own, *halos)
    table = lax.all_to_all(send, "gx", 0, 0)
    found = pl.pallas_call(
        lookup_kernel,
        name="lookup",
        in_specs=[anywhere, vmem],
        out_specs=vmem,
        out_shape=arr(size_y, payload, NZ),
        scratch_shapes=[
            buf(NZ * (FIELDS - 1), 2 * NZ, dtype=bf16),
            buf(size_y, TILE, NZ, dtype=i32),
            pltpu.SemaphoreType.DMA(()),
        ],
        compiler_params=params(20),
    )(*in_hbm(sites), table)
    got = lax.all_to_all(found, "gy", 0, 0)
    temperature, growth = pl.pallas_call(
        final_kernel,
        name="finish",
        in_specs=[vmem, anywhere, vmem, vmem, vmem, vmem],
        out_specs=[vmem] * 2,
        out_shape=[arr(NX, NY, NZ), arr(TILE, NZ)],
        scratch_shapes=[buf(TILE, NZ), pltpu.SemaphoreType.DMA(())],
        compiler_params=params(12),
    )(got, *in_hbm(clearance_face_pressure.reshape(TILE, NZ)), start, w0, w1, w2)
    return temperature, growth.reshape(-1)


def solution(mesh):
    in_specs = (
        P("gx", "gy", None),
        P("gx", "gy", None),
        P("gx", "gy", None),
        P(),
        P(),
        P(),
        P(("gx", "gy")),
        P(("gx", "gy")),
    )
    out_specs = (P("gx", "gy", None), P(("gx", "gy")))
    return jax.shard_map(local, mesh=mesh, in_specs=in_specs, out_specs=out_specs, check_vma=False)
```

time: 127 us -> 116 us (0.913)
  Pallas kernels: 50.5 us -> 17.6 us
  blocking collectives: 33 us -> 48.2 us
  between operations: 0.76 us -> 14.2 us
  starting transfers between devices: 30.9 us -> 19.9 us
  waiting for transfers between devices: 4.13 us -> 13.9 us
  other arithmetic: 3.31 us -> 0 us
  local copies, waits for them, and re-layouts: 3.56 us -> 1.35 us
    all_to_all x0 -> x1, blocking collectives: none -> 32.1 us  [local(): table = lax.all_to_all(send, 'gx', 0, 0)]
    all_gather x1 -> x0, blocking collectives: 19.4 us -> none  [local(): sites = lax.all_gather(clearance_point_indices, 'gy')]
    pallas_call x3 -> x4, Pallas kernels: 29.1 us -> 11.2 us  [the longest x1 6.95 us: local(): pl.pallas_call(lookup_kernel, name='lookup', in_specs=[anywhere, vmem], o...]
    all_to_all x1 -> x0, starting transfers between devices: 17.3 us -> none  [local(): table = lax.all_to_all(send, 'gx', 0, 0)]
    pallas_call x1, Pallas kernels: 21.4 us -> 6.42 us  [local(): pl.pallas_call(krylov_kernel, name='krylov', in_specs=[smem] * 3 + [vmem]...]
    ppermute x4 -> x8, waiting for transfers between devices: 4.13 us -> 13.9 us  [shift(): return lax.ppermute(block, ('gx', 'gy'), pairs)]
    ppermute x4 -> x8, starting transfers between devices: 13.6 us -> 19.8 us  [shift(): return lax.ppermute(block, ('gx', 'gy'), pairs)]
    unnamed x18 -> x12, local copies, waits for them, and re-layouts: 3.52 us -> 0.03 us
  transfers between devices with their start and end apart: 5 -> 9, of which waited for: 2 -> 4; matrix products, arithmetic and copies ran while one was open for 1% -> 0% of each run, Pallas kernels for 0% -> 8%
where the time goes in v1:
time: 116 us; the launch traced here: 115 us
  blocking collectives  48.2 us (42%)
  starting transfers between devices  19.9 us (17%)
  Pallas kernels  17.6 us (15%)
  between operations  14.2 us (12%)
  waiting for transfers between devices  13.9 us (12%)
  local copies, waits for them, and re-layouts  1.35 us (1%)
    all_to_all x1, blocking collectives, local(): table = lax.all_to_all(send, 'gx', 0, 0)  32.1 us
    ppermute x8, starting transfers between devices, shift(): return lax.ppermute(block, ('gx', 'gy'), pairs)  19.8 us
    all_to_all x1, blocking collectives, local(): got = lax.all_to_all(found, 'gy', 0, 0)  16.1 us
    ppermute x8, waiting for transfers between devices, shift(): return lax.ppermute(block, ('gx', 'gy'), pairs)  13.9 us
    pallas_call x1, Pallas kernels, local(): pl.pallas_call(lookup_kernel, name='lookup', in_specs=[anywhere, vmem], o...  6.95 us
    pallas_call x1, Pallas kernels, local(): pl.pallas_call(krylov_kernel, name='krylov', in_specs=[smem] * 3 + [vmem]...  6.42 us
  transfers between devices with their start and end apart: 9, of which 4 were waited for; matrix products, arithmetic and copies ran while one was open for 0% of the time, Pallas kernels for 8%

profile of v1, /device:TPU:1, one launch (start us, length us, event | category | flops | bytes accessed | tf_op | source)
XLA Modules:
  0.0 115.2 jit_solution(4025368312286819728)
XLA Ops:
  7.2 0.0 all-gather.3.cloned.1.call-start
  7.2 1.3 %pad.4 = s32[128,128]{1,0:T(8,128)} pad(s32[8,128]{1,0:T(8,128)} %bitcast.5, s32[]{:T(128)} %constant.0.clone.1), padding=0_120x0_0 | pad | bytes 69636 | tf_op jit(solution)/shard_map/jit(_pad)/pad | solution.py:547
  8.5 0.0 all-gather.3.cloned.1.call-update
  8.6 0.0 copy-start
  8.6 0.0 copy-start.1
  8.6 0.0 copy-start.2
  8.6 1.6 %pack.1 = (f32[11,32,128]{2,1,0:T(8,128)S(1)}, f32[8,32,128]{2,1,0:T(8,128)S(1)}, f32[48,8,128]{2,1,0:T(8,128)S(1)}, f32[32,8,128]{2,1,0:T(8,128)S(1)}, f32[7,8,...) custom-call(f32[32,32,128]{2,1,0:T(8,128)} %t_hbm.1, ...), custom_call_target="tpu_custom_call" | custom-call | tf_op jit(solution)/shard_map/pack/pallas_call | solution.py:562
  10.2 5.1 %collective-permute-start.2 = (f32[48,8,128]{2,1,0:T(8,128)S(1)}, f32[48,8,128]{2,1,0:T(8,128)S(1)}, u32[]{:S(2)}, u32[]{:S(2)}) collective-permute-start(f32[48,8,128]{2,1,0:T(8,128)S(1)} %get-tuple-element.27), channel_id=1, source_target_pairs={{1,0},{2,1},{3,2},{4,3},{5,4},{6,5},{7,6},{8,7},{9,8},{10,9},{11,1... | collective-permute-start | bytes 589832 | tf_op jit(solution)/shard_map/ppermute | solution.py:602
  15.4 1.3 %collective-permute-start = (f32[11,32,128]{2,1,0:T(8,128)S(1)}, f32[11,32,128]{2,1,0:T(8,128)S(1)}, u32[]{:S(2)}, u32[]{:S(2)}) collective-permute-start(f32[11,32,128]{2,1,0:T(8,128)S(1)} %get-tuple-element.25), channel_id=1, source_target_pairs={{16,0},{17,1},{18,2},{19,3},{20,4},{21,5},{22,6},{23,7},{24,8},{25... | collective-permute-start | bytes 540680 | tf_op jit(solution)/shard_map/ppermute | solution.py:602
  16.7 4.0 %collective-permute-start.1 = (f32[8,32,128]{2,1,0:T(8,128)S(1)}, f32[8,32,128]{2,1,0:T(8,128)S(1)}, u32[]{:S(2)}, u32[]{:S(2)}) collective-permute-start(f32[8,32,128]{2,1,0:T(8,128)S(1)} %get-tuple-element.26), channel_id=1, source_target_pairs={{0,16},{1,17},{2,18},{3,19},{4,20},{5,21},{6,22},{7,23},{8,24},{9,... | collective-permute-start | bytes 393224 | tf_op jit(solution)/shard_map/ppermute | solution.py:602
  20.7 1.9 %collective-permute-start.3 = (f32[32,8,128]{2,1,0:T(8,128)S(1)}, f32[32,8,128]{2,1,0:T(8,128)S(1)}, u32[]{:S(2)}, u32[]{:S(2)}) collective-permute-start(f32[32,8,128]{2,1,0:T(8,128)S(1)} %get-tuple-element.28), channel_id=1, source_target_pairs={{0,1},{1,2},{2,3},{3,4},{4,5},{5,6},{6,7},{7,8},{8,9},{9,10},{10,1... | collective-permute-start | bytes 393224 | tf_op jit(solution)/shard_map/ppermute | solution.py:602
  22.6 2.8 %collective-permute-start.7 = (f32[3,8,128]{2,1,0:T(8,128)S(1)}, f32[3,8,128]{2,1,0:T(8,128)S(1)}, u32[]{:S(2)}, u32[]{:S(2)}) collective-permute-start(f32[3,8,128]{2,1,0:T(8,128)S(1)} %get-tuple-element.32), channel_id=1, source_target_pairs={{0,17},{1,18},{2,19},{3,20},{4,21},{5,22},{6,23},{7,24},{8,25},{9,... | collective-permute-start | bytes 36872 | tf_op jit(solution)/shard_map/ppermute | solution.py:602
  25.5 0.8 collective-permute-done.7.mm_ref
  26.3 1.3 %collective-permute-start.5 = (f32[4,8,128]{2,1,0:T(8,128)S(1)}, f32[4,8,128]{2,1,0:T(8,128)S(1)}, u32[]{:S(2)}, u32[]{:S(2)}) collective-permute-start(f32[4,8,128]{2,1,0:T(8,128)S(1)} %get-tuple-element.30), channel_id=1, source_target_pairs={{16,1},{17,2},{18,3},{19,4},{20,5},{21,6},{22,7},{23,8},{24,9},{25... | collective-permute-start | bytes 49160 | tf_op jit(solution)/shard_map/ppermute | solution.py:602
  27.6 3.8 %collective-permute-done.5.pm_ref = f32[4,8,128]{2,1,0:T(8,128)S(1)} collective-permute-done((f32[4,8,128]{2,1,0:T(8,128)S(1)}, f32[4,8,128]{2,1,0:T(8,128)S(1)}, u32[]{:S(2)}, u32[]{:S(2)}) %collective-permute-start.5) | collective-permute-done | bytes 16416 | tf_op jit(solution)/shard_map/ppermute | solution.py:602
  31.4 2.1 %collective-permute-start.6 = (f32[5,8,128]{2,1,0:T(8,128)S(1)}, f32[5,8,128]{2,1,0:T(8,128)S(1)}, u32[]{:S(2)}, u32[]{:S(2)}) collective-permute-start(f32[5,8,128]{2,1,0:T(8,128)S(1)} %get-tuple-element.31), channel_id=1, source_target_pairs={{1,16},{2,17},{3,18},{4,19},{5,20},{6,21},{7,22},{8,23},{9,24},{10... | collective-permute-start | bytes 61448 | tf_op jit(solution)/shard_map/ppermute | solution.py:602
  33.5 0.9 collective-permute-done.6.mp_ref
  34.4 1.3 %collective-permute-start.4 = (f32[7,8,128]{2,1,0:T(8,128)S(1)}, f32[7,8,128]{2,1,0:T(8,128)S(1)}, u32[]{:S(2)}, u32[]{:S(2)}) collective-permute-start(f32[7,8,128]{2,1,0:T(8,128)S(1)} %get-tuple-element.29), channel_id=1, source_target_pairs={{17,0},{18,1},{19,2},{20,3},{21,4},{22,5},{23,6},{24,7},{25,8},{26... | collective-permute-start | bytes 86024 | tf_op jit(solution)/shard_map/ppermute | solution.py:602
  35.6 0.0 copy-done
  35.7 0.0 copy-done.1
  35.7 0.0 copy-done.2
  35.7 0.9 own_cells.1
  36.6 8.4 %collective-permute-done.4.pp_ref = f32[7,8,128]{2,1,0:T(8,128)S(1)} collective-permute-done((f32[7,8,128]{2,1,0:T(8,128)S(1)}, f32[7,8,128]{2,1,0:T(8,128)S(1)}, u32[]{:S(2)}, u32[]{:S(2)}) %collective-permute-start.4) | collective-permute-done | bytes 28704 | tf_op jit(solution)/shard_map/ppermute | solution.py:602
  45.0 0.0 collective-permute-done.1.xm_ref
  45.0 0.0 collective-permute-done.3.ym_ref
  45.0 0.0 collective-permute-done.xp_ref
  45.0 0.0 collective-permute-done.2.yp_ref
  45.0 6.4 %krylov.1 = (f32[39,40,128]{2,1,0:T(8,128)S(1)}, f32[39,40,128]{2,1,0:T(8,128)S(1)}, f32[39,40,128]{2,1,0:T(8,128)S(1)}, f32[39,40,128]{2,1,0:T(8,128)S(1)}, f32...) custom-call(f32[4]{0:T(128)S(1)} %copy-done.3, ...), custom_call_target="tpu_custom_call", output_to_operand_aliasing={{0}: (3, {}), {1}: (4, {}), {2}: (5, {}), {3}: (6, {})} | custom-call | tf_op jit(solution)/shard_map/krylov/pallas_call | solution.py:623
  51.4 32.1 %all_to_all.10.table_ref = f32[16,40,128]{2,1,0:T(8,128)S(1)} all-to-all(f32[16,40,128]{2,1,0:T(8,128)S(1)} %get-tuple-element.33), channel_id=1, replica_groups=mesh['gx'=16,'gy'=16] {'gx'}, dimensions={0} | all-to-all | bytes 655360 | tf_op jit(solution)/shard_map/all_to_all | solution.py:633
  83.6 6.9 %lookup.1 = f32[16,40,128]{2,1,0:T(8,128)S(1)} custom-call(s32[16,128,128]{2,1,0:T(8,128)} %bitcast.4, f32[16,40,128]{2,1,0:T(8,128)S(1)} %all_to_all.10.table_ref), custom_call_target="tpu_custom_call" | custom-call | tf_op jit(solution)/shard_map/lookup/pallas_call | solution.py:634
  90.5 16.1 %all_to_all.11.got_ref = f32[16,40,128]{2,1,0:T(8,128)S(1)} all-to-all(f32[16,40,128]{2,1,0:T(8,128)S(1)} %lookup.1), channel_id=1, replica_groups=mesh['gx'=16,'gy'=16] {'gy'}, dimensions={0} | all-to-all | bytes 655360 | tf_op jit(solution)/shard_map/all_to_all | solution.py:647
  106.7 1.7 %finish.1 = (f32[32,32,128]{2,1,0:T(8,128)}, f32[8,128]{1,0:T(8,128)}) custom-call(f32[16,40,128]{2,1,0:T(8,128)S(1)} %all_to_all.11.got_ref, f32[8,128]{1,0:T(8,128)} %bitcast.6, f32[39,40,128]{2,1,0:T(8,128)S(1)} %get-tuple-element.34.t_ref, f32[39,40,128]{2,1,0:T(8,128)S(1)} %get-tuple-element.35.w0_ref, f32[39,40,128]{2,1,0:T(8,128)S(1)} %get-tuple-element.36.w1_ref, ...), custom_call_target="tpu_custom_call" | custom-call | tf_op jit(solution)/shard_map/finish/pallas_call | solution.py:648
  (7 shorter events, 0.0 us)
Async XLA Ops:
  7.2 76.4 %all-gather.3.cloned.1.call-start = ((), (), s32[]{:S(2)}) async-start(), calls=%async_computation.2 | async-start | bytes 1114112 | tf_op jit(solution)/shard_map/all_gather | solution.py:548
  8.6 27.1 %copy-start = (f32[32,32,128]{2,1,0:T(8,128)S(1)}, f32[32,32,128]{2,1,0:T(8,128)}, u32[]{:S(2)}) copy-start(f32[32,32,128]{2,1,0:T(8,128)} %t_hbm.1) | copy-start | bytes 1572868
  8.6 27.1 %copy-start.1 = (s32[32,32,128]{2,1,0:T(8,128)S(1)}, s32[32,32,128]{2,1,0:T(8,128)}, u32[]{:S(2)}) copy-start(s32[32,32,128]{2,1,0:T(8,128)} %id_hbm.1) | copy-start | bytes 1572868
  8.6 27.1 %copy-start.2 = (s32[32,32,128]{2,1,0:T(8,128)S(1)}, s32[32,32,128]{2,1,0:T(8,128)}, u32[]{:S(2)}) copy-start(s32[32,32,128]{2,1,0:T(8,128)} %chip_hbm.1) | copy-start | bytes 1572868
  10.2 34.8 %collective-permute-start.2 = (f32[48,8,128]{2,1,0:T(8,128)S(1)}, f32[48,8,128]{2,1,0:T(8,128)S(1)}, u32[]{:S(2)}, u32[]{:S(2)}) collective-permute-start(f32[48,8,128]{2,1,0:T(8,128)S(1)} %get-tuple-element.27), channel_id=1, source_target_pairs={{1,0},{2,1},{3,2},{4,3},{5,4},{6,5},{7,6},{8,7},{9,8},{10,9},{11,1... | collective-permute-start | bytes 589832 | tf_op jit(solution)/shard_map/ppermute | solution.py:602
  15.4 29.6 %collective-permute-start = (f32[11,32,128]{2,1,0:T(8,128)S(1)}, f32[11,32,128]{2,1,0:T(8,128)S(1)}, u32[]{:S(2)}, u32[]{:S(2)}) collective-permute-start(f32[11,32,128]{2,1,0:T(8,128)S(1)} %get-tuple-element.25), channel_id=1, source_target_pairs={{16,0},{17,1},{18,2},{19,3},{20,4},{21,5},{22,6},{23,7},{24,8},{25... | collective-permute-start | bytes 540680 | tf_op jit(solution)/shard_map/ppermute | solution.py:602
  16.7 28.3 %collective-permute-start.1 = (f32[8,32,128]{2,1,0:T(8,128)S(1)}, f32[8,32,128]{2,1,0:T(8,128)S(1)}, u32[]{:S(2)}, u32[]{:S(2)}) collective-permute-start(f32[8,32,128]{2,1,0:T(8,128)S(1)} %get-tuple-element.26), channel_id=1, source_target_pairs={{0,16},{1,17},{2,18},{3,19},{4,20},{5,21},{6,22},{7,23},{8,24},{9,... | collective-permute-start | bytes 393224 | tf_op jit(solution)/shard_map/ppermute | solution.py:602
  20.7 24.3 %collective-permute-start.3 = (f32[32,8,128]{2,1,0:T(8,128)S(1)}, f32[32,8,128]{2,1,0:T(8,128)S(1)}, u32[]{:S(2)}, u32[]{:S(2)}) collective-permute-start(f32[32,8,128]{2,1,0:T(8,128)S(1)} %get-tuple-element.28), channel_id=1, source_target_pairs={{0,1},{1,2},{2,3},{3,4},{4,5},{5,6},{6,7},{7,8},{8,9},{9,10},{10,1... | collective-permute-start | bytes 393224 | tf_op jit(solution)/shard_map/ppermute | solution.py:602
  22.6 3.7 %collective-permute-start.7 = (f32[3,8,128]{2,1,0:T(8,128)S(1)}, f32[3,8,128]{2,1,0:T(8,128)S(1)}, u32[]{:S(2)}, u32[]{:S(2)}) collective-permute-start(f32[3,8,128]{2,1,0:T(8,128)S(1)} %get-tuple-element.32), channel_id=1, source_target_pairs={{0,17},{1,18},{2,19},{3,20},{4,21},{5,22},{6,23},{7,24},{8,25},{9,... | collective-permute-start | bytes 36872 | tf_op jit(solution)/shard_map/ppermute | solution.py:602
  26.3 5.1 %collective-permute-start.5 = (f32[4,8,128]{2,1,0:T(8,128)S(1)}, f32[4,8,128]{2,1,0:T(8,128)S(1)}, u32[]{:S(2)}, u32[]{:S(2)}) collective-permute-start(f32[4,8,128]{2,1,0:T(8,128)S(1)} %get-tuple-element.30), channel_id=1, source_target_pairs={{16,1},{17,2},{18,3},{19,4},{20,5},{21,6},{22,7},{23,8},{24,9},{25... | collective-permute-start | bytes 49160 | tf_op jit(solution)/shard_map/ppermute | solution.py:602
  31.4 4.3 %copy-start.3 = (f32[4]{0:T(128)S(1)}, f32[4]{0:T(128)}, u32[]{:S(2)}) copy-start(f32[4]{0:T(128)} %ref_ref.3) | copy-start | bytes 52
  31.4 4.3 %copy-start.4 = (f32[4]{0:T(128)S(1)}, f32[4]{0:T(128)}, u32[]{:S(2)}) copy-start(f32[4]{0:T(128)} %grad_ref.3) | copy-start | bytes 52
  31.4 4.3 %copy-start.5 = (f32[4]{0:T(128)S(1)}, f32[4]{0:T(128)}, u32[]{:S(2)}) copy-start(f32[4]{0:T(128)} %store_ref.3) | copy-start | bytes 52
  31.4 2.9 %collective-permute-start.6 = (f32[5,8,128]{2,1,0:T(8,128)S(1)}, f32[5,8,128]{2,1,0:T(8,128)S(1)}, u32[]{:S(2)}, u32[]{:S(2)}) collective-permute-start(f32[5,8,128]{2,1,0:T(8,128)S(1)} %get-tuple-element.31), channel_id=1, source_target_pairs={{1,16},{2,17},{3,18},{4,19},{5,20},{6,21},{7,22},{8,23},{9,24},{10... | collective-permute-start | bytes 61448 | tf_op jit(solution)/shard_map/ppermute | solution.py:602
  34.4 10.6 %collective-permute-start.4 = (f32[7,8,128]{2,1,0:T(8,128)S(1)}, f32[7,8,128]{2,1,0:T(8,128)S(1)}, u32[]{:S(2)}, u32[]{:S(2)}) collective-permute-start(f32[7,8,128]{2,1,0:T(8,128)S(1)} %get-tuple-element.29), channel_id=1, source_target_pairs={{17,0},{18,1},{19,2},{20,3},{21,4},{22,5},{23,6},{24,7},{25,8},{26... | collective-permute-start | bytes 86024 | tf_op jit(solution)/shard_map/ppermute | solution.py:602
Sparse Core Ops, SparseCore 0:
  10.4 39.1 all-gather.2

commit v2 on v1

--- a/solution.py
+++ b/solution.py
@@ -20,32 +20,45 @@
 PY = NY + 8
 FIELDS = 4
 TILE = 8
-PAIRS = 16
+PAIRS = 20
 MIB = 1024 * 1024
 f32 = jnp.float32
 bf16 = jnp.bfloat16
 
 
+def shift_pairs(count):
+    up = [(i, i + 1) for i in range(count - 1)]
+    return up, [(target, source) for source, target in up]
+
+
 def sublane(shape):
     return lax.broadcasted_iota(jnp.int32, shape, len(shape) - 2)
 
 
 def lane(shape):
     return lax.broadcasted_iota(jnp.int32, shape, len(shape) - 1)
+
+
+def first_tile(sub, temp, ident):
+    return jnp.where(sub < 4, temp, pltpu.roll(ident, 4, 0))
+
+
+def last_tile(sub, temp, ident, chip):
+    return jnp.where(
+        sub >= 5, temp, jnp.where(sub >= 2, pltpu.roll(ident, 5, 0), pltpu.roll(chip, 2, 0))
+    )
 
 
 def pack_kernel(
     t_hbm,
     id_hbm,
     chip_hbm,
+    site_hbm,
     x_low,
     x_high,
     y_low,
     y_high,
-    low_low,
-    low_high,
-    high_low,
-    high_high,
+    sites,
     t_a,
     t_b,
     i_a,
@@ -58,6 +71,7 @@
     i_m,
     c_p,
     c_m,
+    site_ref,
     sems,
 ):
     copies = []
@@ -75,6 +89,7 @@
             (t_hbm.at[:, pl.ds(NY - TILE, TILE)], t_b),
             (id_hbm.at[:, pl.ds(NY - TILE, TILE)], i_b),
             (chip_hbm.at[:, pl.ds(NY - TILE, TILE)], c_b),
+            (site_hbm, site_ref),
         )
     ):
         copies.append(pltpu.make_async_copy(src, dst, sems.at[k]))
@@ -93,43 +108,41 @@
         if k < 2:
             x_high[6 + k] = c_m[2 + k].astype(f32)
 
-    def first_rows(q):
-        return jnp.where(sub < 4, t_a[q], pltpu.roll(i_a[q].astype(f32), 4, 0))
-
-    def last_rows(q):
-        return jnp.where(
-            sub >= 5,
-            t_b[q],
-            jnp.where(
-                sub >= 2,
-                pltpu.roll(i_b[q].astype(f32), 5, 0),
-                pltpu.roll(c_b[q].astype(f32), 2, 0),
-            ),
-        )
-
     def own(q, _):
-        y_low[q] = first_rows(q)
-        y_high[q] = last_rows(q)
+        y_low[q] = first_tile(sub, t_a[q], i_a[q].astype(f32))
+        y_high[q] = last_tile(sub, t_b[q], i_b[q].astype(f32), c_b[q].astype(f32))
         return 0
 
     lax.fori_loop(0, NX, own, 0, unroll=8)
-
-    def pair(j, _):
-        y_low[NX + j] = jnp.where(
-            sub < 4, c_a[j].astype(f32), pltpu.roll(c_a[j + PAIRS].astype(f32), 4, 0)
-        )
-        return 0
-
-    lax.fori_loop(0, PAIRS, pair, 0, unroll=8)
-    for k in range(HIGH):
-        low_low[k] = first_rows(k)
-        low_high[k] = last_rows(k)
-        if k < 3:
-            low_low[4 + k] = c_a[k].astype(f32)
-            high_low[k] = first_rows(NX - 3 + k)
-            high_high[k] = last_rows(NX - 3 + k)
-        if k < 2:
-            high_low[3 + k] = c_a[NX - 2 + k].astype(f32)
+    for j in range(PAIRS):
+        tile = c_a[j].astype(f32)
+        if j + PAIRS < NX:
+            tile = jnp.where(sub < 4, tile, pltpu.roll(c_a[j + PAIRS].astype(f32), 4, 0))
+        y_low[PX + j] = tile
+    for k in range(sites.shape[0]):
+        sites[k] = site_ref[...]
+
+
+def corner_kernel(low_in, high_in, xp_ref, xm_ref, sites_in, y_low, y_high, sites_out):
+    del low_in, high_in, sites_in, sites_out
+    sub = sublane((TILE, NZ))
+    zero = jnp.zeros((TILE, NZ), f32)
+    last = pl.ds(NY - TILE, TILE)
+    first = pl.ds(0, TILE)
+    for k in range(HIGH + LOW):
+        q = NX + k
+        if k < HIGH:
+            temp, ident, chip = xp_ref.at[k], xp_ref.at[4 + k], xp_ref.at[8 + k] if k < 3 else None
+        else:
+            j = k - HIGH
+            temp, ident, chip = xm_ref.at[j], xm_ref.at[3 + j], xm_ref.at[5 + j] if j else None
+        y_low[q] = first_tile(sub, temp[first, :], ident[first, :])
+        y_high[q] = last_tile(
+            sub, temp[last, :], ident[last, :], zero if chip is None else chip[last, :]
+        )
+        if chip is not None:
+            tile = y_low[PX + q - PAIRS]
+            y_low[PX + q - PAIRS] = jnp.where(sub < 4, tile, pltpu.roll(chip[first, :], 4, 0))
 
 
 def pick(ident, table):
@@ -145,7 +158,11 @@
     return conduct, pick(ident, store_ref)
 
 
-def own_kernel(ref_ref, grad_ref, store_ref, t_ref, id_ref, chip_ref, tp, cp, capp, chp):
+def own_kernel(
+    ref_ref, grad_ref, store_ref, t_ref, id_ref, chip_ref, sites_in, tp, cp, capp, chp, sites_out
+):
+    del sites_in, sites_out
+
     def own_plane(q, _):
         temp = t_ref[q]
         conduct, store = element(temp, id_ref[q], ref_ref, grad_ref, store_ref)
@@ -170,10 +187,6 @@
     xm_ref,
     yp_ref,
     ym_ref,
-    pp_ref,
-    pm_ref,
-    mp_ref,
-    mm_ref,
     tp,
     cp,
     capp,
@@ -201,7 +214,9 @@
     rows_halo = jnp.where(sub < 4, high_y, low_y)
     rate = clock_advance * interface_warming_rate
 
-    def put_halo(q, high, low, chip_high, plane_in):
+    def put_halo(q, chip_high, plane_in):
+        high = yp_ref[q]
+        low = ym_ref[q]
         temp = jnp.where(sub < 4, high, low)
         ident = jnp.where(sub < 4, pltpu.roll(high, 4, 0), pltpu.roll(low, 3, 0))
         chip = jnp.where(sub < 4, chip_high, pltpu.roll(low, 6, 0))
@@ -211,36 +226,31 @@
         capp[q, NY:, :] = store
         chp[q, NY:, :] = rate * chip
 
-    def own_halo(j, _):
-        chips = yp_ref[NX + j]
-        put_halo(j, yp_ref[j], ym_ref[j], chips, one)
-        q = j + PAIRS
-        put_halo(q, yp_ref[q], ym_ref[q], pltpu.roll(chips, 4, 0), one)
+    def own_halo_first(q, _):
+        put_halo(q, yp_ref[PX + q], one)
         return 0
 
-    lax.fori_loop(0, PAIRS, own_halo, 0, unroll=4)
+    def own_halo_second(q, _):
+        put_halo(q, pltpu.roll(yp_ref[PX + q - PAIRS], 4, 0), one)
+        return 0
+
+    lax.fori_loop(0, PAIRS, own_halo_first, 0, unroll=5)
+    lax.fori_loop(PAIRS, NX, own_halo_second, 0, unroll=6)
 
     zero_plane = jnp.zeros((NY, NZ), f32)
     zero_tile = jnp.zeros((TILE, NZ), f32)
 
-    def side_plane(q, temp, ident, chip, high, low, chip_high, plane_in):
+    def side_plane(q, temp, ident, chip, plane_in):
         conduct, store = element(temp, ident, ref_ref, grad_ref, store_ref)
         tp[q, :NY, :] = temp
         cp[q, :NY, :] = conduct * plane_in
         capp[q, :NY, :] = store
         chp[q, :NY, :] = rate * chip
-        put_halo(q, high, low, chip_high, plane_in)
+        put_halo(q, pltpu.roll(yp_ref[PX + q - PAIRS], 4, 0), plane_in)
 
     for k in range(HIGH):
         side_plane(
-            NX + k,
-            xp_ref[k],
-            xp_ref[4 + k],
-            xp_ref[8 + k] if k < 3 else zero_plane,
-            pp_ref[k],
-            pm_ref[k],
-            pp_ref[4 + k] if k < 3 else zero_tile,
-            high_x,
+            NX + k, xp_ref[k], xp_ref[4 + k], xp_ref[8 + k] if k < 3 else zero_plane, high_x
         )
     for k in range(LOW):
         side_plane(
@@ -248,9 +258,6 @@
             xm_ref[k],
             xm_ref[3 + k],
             xm_ref[5 + k] if k > 0 else zero_plane,
-            mp_ref[k],
-            mm_ref[k],
-            mp_ref[2 + k] if k > 0 else zero_tile,
             low_x,
         )
 
@@ -379,9 +386,7 @@
             send_ref[k, TILE * j : TILE * (j + 1), :] = tile
 
 
-def lookup_kernel(site_hbm, table_ref, out_ref, parts, site_ref, sem):
-    copy = pltpu.make_async_copy(site_hbm.at[:, pl.ds(0, TILE)], site_ref, sem)
-    copy.start()
+def lookup_kernel(site_ref, table_ref, out_ref, parts):
     blocks = table_ref.shape[0]
     targets = site_ref.shape[0]
     iy = lax.axis_index("gy")
@@ -402,7 +407,6 @@
     total = table_ref[0, TILE * FIELDS :, :]
     for a in range(1, blocks):
         total = total + table_ref[a, TILE * FIELDS :, :]
-    copy.wait()
 
     def one(b, _):
         site = site_ref[b]
@@ -544,9 +548,6 @@
         return pltpu.CompilerParams(vmem_limit_bytes=mib * MIB)
 
 
-    sites = jnp.pad(clearance_point_indices.reshape(TILE, NZ), ((0, NZ - TILE), (0, 0)))
-    sites = lax.all_gather(sites, "gy")
-
     anywhere = pl.BlockSpec(memory_space=pltpu.HBM)
 
     def arr(*shape, dtype=f32):
@@ -559,20 +560,17 @@
         return [pltpu.with_memory_space_constraint(a, pltpu.HBM) for a in arrays]
 
     i32 = jnp.int32
-    packed = pl.pallas_call(
+    x_low, x_high, y_low, y_high, sites = pl.pallas_call(
         pack_kernel,
         name="pack",
-        in_specs=[anywhere] * 3,
-        out_specs=[vmem] * 8,
+        in_specs=[anywhere] * 4,
+        out_specs=[vmem] * 5,
         out_shape=[
             arr(11, NY, NZ),
             arr(8, NY, NZ),
-            arr(NX + PAIRS, TILE, NZ),
-            arr(NX, TILE, NZ),
-            arr(7, TILE, NZ),
-            arr(4, TILE, NZ),
-            arr(5, TILE, NZ),
-            arr(3, TILE, NZ),
+            arr(PX + PAIRS, TILE, NZ),
+            arr(PX, TILE, NZ),
+            arr(size_y, TILE, NZ, dtype=i32),
         ],
         scratch_shapes=[
             buf(NX, TILE, NZ),
@@ -587,22 +585,32 @@
             buf(HIGH, NY, NZ, dtype=i32),
             buf(HIGH, NY, NZ, dtype=i32),
             buf(HIGH, NY, NZ, dtype=i32),
-            pltpu.SemaphoreType.DMA((12,)),
+            buf(TILE, NZ, dtype=i32),
+            pltpu.SemaphoreType.DMA((13,)),
         ],
         compiler_params=params(10),
-    )(*in_hbm(temp, ident, chip))
-
-    def shift(block, dx, dy):
-        pairs = [
-            (i * size_y + j, (i + dx) * size_y + j + dy)
-            for i in range(size_x)
-            for j in range(size_y)
-            if 0 <= i + dx < size_x and 0 <= j + dy < size_y
-        ]
-        return lax.ppermute(block, ("gx", "gy"), pairs)
-
-    moves = ((-1, 0), (1, 0), (0, -1), (0, 1), (-1, -1), (-1, 1), (1, -1), (1, 1))
-    halos = [shift(block, dx, dy) for block, (dx, dy) in zip(packed, moves)]
+    )(*in_hbm(temp, ident, chip, clearance_point_indices.reshape(TILE, NZ)))
+    sites = lax.all_to_all(sites, "gy", 0, 0)
+
+    up, down = shift_pairs(size_x)
+    xp = lax.ppermute(x_low, "gx", down)
+    xm = lax.ppermute(x_high, "gx", up)
+    y_low, y_high, sites = pl.pallas_call(
+        corner_kernel,
+        name="corners",
+        in_specs=[vmem] * 5,
+        out_specs=[vmem] * 3,
+        out_shape=[
+            arr(PX + PAIRS, TILE, NZ),
+            arr(PX, TILE, NZ),
+            arr(size_y, TILE, NZ, dtype=i32),
+        ],
+        input_output_aliases={0: 0, 1: 1, 4: 2},
+        compiler_params=params(8),
+    )(y_low, y_high, xp, xm, sites)
+    up, down = shift_pairs(size_y)
+    yp = lax.ppermute(y_low, "gy", down)
+    ym = lax.ppermute(y_high, "gy", up)
 
     tables = (
         substance_reference_diffusivity,
@@ -610,40 +618,37 @@
         substance_storage_coefficient,
     )
     padded = arr(PX, PY, NZ)
-    own = pl.pallas_call(
+    *own, sites = pl.pallas_call(
         own_kernel,
         name="own_cells",
-        in_specs=[smem] * 3 + [vmem] * 3,
-        out_specs=[vmem] * 4,
-        out_shape=[padded] * 4,
+        in_specs=[smem] * 3 + [vmem] * 4,
+        out_specs=[vmem] * 5,
+        out_shape=[padded] * 4 + [arr(size_y, TILE, NZ, dtype=i32)],
+        input_output_aliases={6: 4},
         compiler_params=params(12),
-    )(*tables, temp, ident, chip)
+    )(*tables, temp, ident, chip, sites)
 
     payload = TILE * (FIELDS + 1)
     start, _, _, _, w0, w1, w2, send = pl.pallas_call(
         krylov_kernel,
         name="krylov",
-        in_specs=[smem] * 3 + [vmem] * 12,
+        in_specs=[smem] * 3 + [vmem] * 8,
         out_specs=[vmem] * 8,
         out_shape=[padded] * 7 + [arr(size_x, payload, NZ)],
         input_output_aliases={3: 0, 4: 1, 5: 2, 6: 3},
         scratch_shapes=[buf(PX, PY, NZ)] * 4,
         compiler_params=params(24),
-    )(*tables, *own, *halos)
+    )(*tables, *own, xp, xm, yp, ym)
     table = lax.all_to_all(send, "gx", 0, 0)
     found = pl.pallas_call(
         lookup_kernel,
         name="lookup",
-        in_specs=[anywhere, vmem],
+        in_specs=[vmem] * 2,
         out_specs=vmem,
         out_shape=arr(size_y, payload, NZ),
-        scratch_shapes=[
-            buf(NZ * (FIELDS - 1), 2 * NZ, dtype=bf16),
-            buf(size_y, TILE, NZ, dtype=i32),
-            pltpu.SemaphoreType.DMA(()),
-        ],
+        scratch_shapes=[buf(NZ * (FIELDS - 1), 2 * NZ, dtype=bf16)],
         compiler_params=params(20),
-    )(*in_hbm(sites), table)
+    )(sites, table)
     got = lax.all_to_all(found, "gy", 0, 0)
     temperature, growth = pl.pallas_call(
         final_kernel,

time: 116 us -> 82.3 us (0.71)
  between operations: 14.2 us -> 0.8 us
  waiting for transfers between devices: 13.9 us -> 1.22 us
  starting transfers between devices: 19.9 us -> 11.8 us
  blocking collectives: 48.2 us -> 51.3 us
  local copies, waits for them, and re-layouts: 1.35 us -> 0.03 us
    all_to_all x0 -> x1, blocking collectives: none -> 13.4 us  [local(): sites = lax.all_to_all(sites, 'gy', 0, 0)]
    ppermute x8 -> x4, waiting for transfers between devices: 13.9 us -> 1.22 us  [the longest x1 1.21 us: local(): ym = lax.ppermute(y_high, 'gy', up)]
    ppermute x8 -> x4, starting transfers between devices: 19.8 us -> 11.8 us  [the longest x1 4.67 us: local(): xm = lax.ppermute(x_high, 'gx', up)]
    all_to_all x1, blocking collectives: 32.1 us -> 24.2 us  [local(): table = lax.all_to_all(send, 'gx', 0, 0)]
    all_to_all x1, blocking collectives: 16.1 us -> 13.7 us  [local(): got = lax.all_to_all(found, 'gy', 0, 0)]
    pad x1 -> x0, local copies, waits for them, and re-layouts: 1.32 us -> none  [local(): jnp.pad(clearance_point_indices.reshape(TILE, NZ), ((0, NZ - TILE), (0, 0)))]
    pallas_call x2 -> x3, Pallas kernels: 8.58 us -> 7.76 us  [the longest x1 6.14 us: local(): pl.pallas_call(lookup_kernel, name='lookup', in_specs=[vmem] * 2, out_spe...]
  transfers between devices with their start and end apart: 9 -> 4, of which waited for: 4 -> 1; matrix products, arithmetic and copies ran while one was open for 0% -> 0% of each run, Pallas kernels for 8% -> 1%
where the time goes in v2:
time: 82.3 us; the launch traced here: 82 us
  blocking collectives  51.3 us (62%)
  Pallas kernels  16.8 us (20%)
  starting transfers between devices  11.8 us (14%)
  waiting for transfers between devices  1.22 us (1%)
    all_to_all x1, blocking collectives, local(): table = lax.all_to_all(send, 'gx', 0, 0)  24.2 us
    all_to_all x1, blocking collectives, local(): got = lax.all_to_all(found, 'gy', 0, 0)  13.7 us
    all_to_all x1, blocking collectives, local(): sites = lax.all_to_all(sites, 'gy', 0, 0)  13.4 us
    pallas_call x1, Pallas kernels, local(): pl.pallas_call(krylov_kernel, name='krylov', in_specs=[smem] * 3 + [vmem]...  6.41 us
    pallas_call x1, Pallas kernels, local(): pl.pallas_call(lookup_kernel, name='lookup', in_specs=[vmem] * 2, out_spe...  6.14 us
    ppermute x1, starting transfers between devices, local(): xm = lax.ppermute(x_high, 'gx', up)  4.67 us
    ppermute x1, starting transfers between devices, local(): ym = lax.ppermute(y_high, 'gy', up)  3.34 us
    ppermute x1, starting transfers between devices, local(): yp = lax.ppermute(y_low, 'gy', down)  2.35 us
  transfers between devices with their start and end apart: 4, of which 1 were waited for; matrix products, arithmetic and copies ran while one was open for 0% of the time, Pallas kernels for 1%

profile of v2, /device:TPU:1, one launch (start us, length us, event | category | flops | bytes accessed | tf_op | source)
XLA Modules:
  0.0 82.0 jit_solution(2595106868388431145)
XLA Ops:
  0.6 0.0 copy-start.1
  0.6 0.0 copy-start.2
  0.7 1.6 %pack.1 = (f32[11,32,128]{2,1,0:T(8,128)S(1)}, f32[8,32,128]{2,1,0:T(8,128)S(1)}, f32[59,8,128]{2,1,0:T(8,128)S(1)}, f32[39,8,128]{2,1,0:T(8,128)S(1)}, s32[16,8,128]{2,1,0:T(8,128)S(1)}) custom-call(f32[32,32,128]{2,1,0:T(8,128)} %t_ref.1, s32[32,32,128]{2,1,0:T(8,128)} %id_ref.1, s32[32,32,128]{2,1,0:T(8,128)} %chip_ref.1, s32[8,128]{1,0:T(8,128)} %bitcast.3), custom_call_target="tpu_custom_call" | custom-call | tf_op jit(solution)/shard_map/pack/pallas_call | solution.py:563
  2.3 0.0 copy-start
  2.3 1.4 %collective-permute-start = (f32[11,32,128]{2,1,0:T(8,128)S(1)}, f32[11,32,128]{2,1,0:T(8,128)S(1)}, u32[]{:S(2)}, u32[]{:S(2)}) collective-permute-start(f32[11,32,128]{2,1,0:T(8,128)S(1)} %get-tuple-element.24), channel_id=1, source_target_pairs={{16,0},{32,16},{48,32},{64,48},{80,64},{96,80},{112,96},{128,112},... | collective-permute-start | bytes 540680 | tf_op jit(solution)/shard_map/ppermute | solution.py:596
  3.7 4.7 %collective-permute-start.1 = (f32[8,32,128]{2,1,0:T(8,128)S(1)}, f32[8,32,128]{2,1,0:T(8,128)S(1)}, u32[]{:S(2)}, u32[]{:S(2)}) collective-permute-start(f32[8,32,128]{2,1,0:T(8,128)S(1)} %get-tuple-element.25), channel_id=1, source_target_pairs={{0,16},{16,32},{32,48},{48,64},{64,80},{80,96},{96,112},{112,128},... | collective-permute-start | bytes 393224 | tf_op jit(solution)/shard_map/ppermute | solution.py:597
  8.4 13.4 %all_to_all.15.sites_in = s32[16,8,128]{2,1,0:T(8,128)S(1)} all-to-all(s32[16,8,128]{2,1,0:T(8,128)S(1)} %get-tuple-element.26), channel_id=1, replica_groups=mesh['gx'=16,'gy'=16] {'gy'}, dimensions={0} | all-to-all | bytes 131072 | tf_op jit(solution)/shard_map/all_to_all | solution.py:593
  21.8 0.0 collective-permute-done.1.xm_ref
  21.8 0.0 collective-permute-done.xp_ref
  21.8 2.4 %collective-permute-start.2 = (f32[59,8,128]{2,1,0:T(8,128)S(1)}, f32[59,8,128]{2,1,0:T(8,128)S(1)}, u32[]{:S(2)}, u32[]{:S(2)}) collective-permute-start(f32[59,8,128]{2,1,0:T(8,128)S(1)} %get-tuple-element.33), channel_id=1, source_target_pairs={{1,0},{2,1},{3,2},{4,3},{5,4},{6,5},{7,6},{8,7},{9,8},{10,9},{11,1... | collective-permute-start | bytes 725000 | tf_op jit(solution)/shard_map/ppermute | solution.py:612
  24.2 0.0 copy-start.3
  24.2 0.0 copy-start.4
  24.2 0.0 copy-start.5
  24.2 3.3 %collective-permute-start.3 = (f32[39,8,128]{2,1,0:T(8,128)S(1)}, f32[39,8,128]{2,1,0:T(8,128)S(1)}, u32[]{:S(2)}, u32[]{:S(2)}) collective-permute-start(f32[39,8,128]{2,1,0:T(8,128)S(1)} %get-tuple-element.34), channel_id=1, source_target_pairs={{0,1},{1,2},{2,3},{3,4},{4,5},{5,6},{6,7},{7,8},{8,9},{9,10},{10,1... | collective-permute-start | bytes 479240 | tf_op jit(solution)/shard_map/ppermute | solution.py:613
  27.5 0.0 copy-done.1
  27.5 0.0 copy-done.2
  27.6 0.0 copy-done
  27.6 0.0 copy-done.3
  27.6 0.0 copy-done.4
  27.6 0.0 copy-done.5
  27.6 0.9 %own_cells.1 = (f32[39,40,128]{2,1,0:T(8,128)S(1)}, f32[39,40,128]{2,1,0:T(8,128)S(1)}, f32[39,40,128]{2,1,0:T(8,128)S(1)}, f32[39,40,128]{2,1,0:T(8,128)S(1)}, s32[16,8,128]{2,1,0:T(8,128)S(1)}) custom-call(f32[4]{0:T(128)S(1)} %copy-done.3, f32[4]{0:T(128)S(1)} %copy-done.4, f32[4]{0:T(128)S(1)} %copy-done.5, ...), custom_call_target="tpu_custom_call", output_to_operand_aliasing={{4}: (6, {})} | custom-call | tf_op jit(solution)/shard_map/own_cells/pallas_call | solution.py:621
  28.5 1.2 %collective-permute-done.3.ym_ref = f32[39,8,128]{2,1,0:T(8,128)S(1)} collective-permute-done((f32[39,8,128]{2,1,0:T(8,128)S(1)}, f32[39,8,128]{2,1,0:T(8,128)S(1)}, u32[]{:S(2)}, u32[]{:S(2)}) %collective-permute-start.3) | collective-permute-done | bytes 159776 | tf_op jit(solution)/shard_map/ppermute | solution.py:613
  29.7 0.0 collective-permute-done.2.yp_ref
  29.7 6.4 %krylov.1 = (f32[39,40,128]{2,1,0:T(8,128)S(1)}, f32[39,40,128]{2,1,0:T(8,128)S(1)}, f32[39,40,128]{2,1,0:T(8,128)S(1)}, f32[39,40,128]{2,1,0:T(8,128)S(1)}, f32...) custom-call(f32[4]{0:T(128)S(1)} %copy-done.3, ...), custom_call_target="tpu_custom_call", output_to_operand_aliasing={{0}: (3, {}), {1}: (4, {}), {2}: (5, {}), {3}: (6, {})} | custom-call | tf_op jit(solution)/shard_map/krylov/pallas_call | solution.py:632
  36.2 24.2 %all_to_all.16.table_ref = f32[16,40,128]{2,1,0:T(8,128)S(1)} all-to-all(f32[16,40,128]{2,1,0:T(8,128)S(1)} %get-tuple-element.35), channel_id=1, replica_groups=mesh['gx'=16,'gy'=16] {'gx'}, dimensions={0} | all-to-all | bytes 655360 | tf_op jit(solution)/shard_map/all_to_all | solution.py:642
  60.4 6.1 %lookup.1 = f32[16,40,128]{2,1,0:T(8,128)S(1)} custom-call(s32[16,8,128]{2,1,0:T(8,128)S(1)} %get-tuple-element.28.site_ref, f32[16,40,128]{2,1,0:T(8,128)S(1)} %all_to_all.16.table_ref), custom_call_target="tpu_custom_call" | custom-call | tf_op jit(solution)/shard_map/lookup/pallas_call | solution.py:643
  66.5 13.7 %all_to_all.17.got_ref = f32[16,40,128]{2,1,0:T(8,128)S(1)} all-to-all(f32[16,40,128]{2,1,0:T(8,128)S(1)} %lookup.1), channel_id=1, replica_groups=mesh['gx'=16,'gy'=16] {'gy'}, dimensions={0} | all-to-all | bytes 655360 | tf_op jit(solution)/shard_map/all_to_all | solution.py:652
  80.2 1.7 %finish.1 = (f32[32,32,128]{2,1,0:T(8,128)}, f32[8,128]{1,0:T(8,128)}) custom-call(f32[16,40,128]{2,1,0:T(8,128)S(1)} %all_to_all.17.got_ref, f32[8,128]{1,0:T(8,128)} %bitcast.4, f32[39,40,128]{2,1,0:T(8,128)S(1)} %get-tuple-element.36.t_ref, f32[39,40,128]{2,1,0:T(8,128)S(1)} %get-tuple-element.37.w0_ref, f32[39,40,128]{2,1,0:T(8,128)S(1)} %get-tuple-element.38.w1_ref, ...), custom_call_target="tpu_custom_call" | custom-call | tf_op jit(solution)/shard_map/finish/pallas_call | solution.py:653
  (1 shorter events, 0.0 us)
Async XLA Ops:
  0.6 26.9 %copy-start.1 = (s32[32,32,128]{2,1,0:T(8,128)S(1)}, s32[32,32,128]{2,1,0:T(8,128)}, u32[]{:S(2)}) copy-start(s32[32,32,128]{2,1,0:T(8,128)} %id_ref.1) | copy-start | bytes 1572868
  0.6 26.9 %copy-start.2 = (s32[32,32,128]{2,1,0:T(8,128)S(1)}, s32[32,32,128]{2,1,0:T(8,128)}, u32[]{:S(2)}) copy-start(s32[32,32,128]{2,1,0:T(8,128)} %chip_ref.1) | copy-start | bytes 1572868
  2.3 25.3 %copy-start = (f32[32,32,128]{2,1,0:T(8,128)S(1)}, f32[32,32,128]{2,1,0:T(8,128)}, u32[]{:S(2)}) copy-start(f32[32,32,128]{2,1,0:T(8,128)} %t_ref.1) | copy-start | bytes 1572868
  2.3 19.5 %collective-permute-start = (f32[11,32,128]{2,1,0:T(8,128)S(1)}, f32[11,32,128]{2,1,0:T(8,128)S(1)}, u32[]{:S(2)}, u32[]{:S(2)}) collective-permute-start(f32[11,32,128]{2,1,0:T(8,128)S(1)} %get-tuple-element.24), channel_id=1, source_target_pairs={{16,0},{32,16},{48,32},{64,48},{80,64},{96,80},{112,96},{128,112},... | collective-permute-start | bytes 540680 | tf_op jit(solution)/shard_map/ppermute | solution.py:596
  3.7 18.1 %collective-permute-start.1 = (f32[8,32,128]{2,1,0:T(8,128)S(1)}, f32[8,32,128]{2,1,0:T(8,128)S(1)}, u32[]{:S(2)}, u32[]{:S(2)}) collective-permute-start(f32[8,32,128]{2,1,0:T(8,128)S(1)} %get-tuple-element.25), channel_id=1, source_target_pairs={{0,16},{16,32},{32,48},{48,64},{64,80},{80,96},{96,112},{112,128},... | collective-permute-start | bytes 393224 | tf_op jit(solution)/shard_map/ppermute | solution.py:597
  21.8 7.9 %collective-permute-start.2 = (f32[59,8,128]{2,1,0:T(8,128)S(1)}, f32[59,8,128]{2,1,0:T(8,128)S(1)}, u32[]{:S(2)}, u32[]{:S(2)}) collective-permute-start(f32[59,8,128]{2,1,0:T(8,128)S(1)} %get-tuple-element.33), channel_id=1, source_target_pairs={{1,0},{2,1},{3,2},{4,3},{5,4},{6,5},{7,6},{8,7},{9,8},{10,9},{11,1... | collective-permute-start | bytes 725000 | tf_op jit(solution)/shard_map/ppermute | solution.py:612
  24.2 3.4 %copy-start.3 = (f32[4]{0:T(128)S(1)}, f32[4]{0:T(128)}, u32[]{:S(2)}) copy-start(f32[4]{0:T(128)} %ref_ref.3) | copy-start | bytes 52
  24.2 3.4 %copy-start.4 = (f32[4]{0:T(128)S(1)}, f32[4]{0:T(128)}, u32[]{:S(2)}) copy-start(f32[4]{0:T(128)} %grad_ref.3) | copy-start | bytes 52
  24.2 3.4 %copy-start.5 = (f32[4]{0:T(128)S(1)}, f32[4]{0:T(128)}, u32[]{:S(2)}) copy-start(f32[4]{0:T(128)} %store_ref.3) | copy-start | bytes 52
  24.2 5.5 %collective-permute-start.3 = (f32[39,8,128]{2,1,0:T(8,128)S(1)}, f32[39,8,128]{2,1,0:T(8,128)S(1)}, u32[]{:S(2)}, u32[]{:S(2)}) collective-permute-start(f32[39,8,128]{2,1,0:T(8,128)S(1)} %get-tuple-element.34), channel_id=1, source_target_pairs={{0,1},{1,2},{2,3},{3,4},{4,5},{5,6},{6,7},{7,8},{8,9},{9,10},{10,1... | collective-permute-start | bytes 479240 | tf_op jit(solution)/shard_map/ppermute | solution.py:613

commit v3 on v2

--- a/solution.py
+++ b/solution.py
@@ -26,9 +26,9 @@
 bf16 = jnp.bfloat16
 
 
-def shift_pairs(count):
-    up = [(i, i + 1) for i in range(count - 1)]
-    return up, [(target, source) for source, target in up]
+def swaps(count, first):
+    low = range(first, count - 1, 2)
+    return [(i, i + 1) for i in low] + [(i + 1, i) for i in low]
 
 
 def sublane(shape):
@@ -54,10 +54,10 @@
     id_hbm,
     chip_hbm,
     site_hbm,
-    x_low,
-    x_high,
-    y_low,
-    y_high,
+    xa,
+    xb,
+    ya,
+    yb,
     sites,
     t_a,
     t_b,
@@ -97,20 +97,35 @@
     for copy in copies:
         copy.wait()
 
+    def x_sides(low, high):
+        for k in range(HIGH):
+            low[k] = t_p[k]
+            low[4 + k] = i_p[k].astype(f32)
+            if k < 3:
+                low[8 + k] = c_p[k].astype(f32)
+                high[k] = t_m[1 + k]
+                high[3 + k] = i_m[1 + k].astype(f32)
+            if k < 2:
+                high[6 + k] = c_m[2 + k].astype(f32)
+
+    even_x = lax.rem(lax.axis_index("gx"), 2) == 0
+    even_y = lax.rem(lax.axis_index("gy"), 2) == 0
+
+    @pl.when(even_x)
+    def _():
+        x_sides(xa, xb)
+
+    @pl.when(jnp.logical_not(even_x))
+    def _():
+        x_sides(xb, xa)
+
     sub = sublane((TILE, NZ))
-    for k in range(HIGH):
-        x_low[k] = t_p[k]
-        x_low[4 + k] = i_p[k].astype(f32)
-        if k < 3:
-            x_low[8 + k] = c_p[k].astype(f32)
-            x_high[k] = t_m[1 + k]
-            x_high[3 + k] = i_m[1 + k].astype(f32)
-        if k < 2:
-            x_high[6 + k] = c_m[2 + k].astype(f32)
 
     def own(q, _):
-        y_low[q] = first_tile(sub, t_a[q], i_a[q].astype(f32))
-        y_high[q] = last_tile(sub, t_b[q], i_b[q].astype(f32), c_b[q].astype(f32))
+        low = first_tile(sub, t_a[q], i_a[q].astype(f32))
+        high = last_tile(sub, t_b[q], i_b[q].astype(f32), c_b[q].astype(f32))
+        ya[q] = jnp.where(even_y, low, high)
+        yb[q] = jnp.where(even_y, high, low)
         return 0
 
     lax.fori_loop(0, NX, own, 0, unroll=8)
@@ -118,31 +133,46 @@
         tile = c_a[j].astype(f32)
         if j + PAIRS < NX:
             tile = jnp.where(sub < 4, tile, pltpu.roll(c_a[j + PAIRS].astype(f32), 4, 0))
-        y_low[PX + j] = tile
+        ya[PX + j] = tile
+        yb[PX + j] = tile
     for k in range(sites.shape[0]):
         sites[k] = site_ref[...]
 
 
-def corner_kernel(low_in, high_in, xp_ref, xm_ref, sites_in, y_low, y_high, sites_out):
-    del low_in, high_in, sites_in, sites_out
+def corner_kernel(ya_in, yb_in, xa_ref, xb_ref, sites_in, ya, yb, sites_out):
+    del ya_in, yb_in, sites_in, sites_out
+    even_x = lax.rem(lax.axis_index("gx"), 2) == 0
+    even_y = lax.rem(lax.axis_index("gy"), 2) == 0
     sub = sublane((TILE, NZ))
     zero = jnp.zeros((TILE, NZ), f32)
+    first = pl.ds(0, TILE)
     last = pl.ds(NY - TILE, TILE)
-    first = pl.ds(0, TILE)
+
+    def high_side(k, rows):
+        return jnp.where(even_x, xb_ref[k, rows, :], xa_ref[k, rows, :])
+
+    def low_side(k, rows):
+        return jnp.where(even_x, xa_ref[k, rows, :], xb_ref[k, rows, :])
+
     for k in range(HIGH + LOW):
         q = NX + k
         if k < HIGH:
-            temp, ident, chip = xp_ref.at[k], xp_ref.at[4 + k], xp_ref.at[8 + k] if k < 3 else None
+            side, places = high_side, (k, 4 + k, 8 + k if k < 3 else None)
         else:
             j = k - HIGH
-            temp, ident, chip = xm_ref.at[j], xm_ref.at[3 + j], xm_ref.at[5 + j] if j else None
-        y_low[q] = first_tile(sub, temp[first, :], ident[first, :])
-        y_high[q] = last_tile(
-            sub, temp[last, :], ident[last, :], zero if chip is None else chip[last, :]
-        )
+            side, places = low_side, (j, 3 + j, 5 + j if j else None)
+        temp, ident, chip = places
+        low = first_tile(sub, side(temp, first), side(ident, first))
+        high = last_tile(
+            sub, side(temp, last), side(ident, last), zero if chip is None else side(chip, last)
+        )
+        ya[q] = jnp.where(even_y, low, high)
+        yb[q] = jnp.where(even_y, high, low)
         if chip is not None:
-            tile = y_low[PX + q - PAIRS]
-            y_low[PX + q - PAIRS] = jnp.where(sub < 4, tile, pltpu.roll(chip[first, :], 4, 0))
+            place = PX + q - PAIRS
+            tile = jnp.where(sub < 4, ya[place], pltpu.roll(side(chip, first), 4, 0))
+            ya[place] = tile
+            yb[place] = tile
 
 
 def pick(ident, table):
@@ -183,10 +213,10 @@
     cp_in,
     capp_in,
     chp_in,
-    xp_ref,
-    xm_ref,
-    yp_ref,
-    ym_ref,
+    xa_ref,
+    xb_ref,
+    ya_ref,
+    yb_ref,
     tp,
     cp,
     capp,
@@ -214,9 +244,24 @@
     rows_halo = jnp.where(sub < 4, high_y, low_y)
     rate = clock_advance * interface_warming_rate
 
+    even_x = lax.rem(ix, 2) == 0
+    even_y = lax.rem(iy, 2) == 0
+
+    def high_row(q):
+        return jnp.where(even_y, yb_ref[q], ya_ref[q])
+
+    def low_row(q):
+        return jnp.where(even_y, ya_ref[q], yb_ref[q])
+
+    def high_plane(k):
+        return jnp.where(even_x, xb_ref[k], xa_ref[k])
+
+    def low_plane(k):
+        return jnp.where(even_x, xa_ref[k], xb_ref[k])
+
     def put_halo(q, chip_high, plane_in):
-        high = yp_ref[q]
-        low = ym_ref[q]
+        high = high_row(q)
+        low = low_row(q)
         temp = jnp.where(sub < 4, high, low)
         ident = jnp.where(sub < 4, pltpu.roll(high, 4, 0), pltpu.roll(low, 3, 0))
         chip = jnp.where(sub < 4, chip_high, pltpu.roll(low, 6, 0))
@@ -227,11 +272,11 @@
         chp[q, NY:, :] = rate * chip
 
     def own_halo_first(q, _):
-        put_halo(q, yp_ref[PX + q], one)
+        put_halo(q, high_row(PX + q), one)
         return 0
 
     def own_halo_second(q, _):
-        put_halo(q, pltpu.roll(yp_ref[PX + q - PAIRS], 4, 0), one)
+        put_halo(q, pltpu.roll(high_row(PX + q - PAIRS), 4, 0), one)
         return 0
 
     lax.fori_loop(0, PAIRS, own_halo_first, 0, unroll=5)
@@ -246,18 +291,22 @@
         cp[q, :NY, :] = conduct * plane_in
         capp[q, :NY, :] = store
         chp[q, :NY, :] = rate * chip
-        put_halo(q, pltpu.roll(yp_ref[PX + q - PAIRS], 4, 0), plane_in)
+        put_halo(q, pltpu.roll(high_row(PX + q - PAIRS), 4, 0), plane_in)
 
     for k in range(HIGH):
         side_plane(
-            NX + k, xp_ref[k], xp_ref[4 + k], xp_ref[8 + k] if k < 3 else zero_plane, high_x
+            NX + k,
+            high_plane(k),
+            high_plane(4 + k),
+            high_plane(8 + k) if k < 3 else zero_plane,
+            high_x,
         )
     for k in range(LOW):
         side_plane(
             NX + HIGH + k,
-            xm_ref[k],
-            xm_ref[3 + k],
-            xm_ref[5 + k] if k > 0 else zero_plane,
+            low_plane(k),
+            low_plane(3 + k),
+            low_plane(5 + k) if k > 0 else zero_plane,
             low_x,
         )
 
@@ -497,7 +546,18 @@
 
 
 def final_kernel(
-    got_ref, pressure_hbm, t_ref, w0_ref, w1_ref, w2_ref, temp_ref, growth_ref, pressure_ref, sem
+    got_ref,
+    pressure_hbm,
+    t_ref,
+    w0_ref,
+    w1_ref,
+    w2_ref,
+    temp_hbm,
+    growth_ref,
+    pressure_ref,
+    temp_ref,
+    sem,
+    out_sems,
 ):
     copy = pltpu.make_async_copy(pressure_hbm, pressure_ref, sem)
     copy.start()
@@ -509,23 +569,32 @@
     c = cg_coefficients(m)
     c_tile = [jnp.broadcast_to(e, (TILE, NZ)) for e in c]
     c_plane = [jnp.broadcast_to(e, (NY, NZ)) for e in c]
+
+    def plane(q, _):
+        temp_ref[q] = (
+            t_ref[q, :NY, :]
+            + c_plane[0] * w0_ref[q, :NY, :]
+            + c_plane[1] * w1_ref[q, :NY, :]
+            + c_plane[2] * w2_ref[q, :NY, :]
+        )
+        return 0
+
+    outs = []
+    step = NX // 4
+    for k in range(4):
+        lax.fori_loop(step * k, step * (k + 1), plane, 0, unroll=4)
+        part = pl.ds(step * k, step)
+        outs.append(pltpu.make_async_copy(temp_ref.at[part], temp_hbm.at[part], out_sems.at[k]))
+        outs[-1].start()
+
     flank = total[0:TILE]
     for k in range(3):
         flank = flank + c_tile[k] * total[TILE * (k + 1) : TILE * (k + 2)]
     soft = jnp.maximum(flank, 0.0) + jnp.log1p(jnp.exp(-jnp.abs(flank)))
     copy.wait()
     growth_ref[...] = usui_rate * pressure_ref[...] * jnp.exp(-usui_energy / (1.0 + soft))
-
-    def plane(q, _):
-        temp_ref[q] = (
-            t_ref[q, :NY, :]
-            + c_plane[0] * w0_ref[q, :NY, :]
-            + c_plane[1] * w1_ref[q, :NY, :]
-            + c_plane[2] * w2_ref[q, :NY, :]
-        )
-        return 0
-
-    lax.fori_loop(0, NX, plane, 0, unroll=2)
+    for out in outs:
+        out.wait()
 
 
 def local(
@@ -560,16 +629,16 @@
         return [pltpu.with_memory_space_constraint(a, pltpu.HBM) for a in arrays]
 
     i32 = jnp.int32
-    x_low, x_high, y_low, y_high, sites = pl.pallas_call(
+    xa, xb, ya, yb, sites = pl.pallas_call(
         pack_kernel,
         name="pack",
         in_specs=[anywhere] * 4,
         out_specs=[vmem] * 5,
         out_shape=[
             arr(11, NY, NZ),
-            arr(8, NY, NZ),
+            arr(11, NY, NZ),
             arr(PX + PAIRS, TILE, NZ),
-            arr(PX, TILE, NZ),
+            arr(PX + PAIRS, TILE, NZ),
             arr(size_y, TILE, NZ, dtype=i32),
         ],
         scratch_shapes=[
@@ -592,25 +661,23 @@
     )(*in_hbm(temp, ident, chip, clearance_point_indices.reshape(TILE, NZ)))
     sites = lax.all_to_all(sites, "gy", 0, 0)
 
-    up, down = shift_pairs(size_x)
-    xp = lax.ppermute(x_low, "gx", down)
-    xm = lax.ppermute(x_high, "gx", up)
-    y_low, y_high, sites = pl.pallas_call(
+    xa = lax.ppermute(xa, "gx", swaps(size_x, 1))
+    xb = lax.ppermute(xb, "gx", swaps(size_x, 0))
+    ya, yb, sites = pl.pallas_call(
         corner_kernel,
         name="corners",
         in_specs=[vmem] * 5,
         out_specs=[vmem] * 3,
         out_shape=[
             arr(PX + PAIRS, TILE, NZ),
-            arr(PX, TILE, NZ),
+            arr(PX + PAIRS, TILE, NZ),
             arr(size_y, TILE, NZ, dtype=i32),
         ],
         input_output_aliases={0: 0, 1: 1, 4: 2},
         compiler_params=params(8),
-    )(y_low, y_high, xp, xm, sites)
-    up, down = shift_pairs(size_y)
-    yp = lax.ppermute(y_low, "gy", down)
-    ym = lax.ppermute(y_high, "gy", up)
+    )(ya, yb, xa, xb, sites)
+    ya = lax.ppermute(ya, "gy", swaps(size_y, 1))
+    yb = lax.ppermute(yb, "gy", swaps(size_y, 0))
 
     tables = (
         substance_reference_diffusivity,
@@ -638,7 +705,7 @@
         input_output_aliases={3: 0, 4: 1, 5: 2, 6: 3},
         scratch_shapes=[buf(PX, PY, NZ)] * 4,
         compiler_params=params(24),
-    )(*tables, *own, xp, xm, yp, ym)
+    )(*tables, *own, xa, xb, ya, yb)
     table = lax.all_to_all(send, "gx", 0, 0)
     found = pl.pallas_call(
         lookup_kernel,
@@ -654,9 +721,14 @@
         final_kernel,
         name="finish",
         in_specs=[vmem, anywhere, vmem, vmem, vmem, vmem],
-        out_specs=[vmem] * 2,
+        out_specs=[anywhere, vmem],
         out_shape=[arr(NX, NY, NZ), arr(TILE, NZ)],
-        scratch_shapes=[buf(TILE, NZ), pltpu.SemaphoreType.DMA(())],
+        scratch_shapes=[
+            buf(TILE, NZ),
+            buf(NX, NY, NZ),
+            pltpu.SemaphoreType.DMA(()),
+            pltpu.SemaphoreType.DMA((4,)),
+        ],
         compiler_params=params(12),
     )(got, *in_hbm(clearance_face_pressure.reshape(TILE, NZ)), start, w0, w1, w2)
     return temperature, growth.reshape(-1)

time: 82.3 us -> 77 us (0.936)
  starting transfers between devices: 11.8 us -> 7.43 us
  blocking collectives: 51.3 us -> 47.2 us
  waiting for transfers between devices: 1.22 us -> 3.95 us
    ppermute x4, starting transfers between devices: 11.8 us -> 7.43 us  [the longest x1 4.75 us: local(): xb = lax.ppermute(xb, 'gx', swaps(size_x, 0))]
    all_to_all x1, blocking collectives: 24.2 us -> 20.1 us  [local(): table = lax.all_to_all(send, 'gx', 0, 0)]
    ppermute x4, waiting for transfers between devices: 1.22 us -> 3.95 us  [the longest x1 3.94 us: local(): ya = lax.ppermute(ya, 'gy', swaps(size_y, 1))]
where the time goes in v3:
time: 77 us; the launch traced here: 76.7 us
  blocking collectives  47.2 us (61%)
  Pallas kernels  16.8 us (22%)
  starting transfers between devices  7.43 us (10%)
  waiting for transfers between devices  3.95 us (5%)
    all_to_all x1, blocking collectives, local(): table = lax.all_to_all(send, 'gx', 0, 0)  20.1 us
    all_to_all x1, blocking collectives, local(): got = lax.all_to_all(found, 'gy', 0, 0)  13.7 us
    all_to_all x1, blocking collectives, local(): sites = lax.all_to_all(sites, 'gy', 0, 0)  13.4 us
    pallas_call x1, Pallas kernels, local(): pl.pallas_call(krylov_kernel, name='krylov', in_specs=[smem] * 3 + [vmem]...  6.46 us
    pallas_call x1, Pallas kernels, local(): pl.pallas_call(lookup_kernel, name='lookup', in_specs=[vmem] * 2, out_spe...  6.13 us
    ppermute x1, starting transfers between devices, local(): xb = lax.ppermute(xb, 'gx', swaps(size_x, 0))  4.75 us
    ppermute x1, waiting for transfers between devices, local(): ya = lax.ppermute(ya, 'gy', swaps(size_y, 1))  3.94 us
    ppermute x1, starting transfers between devices, local(): ya = lax.ppermute(ya, 'gy', swaps(size_y, 1))  1.92 us
  transfers between devices with their start and end apart: 4, of which 1 were waited for; matrix products, arithmetic and copies ran while one was open for 0% of the time, Pallas kernels for 1%

profile of v3, /device:TPU:1, one launch (start us, length us, event | category | flops | bytes accessed | tf_op | source)
XLA Modules:
  0.0 76.7 jit_solution(7500020540534728353)
XLA Ops:
  0.6 0.0 copy-start.2
  0.6 0.0 copy-start.5
  0.7 1.6 %pack.1 = (f32[11,32,128]{2,1,0:T(8,128)S(1)}, f32[11,32,128]{2,1,0:T(8,128)S(1)}, f32[59,8,128]{2,1,0:T(8,128)S(1)}, f32[59,8,128]{2,1,0:T(8,128)S(1)}, s32[16,8,128]{2,1,0:T(8,128)S(1)}) custom-call(f32[32,32,128]{2,1,0:T(8,128)} %t_ref.1, s32[32,32,128]{2,1,0:T(8,128)} %id_ref.1, s32[32,32,128]{2,1,0:T(8,128)} %chip_ref.1, s32[8,128]{1,0:T(8,128)} %bitcast.3), custom_call_target="tpu_custom_call" | custom-call | tf_op jit(solution)/shard_map/pack/pallas_call | solution.py:632
  2.3 0.7 collective-permute-start
  2.9 4.7 %collective-permute-start.1 = (f32[11,32,128]{2,1,0:T(8,128)S(1)}, f32[11,32,128]{2,1,0:T(8,128)S(1)}, u32[]{:S(2)}, u32[]{:S(2)}) collective-permute-start(f32[11,32,128]{2,1,0:T(8,128)S(1)} %get-tuple-element.25), channel_id=1, source_target_pairs={{0,16},{32,48},{64,80},{96,112},{128,144},{160,176},{192,208},{224... | collective-permute-start | bytes 540680 | tf_op jit(solution)/shard_map/ppermute | solution.py:665
  7.7 0.0 copy-start
  7.7 0.0 copy-start.1
  7.7 13.4 %all_to_all.15.sites_in = s32[16,8,128]{2,1,0:T(8,128)S(1)} all-to-all(s32[16,8,128]{2,1,0:T(8,128)S(1)} %get-tuple-element.26), channel_id=1, replica_groups=mesh['gx'=16,'gy'=16] {'gy'}, dimensions={0} | all-to-all | bytes 131072 | tf_op jit(solution)/shard_map/all_to_all | solution.py:662
  21.1 0.0 collective-permute-done.xa_ref
  21.1 0.0 collective-permute-done.1.xb_ref
  21.2 1.9 %collective-permute-start.2 = (f32[59,8,128]{2,1,0:T(8,128)S(1)}, f32[59,8,128]{2,1,0:T(8,128)S(1)}, u32[]{:S(2)}, u32[]{:S(2)}) collective-permute-start(f32[59,8,128]{2,1,0:T(8,128)S(1)} %get-tuple-element.33), channel_id=1, source_target_pairs={{1,2},{3,4},{5,6},{7,8},{9,10},{11,12},{13,14},{2,1},{4,3},{6,5},{... | collective-permute-start | bytes 725000 | tf_op jit(solution)/shard_map/ppermute | solution.py:679
  23.1 0.0 copy-start.3
  23.1 0.0 copy-start.4
  23.1 0.1 collective-permute-start.3
  23.2 0.0 copy-done.2
  23.2 0.0 copy-done.5
  23.2 0.0 copy-done
  23.2 0.0 copy-done.1
  23.3 0.5 copy-done.3
  23.7 0.0 copy-done.4
  23.8 0.9 %own_cells.1 = (f32[39,40,128]{2,1,0:T(8,128)S(1)}, f32[39,40,128]{2,1,0:T(8,128)S(1)}, f32[39,40,128]{2,1,0:T(8,128)S(1)}, f32[39,40,128]{2,1,0:T(8,128)S(1)}, s32[16,8,128]{2,1,0:T(8,128)S(1)}) custom-call(f32[4]{0:T(128)S(1)} %copy-done.3, f32[4]{0:T(128)S(1)} %copy-done.4, f32[4]{0:T(128)S(1)} %copy-done.5, ...), custom_call_target="tpu_custom_call", output_to_operand_aliasing={{4}: (6, {})} | custom-call | tf_op jit(solution)/shard_map/own_cells/pallas_call | solution.py:688
  24.7 3.9 %collective-permute-done.2.ya_ref = f32[59,8,128]{2,1,0:T(8,128)S(1)} collective-permute-done((f32[59,8,128]{2,1,0:T(8,128)S(1)}, f32[59,8,128]{2,1,0:T(8,128)S(1)}, u32[]{:S(2)}, u32[]{:S(2)}) %collective-permute-start.2) | collective-permute-done | bytes 241696 | tf_op jit(solution)/shard_map/ppermute | solution.py:679
  28.6 0.0 collective-permute-done.3.yb_ref
  28.6 6.5 %krylov.1 = (f32[39,40,128]{2,1,0:T(8,128)S(1)}, f32[39,40,128]{2,1,0:T(8,128)S(1)}, f32[39,40,128]{2,1,0:T(8,128)S(1)}, f32[39,40,128]{2,1,0:T(8,128)S(1)}, f32...) custom-call(f32[4]{0:T(128)S(1)} %copy-done.3, ...), custom_call_target="tpu_custom_call", output_to_operand_aliasing={{0}: (3, {}), {1}: (4, {}), {2}: (5, {}), {3}: (6, {})} | custom-call | tf_op jit(solution)/shard_map/krylov/pallas_call | solution.py:699
  35.1 20.1 %all_to_all.16.table_ref = f32[16,40,128]{2,1,0:T(8,128)S(1)} all-to-all(f32[16,40,128]{2,1,0:T(8,128)S(1)} %get-tuple-element.35), channel_id=1, replica_groups=mesh['gx'=16,'gy'=16] {'gx'}, dimensions={0} | all-to-all | bytes 655360 | tf_op jit(solution)/shard_map/all_to_all | solution.py:709
  55.2 6.1 %lookup.1 = f32[16,40,128]{2,1,0:T(8,128)S(1)} custom-call(s32[16,8,128]{2,1,0:T(8,128)S(1)} %get-tuple-element.28.site_ref, f32[16,40,128]{2,1,0:T(8,128)S(1)} %all_to_all.16.table_ref), custom_call_target="tpu_custom_call" | custom-call | tf_op jit(solution)/shard_map/lookup/pallas_call | solution.py:710
  61.3 13.7 %all_to_all.17.got_ref = f32[16,40,128]{2,1,0:T(8,128)S(1)} all-to-all(f32[16,40,128]{2,1,0:T(8,128)S(1)} %lookup.1), channel_id=1, replica_groups=mesh['gx'=16,'gy'=16] {'gy'}, dimensions={0} | all-to-all | bytes 655360 | tf_op jit(solution)/shard_map/all_to_all | solution.py:719
  75.0 1.7 %finish.1 = (f32[32,32,128]{2,1,0:T(8,128)}, f32[8,128]{1,0:T(8,128)}) custom-call(f32[16,40,128]{2,1,0:T(8,128)S(1)} %all_to_all.17.got_ref, f32[8,128]{1,0:T(8,128)} %bitcast.4, f32[39,40,128]{2,1,0:T(8,128)S(1)} %get-tuple-element.36.t_ref, f32[39,40,128]{2,1,0:T(8,128)S(1)} %get-tuple-element.37.w0_ref, f32[39,40,128]{2,1,0:T(8,128)S(1)} %get-tuple-element.38.w1_ref, ...), custom_call_target="tpu_custom_call" | custom-call | tf_op jit(solution)/shard_map/finish/pallas_call | solution.py:720
  (1 shorter events, 0.0 us)
Async XLA Ops:
  0.6 22.6 %copy-start.2 = (s32[32,32,128]{2,1,0:T(8,128)S(1)}, s32[32,32,128]{2,1,0:T(8,128)}, u32[]{:S(2)}) copy-start(s32[32,32,128]{2,1,0:T(8,128)} %chip_ref.1) | copy-start | bytes 1572868
  0.6 22.6 %copy-start.5 = (f32[4]{0:T(128)S(1)}, f32[4]{0:T(128)}, u32[]{:S(2)}) copy-start(f32[4]{0:T(128)} %store_ref.3) | copy-start | bytes 52
  2.3 18.9 %collective-permute-start = (f32[11,32,128]{2,1,0:T(8,128)S(1)}, f32[11,32,128]{2,1,0:T(8,128)S(1)}, u32[]{:S(2)}, u32[]{:S(2)}) collective-permute-start(f32[11,32,128]{2,1,0:T(8,128)S(1)} %get-tuple-element.24), channel_id=1, source_target_pairs={{16,32},{48,64},{80,96},{112,128},{144,160},{176,192},{208,224},{3... | collective-permute-start | bytes 540680 | tf_op jit(solution)/shard_map/ppermute | solution.py:664
  2.9 18.2 %collective-permute-start.1 = (f32[11,32,128]{2,1,0:T(8,128)S(1)}, f32[11,32,128]{2,1,0:T(8,128)S(1)}, u32[]{:S(2)}, u32[]{:S(2)}) collective-permute-start(f32[11,32,128]{2,1,0:T(8,128)S(1)} %get-tuple-element.25), channel_id=1, source_target_pairs={{0,16},{32,48},{64,80},{96,112},{128,144},{160,176},{192,208},{224... | collective-permute-start | bytes 540680 | tf_op jit(solution)/shard_map/ppermute | solution.py:665
  7.7 15.6 %copy-start = (f32[32,32,128]{2,1,0:T(8,128)S(1)}, f32[32,32,128]{2,1,0:T(8,128)}, u32[]{:S(2)}) copy-start(f32[32,32,128]{2,1,0:T(8,128)} %t_ref.1) | copy-start | bytes 1572868
  7.7 15.6 %copy-start.1 = (s32[32,32,128]{2,1,0:T(8,128)S(1)}, s32[32,32,128]{2,1,0:T(8,128)}, u32[]{:S(2)}) copy-start(s32[32,32,128]{2,1,0:T(8,128)} %id_ref.1) | copy-start | bytes 1572868
  21.2 7.5 %collective-permute-start.2 = (f32[59,8,128]{2,1,0:T(8,128)S(1)}, f32[59,8,128]{2,1,0:T(8,128)S(1)}, u32[]{:S(2)}, u32[]{:S(2)}) collective-permute-start(f32[59,8,128]{2,1,0:T(8,128)S(1)} %get-tuple-element.33), channel_id=1, source_target_pairs={{1,2},{3,4},{5,6},{7,8},{9,10},{11,12},{13,14},{2,1},{4,3},{6,5},{... | collective-permute-start | bytes 725000 | tf_op jit(solution)/shard_map/ppermute | solution.py:679
  23.1 0.7 copy-start.3
  23.1 0.7 copy-start.4
  23.1 5.5 %collective-permute-start.3 = (f32[59,8,128]{2,1,0:T(8,128)S(1)}, f32[59,8,128]{2,1,0:T(8,128)S(1)}, u32[]{:S(2)}, u32[]{:S(2)}) collective-permute-start(f32[59,8,128]{2,1,0:T(8,128)S(1)} %get-tuple-element.34), channel_id=1, source_target_pairs={{0,1},{2,3},{4,5},{6,7},{8,9},{10,11},{12,13},{14,15},{1,0},{3,2},... | collective-permute-start | bytes 725000 | tf_op jit(solution)/shard_map/ppermute | solution.py:680

commit v4 on v3

--- a/solution.py
+++ b/solution.py
@@ -181,28 +181,84 @@
     return jnp.where(ident >= 2, high, low)
 
 
-def element(temp, ident, ref_ref, grad_ref, store_ref):
+def up_z(v):
+    return pltpu.roll(v, NZ - 1, 1)
+
+
+def down_z(v):
+    return pltpu.roll(v, 1, 1)
+
+
+def cells(temp, ident, chip, tables, inside=None):
+    ref_ref, grad_ref, store_ref = tables
     conduct = pick(ident, ref_ref) * (
         1.0 + pick(ident, grad_ref) * jnp.tanh(temp - kelvin_shift_amount)
     )
-    return conduct, pick(ident, store_ref)
+    if inside is not None:
+        conduct = conduct * inside
+    lanes = lane(temp.shape)
+    inner_z = jnp.where(lanes < NZ - 1, 1.0, 0.0).astype(f32)
+    edge_z = jnp.where((lanes == 0) | (lanes == NZ - 1), 1.0, 0.0).astype(f32)
+    e_z = (conduct + up_z(conduct)) * inner_z
+    f_z = e_z * (up_z(temp) - temp)
+    c_b = conduct * edge_z
+    diag = (pick(ident, store_ref) + c_b) + (e_z + down_z(e_z))
+    resid = (clock_advance * interface_warming_rate * chip - c_b * temp) + (f_z - down_z(f_z))
+    return conduct, diag, resid, e_z
+
+
+def surface(read, terms):
+    rows = sublane((TILE, NZ))
+    lanes = lane((TILE, NZ))
+    total = jnp.zeros((TILE, NZ), f32)
+    for s in range(TILE):
+        one_hot = jnp.where((rows == s) & (lanes == 0), 1.0, 0.0).astype(bf16)
+        rest = read(s)
+        for _ in range(terms):
+            part = rest.astype(bf16)
+            total = total + lax.dot_general(
+                one_hot, part, (((1,), (1,)), ((), ())), preferred_element_type=f32
+            )
+            rest = rest - part.astype(f32)
+    return total
+
+
+def own_rows(ref):
+    per = NX // TILE
+    return lambda s: jnp.concatenate([ref[per * s + i, :NY, :] for i in range(per)], axis=0)
 
 
 def own_kernel(
-    ref_ref, grad_ref, store_ref, t_ref, id_ref, chip_ref, sites_in, tp, cp, capp, chp, sites_out
+    ref_ref,
+    grad_ref,
+    store_ref,
+    t_ref,
+    id_ref,
+    chip_ref,
+    sites_in,
+    tp,
+    cp,
+    dp,
+    rp,
+    ez,
+    surf_ref,
+    sites_out,
 ):
     del sites_in, sites_out
+    tables = (ref_ref, grad_ref, store_ref)
 
     def own_plane(q, _):
         temp = t_ref[q]
-        conduct, store = element(temp, id_ref[q], ref_ref, grad_ref, store_ref)
+        conduct, diag, resid, e_z = cells(temp, id_ref[q], chip_ref[q].astype(f32), tables)
         tp[q, :NY, :] = temp
         cp[q, :NY, :] = conduct
-        capp[q, :NY, :] = store
-        chp[q, :NY, :] = clock_advance * interface_warming_rate * chip_ref[q].astype(f32)
+        dp[q, :NY, :] = diag
+        rp[q, :NY, :] = resid
+        ez[q, :NY, :] = e_z
         return 0
 
     lax.fori_loop(0, NX, own_plane, 0, unroll=4)
+    surf_ref[...] = surface(own_rows(t_ref), 3)
 
 
 def krylov_kernel(
@@ -211,26 +267,29 @@
     store_ref,
     tp_in,
     cp_in,
-    capp_in,
-    chp_in,
+    dp_in,
+    rp_in,
+    ez_in,
+    surf_ref,
     xa_ref,
     xb_ref,
     ya_ref,
     yb_ref,
     tp,
     cp,
-    capp,
-    chp,
+    dp,
+    rp,
+    ez,
     w0_ref,
     w1_ref,
     w2_ref,
     send_ref,
     ex,
     ey,
-    ez,
     dinv,
 ):
-    del tp_in, cp_in, capp_in, chp_in
+    del tp_in, cp_in, dp_in, rp_in, ez_in
+    tables = (ref_ref, grad_ref, store_ref)
     ix = lax.axis_index("gx")
     iy = lax.axis_index("gy")
     last_x = lax.axis_size("gx") - 1
@@ -242,7 +301,6 @@
     low_y = jnp.where(iy > 0, 1.0, 0.0).astype(f32)
     high_y = jnp.where(iy < last_y, 1.0, 0.0).astype(f32)
     rows_halo = jnp.where(sub < 4, high_y, low_y)
-    rate = clock_advance * interface_warming_rate
 
     even_x = lax.rem(ix, 2) == 0
     even_y = lax.rem(iy, 2) == 0
@@ -265,11 +323,12 @@
         temp = jnp.where(sub < 4, high, low)
         ident = jnp.where(sub < 4, pltpu.roll(high, 4, 0), pltpu.roll(low, 3, 0))
         chip = jnp.where(sub < 4, chip_high, pltpu.roll(low, 6, 0))
-        conduct, store = element(temp, ident, ref_ref, grad_ref, store_ref)
+        conduct, diag, resid, e_z = cells(temp, ident, chip, tables, rows_halo * plane_in)
         tp[q, NY:, :] = temp
-        cp[q, NY:, :] = conduct * (rows_halo * plane_in)
-        capp[q, NY:, :] = store
-        chp[q, NY:, :] = rate * chip
+        cp[q, NY:, :] = conduct
+        dp[q, NY:, :] = diag
+        rp[q, NY:, :] = resid
+        ez[q, NY:, :] = e_z
 
     def own_halo_first(q, _):
         put_halo(q, high_row(PX + q), one)
@@ -286,11 +345,12 @@
     zero_tile = jnp.zeros((TILE, NZ), f32)
 
     def side_plane(q, temp, ident, chip, plane_in):
-        conduct, store = element(temp, ident, ref_ref, grad_ref, store_ref)
+        conduct, diag, resid, e_z = cells(temp, ident, chip, tables, plane_in)
         tp[q, :NY, :] = temp
-        cp[q, :NY, :] = conduct * plane_in
-        capp[q, :NY, :] = store
-        chp[q, :NY, :] = rate * chip
+        cp[q, :NY, :] = conduct
+        dp[q, :NY, :] = diag
+        rp[q, :NY, :] = resid
+        ez[q, :NY, :] = e_z
         put_halo(q, pltpu.roll(high_row(PX + q - PAIRS), 4, 0), plane_in)
 
     for k in range(HIGH):
@@ -310,12 +370,8 @@
             low_x,
         )
 
-    lanes = lane((PY, NZ))
     subs = sublane((PY, NZ))
-    inner_z = jnp.where(lanes < NZ - 1, 1.0, 0.0).astype(f32)
-    edge_z = jnp.where((lanes == 0) | (lanes == NZ - 1), 1.0, 0.0).astype(f32)
     rows_in = jnp.where(subs < NY, 1.0, jnp.where(subs < NY + 4, high_y, low_y)).astype(f32)
-    lane_tile = lane((TILE, NZ))
 
     def up_y(v):
         return pltpu.roll(v, PY - 1, 0)
@@ -323,22 +379,8 @@
     def down_y(v):
         return pltpu.roll(v, 1, 0)
 
-    def up_z(v):
-        return pltpu.roll(v, NZ - 1, 1)
-
-    def down_z(v):
-        return pltpu.roll(v, 1, 1)
-
     def fold(v):
         return (v[0:8] + v[8:16]) + (v[16:24] + v[24:32])
-
-    def surface(acc, plane, x):
-        for t in range(NY // TILE):
-            part = plane[TILE * t : TILE * (t + 1)]
-            acc = jnp.where(
-                lane_tile == x * 4 + t, jnp.broadcast_to(part[:, 0:1], (TILE, NZ)), acc
-            )
-        return acc
 
     def faces(q, nxt, ex_before, fx_before, plane_in):
         c0 = cp[q]
@@ -347,20 +389,12 @@
         f_x = e_x * (tp[nxt] - t0)
         e_y = c0 + up_y(c0)
         f_y = e_y * (up_y(t0) - t0)
-        e_z = (c0 + up_z(c0)) * inner_z
-        f_z = e_z * (up_z(t0) - t0)
-        c_b = c0 * edge_z
-        diag = (capp[q] + c_b) + (
-            (e_x + ex_before) + ((e_y + down_y(e_y)) + (e_z + down_z(e_z)))
-        )
+        diag = dp[q] + ((e_x + ex_before) + (e_y + down_y(e_y)))
         inverse = (rows_in * plane_in) / diag
-        resid = (chp[q] - c_b * t0) + (
-            (f_x - fx_before) + ((f_y - down_y(f_y)) + (f_z - down_z(f_z)))
-        )
+        resid = rp[q] + ((f_x - fx_before) + (f_y - down_y(f_y)))
         first = resid * inverse
         ex[q] = e_x
         ey[q] = e_y
-        ez[q] = e_z
         dinv[q] = inverse
         w0_ref[q] = first
         return e_x, f_x, resid, first
@@ -371,14 +405,11 @@
         carry = faces(q, nxt, carry[0], carry[1], low_x)[:2]
 
     def faces_own(q, state):
-        e_b, f_b, m0, s_t, s_0 = state
+        e_b, f_b, m0 = state
         e_x, f_x, resid, first = faces(q, q + 1, e_b, f_b, one)
-        m0 = m0 + fold(resid[:NY] * first[:NY])
-        return e_x, f_x, m0, surface(s_t, tp[q, :NY, :], q), surface(s_0, first, q)
-
-    e_b, f_b, m0, surf_t, surf_0 = lax.fori_loop(
-        0, NX, faces_own, (carry[0], carry[1], zero_tile, zero_tile, zero_tile), unroll=8
-    )
+        return e_x, f_x, m0 + fold(resid[:NY] * first[:NY])
+
+    e_b, f_b, m0 = lax.fori_loop(0, NX, faces_own, (carry[0], carry[1], zero_tile), unroll=8)
     carry = (e_b, f_b)
     for q in (32, 33, 34):
         carry = faces(q, q + 1, carry[0], carry[1], high_x)[:2]
@@ -400,24 +431,22 @@
             dst[q] = dinv[q] * total
 
         def step(q, state):
-            g, ma, mb, surf = state
+            g, ma, mb = state
             total, v, g = neighbours(src, q, q + 1, g)
             new = dinv[q] * total
             dst[q] = new
             ma = ma + fold(total[:NY] * v[:NY])
             mb = mb + fold(total[:NY] * new[:NY])
-            return g, ma, mb, surface(surf, new, q)
-
-        carry, ma, mb, surf = lax.fori_loop(
-            0, NX, step, (carry, zero_tile, zero_tile, zero_tile), unroll=8
-        )
+            return g, ma, mb
+
+        carry, ma, mb = lax.fori_loop(0, NX, step, (carry, zero_tile, zero_tile), unroll=8)
         for q, nxt in epilogue:
             total, _, carry = neighbours(src, q, nxt, carry)
             dst[q] = dinv[q] * total
-        return ma, mb, surf
-
-    m1, m2, surf_1 = advance(w0_ref, w1_ref, 37, ((38, 0),), ((32, 33), (33, 34)))
-    m3, m4, surf_2 = advance(w1_ref, w2_ref, 38, (), ((32, 33),))
+        return ma, mb
+
+    m1, m2 = advance(w0_ref, w1_ref, 37, ((38, 0),), ((32, 33), (33, 34)))
+    m3, m4 = advance(w1_ref, w2_ref, 38, (), ((32, 33),))
 
     def last(q, acc):
         v = w2_ref[q]
@@ -430,8 +459,9 @@
     moments = zero_tile
     for k, m in enumerate((m0, m1, m2, m3, m4, m5)):
         moments = jnp.where(sub == k, jnp.sum(m, axis=0, keepdims=True), moments)
+    fields = [surf_ref[...]] + [surface(own_rows(w), 2) for w in (w0_ref, w1_ref, w2_ref)]
     for k in range(send_ref.shape[0]):
-        for j, tile in enumerate((surf_t, surf_0, surf_1, surf_2, moments)):
+        for j, tile in enumerate((*fields, moments)):
             send_ref[k, TILE * j : TILE * (j + 1), :] = tile
 
 
@@ -462,42 +492,45 @@
         row = site // width
         col = site - row * width
         here = (col // NY) == iy
-        y = col % NY
-        row_of = jnp.where(here, (row // NX) * TILE + y % TILE, -1)
-        lane_of = (row % NX) * (NY // TILE) + y // TILE
-        hot = jnp.concatenate(
-            [
-                jnp.where(
-                    subs == jnp.broadcast_to(row_of[s : s + 1], (NZ, NZ)), 1.0, 0.0
-                ).astype(bf16)
-                for s in range(TILE)
-            ],
-            axis=1,
-        )
-        hot = jnp.concatenate([hot, hot], axis=0)
+        cell = (row % NX) * NY + col % NY
+        row_of = jnp.where(here, (row // NX) * TILE + cell // NZ, -1)
+        lane_of = cell % NZ
         found = [zero] * FIELDS
-        lines = [
-            jnp.dot(parts[NZ * f : NZ * (f + 1)], hot, preferred_element_type=f32)
-            for f in range(fields)
-        ]
-        for s in range(TILE):
-            lanes = jnp.broadcast_to(lane_of[s : s + 1], (TILE, NZ))
-            rows = jnp.broadcast_to(row_of[s : s + 1], (TILE, NZ)) - sub
-            acc = [zero] * FIELDS
-            for a in range(blocks):
-                got = jnp.take_along_axis(table_ref[a, 0:TILE, :], lanes, axis=1)
-                acc[0] = jnp.where(rows == a * TILE, got, acc[0])
-            lanes = lanes - sub
-            for t in range(NZ // TILE):
-                hit = lanes == t * TILE
-                for f in range(fields):
-                    acc[f + 1] = jnp.where(
-                        hit,
-                        lines[f][TILE * t : TILE * (t + 1), NZ * s : NZ * (s + 1)],
-                        acc[f + 1],
+        for pair in range(0, TILE, 2):
+            hot = jnp.concatenate(
+                [
+                    jnp.where(
+                        subs == jnp.broadcast_to(row_of[s : s + 1], (NZ, NZ)), 1.0, 0.0
+                    ).astype(bf16)
+                    for s in (pair, pair + 1)
+                ],
+                axis=1,
+            )
+            hot = jnp.concatenate([hot, hot], axis=0)
+            lanes = [jnp.broadcast_to(lane_of[pair + i : pair + i + 1], (TILE, NZ)) for i in (0, 1)]
+            offset = [e - sub for e in lanes]
+            for i in (0, 1):
+                rows = jnp.broadcast_to(row_of[pair + i : pair + i + 1], (TILE, NZ)) - sub
+                acc = zero
+                for a in range(blocks):
+                    got = jnp.take_along_axis(table_ref[a, 0:TILE, :], lanes[i], axis=1)
+                    acc = jnp.where(rows == a * TILE, got, acc)
+                found[0] = jnp.where(
+                    sub == pair + i, jnp.sum(acc, axis=0, keepdims=True), found[0]
+                )
+            for f in range(fields):
+                line = jnp.dot(parts[NZ * f : NZ * (f + 1)], hot, preferred_element_type=f32)
+                for i in (0, 1):
+                    acc = zero
+                    for t in range(NZ // TILE):
+                        acc = jnp.where(
+                            offset[i] == t * TILE,
+                            line[TILE * t : TILE * (t + 1), NZ * i : NZ * (i + 1)],
+                            acc,
+                        )
+                    found[f + 1] = jnp.where(
+                        sub == pair + i, jnp.sum(acc, axis=0, keepdims=True), found[f + 1]
                     )
-            for f in range(FIELDS):
-                found[f] = jnp.where(sub == s, jnp.sum(acc[f], axis=0, keepdims=True), found[f])
         for f in range(FIELDS):
             out_ref[b, TILE * f : TILE * (f + 1), :] = found[f]
         out_ref[b, TILE * FIELDS :, :] = total
@@ -689,21 +722,21 @@
         own_kernel,
         name="own_cells",
         in_specs=[smem] * 3 + [vmem] * 4,
-        out_specs=[vmem] * 5,
-        out_shape=[padded] * 4 + [arr(size_y, TILE, NZ, dtype=i32)],
-        input_output_aliases={6: 4},
+        out_specs=[vmem] * 7,
+        out_shape=[padded] * 5 + [arr(TILE, NZ), arr(size_y, TILE, NZ, dtype=i32)],
+        input_output_aliases={6: 6},
         compiler_params=params(12),
     )(*tables, temp, ident, chip, sites)
 
     payload = TILE * (FIELDS + 1)
-    start, _, _, _, w0, w1, w2, send = pl.pallas_call(
+    start, _, _, _, _, w0, w1, w2, send = pl.pallas_call(
         krylov_kernel,
         name="krylov",
-        in_specs=[smem] * 3 + [vmem] * 8,
-        out_specs=[vmem] * 8,
-        out_shape=[padded] * 7 + [arr(size_x, payload, NZ)],
-        input_output_aliases={3: 0, 4: 1, 5: 2, 6: 3},
-        scratch_shapes=[buf(PX, PY, NZ)] * 4,
+        in_specs=[smem] * 3 + [vmem] * 10,
+        out_specs=[vmem] * 9,
+        out_shape=[padded] * 8 + [arr(size_x, payload, NZ)],
+        input_output_aliases={3: 0, 4: 1, 5: 2, 6: 3, 7: 4},
+        scratch_shapes=[buf(PX, PY, NZ)] * 3,
         compiler_params=params(24),
     )(*tables, *own, xa, xb, ya, yb)
     table = lax.all_to_all(send, "gx", 0, 0)

time: 77 us -> 75.6 us (0.982)
  waiting for transfers between devices: 3.95 us -> 2.28 us
    pallas_call x1, Pallas kernels: 0.92 us -> 2.59 us  [local(): pl.pallas_call(own_kernel, name='own_cells', in_specs=[smem] * 3 + [vmem]...]
    ppermute x1, waiting for transfers between devices: 3.94 us -> 2.28 us  [local(): ya = lax.ppermute(ya, 'gy', swaps(size_y, 1))]
    pallas_call x1, Pallas kernels: 6.46 us -> 5.55 us  [local(): pl.pallas_call(krylov_kernel, name='krylov', in_specs=[smem] * 3 + [vmem]...]
    all_to_all x1, blocking collectives: 13.7 us -> 12.8 us  [local(): got = lax.all_to_all(found, 'gy', 0, 0)]
    all_to_all x1, blocking collectives: 20.1 us -> 20.9 us  [local(): table = lax.all_to_all(send, 'gx', 0, 0)]
  transfers between devices with their start and end apart: 4 -> 4, of which waited for: 1 -> 1; matrix products, arithmetic and copies ran while one was open for 0% -> 0% of each run, Pallas kernels for 1% -> 3%
where the time goes in v4:
time: 75.6 us; the launch traced here: 75.3 us
  blocking collectives  47.2 us (62%)
  Pallas kernels  17.1 us (23%)
  starting transfers between devices  7.43 us (10%)
  waiting for transfers between devices  2.28 us (3%)
    all_to_all x1, blocking collectives, local(): table = lax.all_to_all(send, 'gx', 0, 0)  20.9 us
    all_to_all x1, blocking collectives, local(): sites = lax.all_to_all(sites, 'gy', 0, 0)  13.4 us
    all_to_all x1, blocking collectives, local(): got = lax.all_to_all(found, 'gy', 0, 0)  12.8 us
    pallas_call x1, Pallas kernels, local(): pl.pallas_call(lookup_kernel, name='lookup', in_specs=[vmem] * 2, out_spe...  5.66 us
    pallas_call x1, Pallas kernels, local(): pl.pallas_call(krylov_kernel, name='krylov', in_specs=[smem] * 3 + [vmem]...  5.55 us
    ppermute x1, starting transfers between devices, local(): xb = lax.ppermute(xb, 'gx', swaps(size_x, 0))  4.75 us
    pallas_call x1, Pallas kernels, local(): pl.pallas_call(own_kernel, name='own_cells', in_specs=[smem] * 3 + [vmem]...  2.59 us
    ppermute x1, waiting for transfers between devices, local(): ya = lax.ppermute(ya, 'gy', swaps(size_y, 1))  2.28 us
  transfers between devices with their start and end apart: 4, of which 1 were waited for; matrix products, arithmetic and copies ran while one was open for 0% of the time, Pallas kernels for 3%

profile of v4, /device:TPU:1, one launch (start us, length us, event | category | flops | bytes accessed | tf_op | source)
XLA Modules:
  0.0 75.3 jit_solution(16580534371230139328)
XLA Ops:
  0.6 0.0 copy-start.2
  0.6 0.0 copy-start.5
  0.7 1.6 %pack.1 = (f32[11,32,128]{2,1,0:T(8,128)S(1)}, f32[11,32,128]{2,1,0:T(8,128)S(1)}, f32[59,8,128]{2,1,0:T(8,128)S(1)}, f32[59,8,128]{2,1,0:T(8,128)S(1)}, s32[16,8,128]{2,1,0:T(8,128)S(1)}) custom-call(f32[32,32,128]{2,1,0:T(8,128)} %t_ref.1, s32[32,32,128]{2,1,0:T(8,128)} %id_ref.1, s32[32,32,128]{2,1,0:T(8,128)} %chip_ref.1, s32[8,128]{1,0:T(8,128)} %bitcast.3), custom_call_target="tpu_custom_call" | custom-call | tf_op jit(solution)/shard_map/pack/pallas_call | solution.py:665
  2.3 0.7 collective-permute-start
  2.9 4.7 %collective-permute-start.1 = (f32[11,32,128]{2,1,0:T(8,128)S(1)}, f32[11,32,128]{2,1,0:T(8,128)S(1)}, u32[]{:S(2)}, u32[]{:S(2)}) collective-permute-start(f32[11,32,128]{2,1,0:T(8,128)S(1)} %get-tuple-element.27), channel_id=1, source_target_pairs={{0,16},{32,48},{64,80},{96,112},{128,144},{160,176},{192,208},{224... | collective-permute-start | bytes 540680 | tf_op jit(solution)/shard_map/ppermute | solution.py:698
  7.7 0.0 copy-start
  7.7 0.0 copy-start.1
  7.7 13.4 %all_to_all.15.sites_in = s32[16,8,128]{2,1,0:T(8,128)S(1)} all-to-all(s32[16,8,128]{2,1,0:T(8,128)S(1)} %get-tuple-element.28), channel_id=1, replica_groups=mesh['gx'=16,'gy'=16] {'gy'}, dimensions={0} | all-to-all | bytes 131072 | tf_op jit(solution)/shard_map/all_to_all | solution.py:695
  21.1 0.0 collective-permute-done.xa_ref
  21.1 0.0 collective-permute-done.1.xb_ref
  21.2 1.9 %collective-permute-start.2 = (f32[59,8,128]{2,1,0:T(8,128)S(1)}, f32[59,8,128]{2,1,0:T(8,128)S(1)}, u32[]{:S(2)}, u32[]{:S(2)}) collective-permute-start(f32[59,8,128]{2,1,0:T(8,128)S(1)} %get-tuple-element.37), channel_id=1, source_target_pairs={{1,2},{3,4},{5,6},{7,8},{9,10},{11,12},{13,14},{2,1},{4,3},{6,5},{... | collective-permute-start | bytes 725000 | tf_op jit(solution)/shard_map/ppermute | solution.py:712
  23.1 0.0 copy-start.3
  23.1 0.0 copy-start.4
  23.1 0.1 collective-permute-start.3
  23.2 0.0 copy-done.2
  23.2 0.0 copy-done.5
  23.2 0.0 copy-done
  23.2 0.0 copy-done.1
  23.3 0.5 copy-done.3
  23.7 0.0 copy-done.4
  23.8 2.6 %own_cells.1 = (f32[39,40,128]{2,1,0:T(8,128)S(1)}, f32[39,40,128]{2,1,0:T(8,128)S(1)}, f32[39,40,128]{2,1,0:T(8,128)S(1)}, f32[39,40,128]{2,1,0:T(8,128)S(1)}, ...) custom-call(f32[4]{0:T(128)S(1)} %copy-done.3, ...), custom_call_target="tpu_custom_call", output_to_operand_aliasing={{6}: (6, {})} | custom-call | tf_op jit(solution)/shard_map/own_cells/pallas_call | solution.py:721
  26.4 2.3 %collective-permute-done.2.ya_ref = f32[59,8,128]{2,1,0:T(8,128)S(1)} collective-permute-done((f32[59,8,128]{2,1,0:T(8,128)S(1)}, f32[59,8,128]{2,1,0:T(8,128)S(1)}, u32[]{:S(2)}, u32[]{:S(2)}) %collective-permute-start.2) | collective-permute-done | bytes 241696 | tf_op jit(solution)/shard_map/ppermute | solution.py:712
  28.6 0.0 collective-permute-done.3.yb_ref
  28.6 5.6 %krylov.1 = (f32[39,40,128]{2,1,0:T(8,128)S(1)}, f32[39,40,128]{2,1,0:T(8,128)S(1)}, f32[39,40,128]{2,1,0:T(8,128)S(1)}, f32[39,40,128]{2,1,0:T(8,128)S(1)}, f32...) custom-call(f32[4]{0:T(128)S(1)} %copy-done.3, ...), custom_call_target="tpu_custom_call", output_to_operand_aliasing={{0}: (3, {}), {1}: (4, {}), {2}: (5, {}), {3}: (6, {}), {4}... | custom-call | tf_op jit(solution)/shard_map/krylov/pallas_call | solution.py:732
  34.2 20.9 %all_to_all.16.table_ref = f32[16,40,128]{2,1,0:T(8,128)S(1)} all-to-all(f32[16,40,128]{2,1,0:T(8,128)S(1)} %get-tuple-element.39), channel_id=1, replica_groups=mesh['gx'=16,'gy'=16] {'gx'}, dimensions={0} | all-to-all | bytes 655360 | tf_op jit(solution)/shard_map/all_to_all | solution.py:742
  55.1 5.7 %lookup.1 = f32[16,40,128]{2,1,0:T(8,128)S(1)} custom-call(s32[16,8,128]{2,1,0:T(8,128)S(1)} %get-tuple-element.30.site_ref, f32[16,40,128]{2,1,0:T(8,128)S(1)} %all_to_all.16.table_ref), custom_call_target="tpu_custom_call" | custom-call | tf_op jit(solution)/shard_map/lookup/pallas_call | solution.py:743
  60.8 12.8 %all_to_all.17.got_ref = f32[16,40,128]{2,1,0:T(8,128)S(1)} all-to-all(f32[16,40,128]{2,1,0:T(8,128)S(1)} %lookup.1), channel_id=1, replica_groups=mesh['gx'=16,'gy'=16] {'gy'}, dimensions={0} | all-to-all | bytes 655360 | tf_op jit(solution)/shard_map/all_to_all | solution.py:752
  73.6 1.7 %finish.1 = (f32[32,32,128]{2,1,0:T(8,128)}, f32[8,128]{1,0:T(8,128)}) custom-call(f32[16,40,128]{2,1,0:T(8,128)S(1)} %all_to_all.17.got_ref, f32[8,128]{1,0:T(8,128)} %bitcast.4, f32[39,40,128]{2,1,0:T(8,128)S(1)} %get-tuple-element.40.t_ref, f32[39,40,128]{2,1,0:T(8,128)S(1)} %get-tuple-element.41.w0_ref, f32[39,40,128]{2,1,0:T(8,128)S(1)} %get-tuple-element.42.w1_ref, ...), custom_call_target="tpu_custom_call" | custom-call | tf_op jit(solution)/shard_map/finish/pallas_call | solution.py:753
  (1 shorter events, 0.0 us)
Async XLA Ops:
  0.6 22.6 %copy-start.2 = (s32[32,32,128]{2,1,0:T(8,128)S(1)}, s32[32,32,128]{2,1,0:T(8,128)}, u32[]{:S(2)}) copy-start(s32[32,32,128]{2,1,0:T(8,128)} %chip_ref.1) | copy-start | bytes 1572868
  0.6 22.6 %copy-start.5 = (f32[4]{0:T(128)S(1)}, f32[4]{0:T(128)}, u32[]{:S(2)}) copy-start(f32[4]{0:T(128)} %store_ref.3) | copy-start | bytes 52
  2.3 18.9 %collective-permute-start = (f32[11,32,128]{2,1,0:T(8,128)S(1)}, f32[11,32,128]{2,1,0:T(8,128)S(1)}, u32[]{:S(2)}, u32[]{:S(2)}) collective-permute-start(f32[11,32,128]{2,1,0:T(8,128)S(1)} %get-tuple-element.26), channel_id=1, source_target_pairs={{16,32},{48,64},{80,96},{112,128},{144,160},{176,192},{208,224},{3... | collective-permute-start | bytes 540680 | tf_op jit(solution)/shard_map/ppermute | solution.py:697
  2.9 18.2 %collective-permute-start.1 = (f32[11,32,128]{2,1,0:T(8,128)S(1)}, f32[11,32,128]{2,1,0:T(8,128)S(1)}, u32[]{:S(2)}, u32[]{:S(2)}) collective-permute-start(f32[11,32,128]{2,1,0:T(8,128)S(1)} %get-tuple-element.27), channel_id=1, source_target_pairs={{0,16},{32,48},{64,80},{96,112},{128,144},{160,176},{192,208},{224... | collective-permute-start | bytes 540680 | tf_op jit(solution)/shard_map/ppermute | solution.py:698
  7.7 15.6 %copy-start = (f32[32,32,128]{2,1,0:T(8,128)S(1)}, f32[32,32,128]{2,1,0:T(8,128)}, u32[]{:S(2)}) copy-start(f32[32,32,128]{2,1,0:T(8,128)} %t_ref.1) | copy-start | bytes 1572868
  7.7 15.6 %copy-start.1 = (s32[32,32,128]{2,1,0:T(8,128)S(1)}, s32[32,32,128]{2,1,0:T(8,128)}, u32[]{:S(2)}) copy-start(s32[32,32,128]{2,1,0:T(8,128)} %id_ref.1) | copy-start | bytes 1572868
  21.2 7.5 %collective-permute-start.2 = (f32[59,8,128]{2,1,0:T(8,128)S(1)}, f32[59,8,128]{2,1,0:T(8,128)S(1)}, u32[]{:S(2)}, u32[]{:S(2)}) collective-permute-start(f32[59,8,128]{2,1,0:T(8,128)S(1)} %get-tuple-element.37), channel_id=1, source_target_pairs={{1,2},{3,4},{5,6},{7,8},{9,10},{11,12},{13,14},{2,1},{4,3},{6,5},{... | collective-permute-start | bytes 725000 | tf_op jit(solution)/shard_map/ppermute | solution.py:712
  23.1 0.7 copy-start.3
  23.1 0.7 copy-start.4
  23.1 5.5 %collective-permute-start.3 = (f32[59,8,128]{2,1,0:T(8,128)S(1)}, f32[59,8,128]{2,1,0:T(8,128)S(1)}, u32[]{:S(2)}, u32[]{:S(2)}) collective-permute-start(f32[59,8,128]{2,1,0:T(8,128)S(1)} %get-tuple-element.38), channel_id=1, source_target_pairs={{0,1},{2,3},{4,5},{6,7},{8,9},{10,11},{12,13},{14,15},{1,0},{3,2},... | collective-permute-start | bytes 725000 | tf_op jit(solution)/shard_map/ppermute | solution.py:713

commit v5 on v4

--- a/solution.py
+++ b/solution.py
@@ -209,17 +209,18 @@
 
 def surface(read, terms):
     rows = sublane((TILE, NZ))
-    lanes = lane((TILE, NZ))
+    diagonal = sublane((NZ, NZ)) == lane((NZ, NZ))
+    first = jnp.where(sublane((NZ, NZ)) == 0, 1.0, 0.0).astype(bf16)
     total = jnp.zeros((TILE, NZ), f32)
     for s in range(TILE):
-        one_hot = jnp.where((rows == s) & (lanes == 0), 1.0, 0.0).astype(bf16)
         rest = read(s)
+        line = jnp.zeros((NZ, NZ), f32)
         for _ in range(terms):
             part = rest.astype(bf16)
-            total = total + lax.dot_general(
-                one_hot, part, (((1,), (1,)), ((), ())), preferred_element_type=f32
-            )
+            line = line + jnp.dot(part, first, preferred_element_type=f32)
             rest = rest - part.astype(f32)
+        line = jnp.sum(jnp.where(diagonal, line, 0.0), axis=0, keepdims=True)
+        total = jnp.where(rows == s, line, total)
     return total
 
 
@@ -232,32 +233,90 @@
     ref_ref,
     grad_ref,
     store_ref,
-    t_ref,
-    id_ref,
-    chip_ref,
-    sites_in,
+    t_hbm,
+    id_hbm,
+    chip_hbm,
+    xa_ref,
+    xb_ref,
+    site_ref,
     tp,
     cp,
     dp,
     rp,
     ez,
     surf_ref,
-    sites_out,
+    hot_ref,
+    row_ref,
+    lane_ref,
+    t_ref,
+    id_ref,
+    chip_ref,
+    sems,
 ):
-    del sites_in, sites_out
     tables = (ref_ref, grad_ref, store_ref)
-
-    def own_plane(q, _):
-        temp = t_ref[q]
-        conduct, diag, resid, e_z = cells(temp, id_ref[q], chip_ref[q].astype(f32), tables)
+    ix = lax.axis_index("gx")
+    iy = lax.axis_index("gy")
+
+    copies = [
+        pltpu.make_async_copy(src, dst, sems.at[k])
+        for k, (src, dst) in enumerate(((t_hbm, t_ref), (id_hbm, id_ref), (chip_hbm, chip_ref)))
+    ]
+    for copy in copies:
+        copy.start()
+
+    width = NY * lax.axis_size("gy")
+    subs = sublane((NZ, NZ))
+
+    def places(b, _):
+        site = site_ref[b]
+        row = site // width
+        col = site - row * width
+        here = (col // NY) == iy
+        cell = (row % NX) * NY + col % NY
+        row_of = jnp.where(here, (row // NX) * TILE + cell // NZ, -1)
+        row_ref[b] = row_of
+        lane_ref[b] = cell % NZ
+        for s in range(TILE):
+            hit = subs == jnp.broadcast_to(row_of[s : s + 1], (NZ, NZ))
+            hot_ref[b, :, NZ * s : NZ * (s + 1)] = jnp.where(hit, 1.0, 0.0).astype(bf16)
+        return 0
+
+    lax.fori_loop(0, site_ref.shape[0], places, 0, unroll=2)
+    for copy in copies:
+        copy.wait()
+
+    def put(q, temp, ident, chip, inside=None):
+        conduct, diag, resid, e_z = cells(temp, ident, chip, tables, inside)
         tp[q, :NY, :] = temp
         cp[q, :NY, :] = conduct
         dp[q, :NY, :] = diag
         rp[q, :NY, :] = resid
         ez[q, :NY, :] = e_z
+
+    def own_plane(q, _):
+        put(q, t_ref[q], id_ref[q], chip_ref[q].astype(f32))
         return 0
 
     lax.fori_loop(0, NX, own_plane, 0, unroll=4)
+
+    even_x = lax.rem(ix, 2) == 0
+    low_x = jnp.where(ix > 0, 1.0, 0.0).astype(f32)
+    high_x = jnp.where(ix < lax.axis_size("gx") - 1, 1.0, 0.0).astype(f32)
+    zero_plane = jnp.zeros((NY, NZ), f32)
+
+    def high_plane(k):
+        return jnp.where(even_x, xb_ref[k], xa_ref[k])
+
+    def low_plane(k):
+        return jnp.where(even_x, xa_ref[k], xb_ref[k])
+
+    for k in range(HIGH):
+        chip = high_plane(8 + k) if k < 3 else zero_plane
+        put(NX + k, high_plane(k), high_plane(4 + k), chip, high_x)
+    for k in range(LOW):
+        chip = low_plane(5 + k) if k > 0 else zero_plane
+        put(NX + HIGH + k, low_plane(k), low_plane(3 + k), chip, low_x)
+
     surf_ref[...] = surface(own_rows(t_ref), 3)
 
 
@@ -271,8 +330,6 @@
     rp_in,
     ez_in,
     surf_ref,
-    xa_ref,
-    xb_ref,
     ya_ref,
     yb_ref,
     tp,
@@ -302,7 +359,6 @@
     high_y = jnp.where(iy < last_y, 1.0, 0.0).astype(f32)
     rows_halo = jnp.where(sub < 4, high_y, low_y)
 
-    even_x = lax.rem(ix, 2) == 0
     even_y = lax.rem(iy, 2) == 0
 
     def high_row(q):
@@ -310,12 +366,6 @@
 
     def low_row(q):
         return jnp.where(even_y, ya_ref[q], yb_ref[q])
-
-    def high_plane(k):
-        return jnp.where(even_x, xb_ref[k], xa_ref[k])
-
-    def low_plane(k):
-        return jnp.where(even_x, xa_ref[k], xb_ref[k])
 
     def put_halo(q, chip_high, plane_in):
         high = high_row(q)
@@ -338,37 +388,12 @@
         put_halo(q, pltpu.roll(high_row(PX + q - PAIRS), 4, 0), one)
         return 0
 
-    lax.fori_loop(0, PAIRS, own_halo_first, 0, unroll=5)
-    lax.fori_loop(PAIRS, NX, own_halo_second, 0, unroll=6)
-
-    zero_plane = jnp.zeros((NY, NZ), f32)
+    lax.fori_loop(0, PAIRS, own_halo_first, 0, unroll=20)
+    lax.fori_loop(PAIRS, NX, own_halo_second, 0, unroll=12)
+
     zero_tile = jnp.zeros((TILE, NZ), f32)
-
-    def side_plane(q, temp, ident, chip, plane_in):
-        conduct, diag, resid, e_z = cells(temp, ident, chip, tables, plane_in)
-        tp[q, :NY, :] = temp
-        cp[q, :NY, :] = conduct
-        dp[q, :NY, :] = diag
-        rp[q, :NY, :] = resid
-        ez[q, :NY, :] = e_z
-        put_halo(q, pltpu.roll(high_row(PX + q - PAIRS), 4, 0), plane_in)
-
-    for k in range(HIGH):
-        side_plane(
-            NX + k,
-            high_plane(k),
-            high_plane(4 + k),
-            high_plane(8 + k) if k < 3 else zero_plane,
-            high_x,
-        )
-    for k in range(LOW):
-        side_plane(
-            NX + HIGH + k,
-            low_plane(k),
-            low_plane(3 + k),
-            low_plane(5 + k) if k > 0 else zero_plane,
-            low_x,
-        )
+    for q in range(NX, PX):
+        put_halo(q, pltpu.roll(high_row(PX + q - PAIRS), 4, 0), high_x if q < NX + HIGH else low_x)
 
     subs = sublane((PY, NZ))
     rows_in = jnp.where(subs < NY, 1.0, jnp.where(subs < NY + 4, high_y, low_y)).astype(f32)
@@ -409,7 +434,7 @@
         e_x, f_x, resid, first = faces(q, q + 1, e_b, f_b, one)
         return e_x, f_x, m0 + fold(resid[:NY] * first[:NY])
 
-    e_b, f_b, m0 = lax.fori_loop(0, NX, faces_own, (carry[0], carry[1], zero_tile), unroll=8)
+    e_b, f_b, m0 = lax.fori_loop(0, NX, faces_own, (carry[0], carry[1], zero_tile), unroll=16)
     carry = (e_b, f_b)
     for q in (32, 33, 34):
         carry = faces(q, q + 1, carry[0], carry[1], high_x)[:2]
@@ -446,14 +471,29 @@
         return ma, mb
 
     m1, m2 = advance(w0_ref, w1_ref, 37, ((38, 0),), ((32, 33), (33, 34)))
-    m3, m4 = advance(w1_ref, w2_ref, 38, (), ((32, 33),))
-
-    def last(q, acc):
-        v = w2_ref[q]
-        half = ex[q] * w2_ref[q + 1] + (ey[q] * up_y(v) + ez[q] * up_z(v))
-        return acc + fold(half[:NY] * v[:NY])
-
-    m5 = lax.fori_loop(0, NX, last, zero_tile, unroll=8)
+
+    def crossing(q, v, after):
+        half = ex[q] * after + (ey[q] * up_y(v) + ez[q] * up_z(v))
+        return fold(half[:NY] * v[:NY])
+
+    def second(q, g):
+        total, v, g = neighbours(w1_ref, q, q + 1, g)
+        new = dinv[q] * total
+        w2_ref[q] = new
+        return g, new, fold(total[:NY] * v[:NY]), fold(total[:NY] * new[:NY])
+
+    g, before, m3, m4 = second(0, ex[38] * w1_ref[38])
+
+    def step_2(q, state):
+        g, before, ma, mb, mc = state
+        g, new, a, b = second(q, g)
+        return g, new, ma + a, mb + b, mc + crossing(q - 1, before, new)
+
+    g, before, m3, m4, m5 = lax.fori_loop(
+        1, NX, step_2, (g, before, m3, m4, zero_tile), unroll=31
+    )
+    total, _, _ = neighbours(w1_ref, NX, NX + 1, g)
+    m5 = m5 + crossing(NX - 1, before, dinv[NX] * total)
     m5 = m5 + m5
 
     moments = zero_tile
@@ -465,13 +505,10 @@
             send_ref[k, TILE * j : TILE * (j + 1), :] = tile
 
 
-def lookup_kernel(site_ref, table_ref, out_ref, parts):
+def lookup_kernel(hot_ref, row_ref, lane_ref, table_ref, out_ref, parts):
     blocks = table_ref.shape[0]
-    targets = site_ref.shape[0]
-    iy = lax.axis_index("gy")
-    width = NY * lax.axis_size("gy")
+    targets = hot_ref.shape[0]
     sub = sublane((TILE, NZ))
-    subs = sublane((NZ, NZ))
     zero = jnp.zeros((TILE, NZ), f32)
     fields = FIELDS - 1
     for f in range(fields):
@@ -488,24 +525,11 @@
         total = total + table_ref[a, TILE * FIELDS :, :]
 
     def one(b, _):
-        site = site_ref[b]
-        row = site // width
-        col = site - row * width
-        here = (col // NY) == iy
-        cell = (row % NX) * NY + col % NY
-        row_of = jnp.where(here, (row // NX) * TILE + cell // NZ, -1)
-        lane_of = cell % NZ
+        row_of = row_ref[b]
+        lane_of = lane_ref[b]
         found = [zero] * FIELDS
         for pair in range(0, TILE, 2):
-            hot = jnp.concatenate(
-                [
-                    jnp.where(
-                        subs == jnp.broadcast_to(row_of[s : s + 1], (NZ, NZ)), 1.0, 0.0
-                    ).astype(bf16)
-                    for s in (pair, pair + 1)
-                ],
-                axis=1,
-            )
+            hot = hot_ref[b, :, NZ * pair : NZ * (pair + 2)]
             hot = jnp.concatenate([hot, hot], axis=0)
             lanes = [jnp.broadcast_to(lane_of[pair + i : pair + i + 1], (TILE, NZ)) for i in (0, 1)]
             offset = [e - sub for e in lanes]
@@ -718,37 +742,48 @@
         substance_storage_coefficient,
     )
     padded = arr(PX, PY, NZ)
-    *own, sites = pl.pallas_call(
+    *own, hot, row, place = pl.pallas_call(
         own_kernel,
         name="own_cells",
-        in_specs=[smem] * 3 + [vmem] * 4,
-        out_specs=[vmem] * 7,
-        out_shape=[padded] * 5 + [arr(TILE, NZ), arr(size_y, TILE, NZ, dtype=i32)],
-        input_output_aliases={6: 6},
-        compiler_params=params(12),
-    )(*tables, temp, ident, chip, sites)
+        in_specs=[smem] * 3 + [anywhere] * 3 + [vmem] * 3,
+        out_specs=[vmem] * 9,
+        out_shape=[padded] * 5
+        + [
+            arr(TILE, NZ),
+            arr(size_y, NZ, TILE * NZ, dtype=bf16),
+            arr(size_y, TILE, NZ, dtype=i32),
+            arr(size_y, TILE, NZ, dtype=i32),
+        ],
+        scratch_shapes=[
+            buf(NX, NY, NZ),
+            buf(NX, NY, NZ, dtype=i32),
+            buf(NX, NY, NZ, dtype=i32),
+            pltpu.SemaphoreType.DMA((3,)),
+        ],
+        compiler_params=params(14),
+    )(*tables, *in_hbm(temp, ident, chip), xa, xb, sites)
 
     payload = TILE * (FIELDS + 1)
     start, _, _, _, _, w0, w1, w2, send = pl.pallas_call(
         krylov_kernel,
         name="krylov",
-        in_specs=[smem] * 3 + [vmem] * 10,
+        in_specs=[smem] * 3 + [vmem] * 8,
         out_specs=[vmem] * 9,
         out_shape=[padded] * 8 + [arr(size_x, payload, NZ)],
         input_output_aliases={3: 0, 4: 1, 5: 2, 6: 3, 7: 4},
         scratch_shapes=[buf(PX, PY, NZ)] * 3,
         compiler_params=params(24),
-    )(*tables, *own, xa, xb, ya, yb)
+    )(*tables, *own, ya, yb)
     table = lax.all_to_all(send, "gx", 0, 0)
     found = pl.pallas_call(
         lookup_kernel,
         name="lookup",
-        in_specs=[vmem] * 2,
+        in_specs=[vmem] * 4,
         out_specs=vmem,
         out_shape=arr(size_y, payload, NZ),
         scratch_shapes=[buf(NZ * (FIELDS - 1), 2 * NZ, dtype=bf16)],
         compiler_params=params(20),
-    )(sites, table)
+    )(hot, row, place, table)
     got = lax.all_to_all(found, "gy", 0, 0)
     temperature, growth = pl.pallas_call(
         final_kernel,

time: 75.6 us -> 75 us (level)
  waiting for transfers between devices: 2.28 us -> 0.01 us
  local copies, waits for them, and re-layouts: 0.53 us -> 1.97 us
  Pallas kernels: 17.1 us -> 15.8 us
  blocking collectives: 47.2 us -> 48.1 us
    ppermute x1, waiting for transfers between devices: 2.28 us -> 0.01 us  [local(): ya = lax.ppermute(ya, 'gy', swaps(size_y, 1))]
    pallas_call x1, Pallas kernels: 5.55 us -> 3.47 us  [local(): pl.pallas_call(krylov_kernel, name='krylov', in_specs=[smem] * 3 + [vmem]...]
    all_to_all x1, blocking collectives: 12.8 us -> 14.6 us  [local(): got = lax.all_to_all(found, 'gy', 0, 0)]
    unnamed x12 -> x8, local copies, waits for them, and re-layouts: 0.53 us -> 1.97 us
    all_to_all x1, blocking collectives: 13.4 us -> 12.5 us  [local(): sites = lax.all_to_all(sites, 'gy', 0, 0)]
    pallas_call x2, Pallas kernels: 8.25 us -> 9.13 us  [the longest x1 5.22 us: local(): pl.pallas_call(lookup_kernel, name='lookup', in_specs=[vmem] * 4, out_spe...]
  transfers between devices with their start and end apart: 4 -> 4, of which waited for: 1 -> 0; matrix products, arithmetic and copies ran while one was open for 0% -> 0% of each run, Pallas kernels for 3% -> 5%
where the time goes in v5:
time: 75 us; the launch traced here: 74.7 us
  blocking collectives  48.1 us (64%)
  Pallas kernels  15.8 us (21%)
  starting transfers between devices  7.98 us (11%)
  local copies, waits for them, and re-layouts  1.97 us (3%)
    all_to_all x1, blocking collectives, local(): table = lax.all_to_all(send, 'gx', 0, 0)  21 us
    all_to_all x1, blocking collectives, local(): got = lax.all_to_all(found, 'gy', 0, 0)  14.6 us
    all_to_all x1, blocking collectives, local(): sites = lax.all_to_all(sites, 'gy', 0, 0)  12.5 us
    pallas_call x1, Pallas kernels, local(): pl.pallas_call(lookup_kernel, name='lookup', in_specs=[vmem] * 4, out_spe...  5.22 us
    ppermute x1, starting transfers between devices, local(): xb = lax.ppermute(xb, 'gx', swaps(size_x, 0))  4.75 us
    pallas_call x1, Pallas kernels, local(): pl.pallas_call(own_kernel, name='own_cells', in_specs=[smem] * 3 + [anywh...  3.91 us
    pallas_call x1, Pallas kernels, local(): pl.pallas_call(krylov_kernel, name='krylov', in_specs=[smem] * 3 + [vmem]...  3.47 us
    ppermute x1, starting transfers between devices, local(): ya = lax.ppermute(ya, 'gy', swaps(size_y, 1))  2.47 us
  transfers between devices with their start and end apart: 4, of which 0 were waited for; matrix products, arithmetic and copies ran while one was open for 0% of the time, Pallas kernels for 5%

profile of v5, /device:TPU:1, one launch (start us, length us, event | category | flops | bytes accessed | tf_op | source)
XLA Modules:
  0.0 74.7 jit_solution(13023539345762083564)
XLA Ops:
  0.6 0.0 copy-start.1
  0.6 1.6 %pack.1 = (f32[11,32,128]{2,1,0:T(8,128)S(1)}, f32[11,32,128]{2,1,0:T(8,128)S(1)}, f32[59,8,128]{2,1,0:T(8,128)S(1)}, f32[59,8,128]{2,1,0:T(8,128)S(1)}, s32[16,8,128]{2,1,0:T(8,128)S(1)}) custom-call(f32[32,32,128]{2,1,0:T(8,128)} %t_hbm.3, s32[32,32,128]{2,1,0:T(8,128)} %id_hbm.3, s32[32,32,128]{2,1,0:T(8,128)} %chip_hbm.3, s32[8,128]{1,0:T(8,128)} %bitcast.3), custom_call_target="tpu_custom_call" | custom-call | tf_op jit(solution)/shard_map/pack/pallas_call | solution.py:689
  2.2 0.7 collective-permute-start
  2.9 4.7 %collective-permute-start.1 = (f32[11,32,128]{2,1,0:T(8,128)S(1)}, f32[11,32,128]{2,1,0:T(8,128)S(1)}, u32[]{:S(2)}, u32[]{:S(2)}) collective-permute-start(f32[11,32,128]{2,1,0:T(8,128)S(1)} %get-tuple-element.27), channel_id=1, source_target_pairs={{0,16},{32,48},{64,80},{96,112},{128,144},{160,176},{192,208},{224... | collective-permute-start | bytes 540680 | tf_op jit(solution)/shard_map/ppermute | solution.py:722
  7.6 12.5 %all_to_all.15.sites_in = s32[16,8,128]{2,1,0:T(8,128)S(1)} all-to-all(s32[16,8,128]{2,1,0:T(8,128)S(1)} %get-tuple-element.30), channel_id=1, replica_groups=mesh['gx'=16,'gy'=16] {'gy'}, dimensions={0} | all-to-all | bytes 131072 | tf_op jit(solution)/shard_map/all_to_all | solution.py:719
  20.1 0.0 collective-permute-done.xa_ref
  20.1 0.0 collective-permute-done.1.xb_ref
  20.2 2.5 %collective-permute-start.2 = (f32[59,8,128]{2,1,0:T(8,128)S(1)}, f32[59,8,128]{2,1,0:T(8,128)S(1)}, u32[]{:S(2)}, u32[]{:S(2)}) collective-permute-start(f32[59,8,128]{2,1,0:T(8,128)S(1)} %get-tuple-element.41), channel_id=1, source_target_pairs={{1,2},{3,4},{5,6},{7,8},{9,10},{11,12},{13,14},{2,1},{4,3},{6,5},{... | collective-permute-start | bytes 725000 | tf_op jit(solution)/shard_map/ppermute | solution.py:736
  22.7 0.1 collective-permute-start.3
  22.8 0.0 copy-start
  22.8 0.6 copy-done
  23.4 0.0 copy-start.2
  23.4 0.7 copy-done.2
  24.1 0.0 copy-start.3
  24.1 0.7 copy-done.3
  24.7 3.9 %own_cells.1 = (f32[39,40,128]{2,1,0:T(8,128)S(1)}, f32[39,40,128]{2,1,0:T(8,128)S(1)}, f32[39,40,128]{2,1,0:T(8,128)S(1)}, f32[39,40,128]{2,1,0:T(8,128)S(1)}, ...) custom-call(f32[4]{0:T(128)S(1)} %copy-done, ...), custom_call_target="tpu_custom_call" | custom-call | tf_op jit(solution)/shard_map/own_cells/pallas_call | solution.py:745
  28.7 0.0 collective-permute-done.2.ya_ref
  28.7 0.0 collective-permute-done.3.yb_ref
  28.7 0.0 copy-done.1
  28.7 3.5 %krylov.1 = (f32[39,40,128]{2,1,0:T(8,128)S(1)}, f32[39,40,128]{2,1,0:T(8,128)S(1)}, f32[39,40,128]{2,1,0:T(8,128)S(1)}, f32[39,40,128]{2,1,0:T(8,128)S(1)}, f32...) custom-call(f32[4]{0:T(128)S(1)} %copy-done.1, ...), custom_call_target="tpu_custom_call", output_to_operand_aliasing={{0}: (3, {}), {1}: (4, {}), {2}: (5, {}), {3}: (6, {}), {4}... | custom-call | tf_op jit(solution)/shard_map/krylov/pallas_call | solution.py:767
  32.2 21.0 %all_to_all.16.table_ref = f32[16,40,128]{2,1,0:T(8,128)S(1)} all-to-all(f32[16,40,128]{2,1,0:T(8,128)S(1)} %get-tuple-element.43), channel_id=1, replica_groups=mesh['gx'=16,'gy'=16] {'gx'}, dimensions={0} | all-to-all | bytes 655360 | tf_op jit(solution)/shard_map/all_to_all | solution.py:777
  53.2 5.2 %lookup.1 = f32[16,40,128]{2,1,0:T(8,128)S(1)} custom-call(bf16[16,128,1024]{2,1,0:T(8,128)(2,1)S(1)} %get-tuple-element.32.hot_ref, s32[16,8,128]{2,1,0:T(8,128)S(1)} %get-tuple-element.33.row_ref, s32[16,8,128]{2,1,0:T(8,128)S(1)} %get-tuple-element.34.lane_ref, f32[16,40,128]{2,1,0:T(8,128)S(1)} %all_to_all.16.table_ref), custom_call_target="tpu_custom_call" | custom-call | tf_op jit(solution)/shard_map/lookup/pallas_call | solution.py:778
  58.4 14.6 %all_to_all.17.got_ref = f32[16,40,128]{2,1,0:T(8,128)S(1)} all-to-all(f32[16,40,128]{2,1,0:T(8,128)S(1)} %lookup.1), channel_id=1, replica_groups=mesh['gx'=16,'gy'=16] {'gy'}, dimensions={0} | all-to-all | bytes 655360 | tf_op jit(solution)/shard_map/all_to_all | solution.py:787
  73.0 1.7 %finish.1 = (f32[32,32,128]{2,1,0:T(8,128)}, f32[8,128]{1,0:T(8,128)}) custom-call(f32[16,40,128]{2,1,0:T(8,128)S(1)} %all_to_all.17.got_ref, f32[8,128]{1,0:T(8,128)} %bitcast.4, f32[39,40,128]{2,1,0:T(8,128)S(1)} %get-tuple-element.44.t_ref, f32[39,40,128]{2,1,0:T(8,128)S(1)} %get-tuple-element.45.w0_ref, f32[39,40,128]{2,1,0:T(8,128)S(1)} %get-tuple-element.46.w1_ref, ...), custom_call_target="tpu_custom_call" | custom-call | tf_op jit(solution)/shard_map/finish/pallas_call | solution.py:788
  (1 shorter events, 0.0 us)
Async XLA Ops:
  0.6 28.0 %copy-start.1 = (f32[4]{0:T(128)S(1)}, f32[4]{0:T(128)}, u32[]{:S(2)}) copy-start(f32[4]{0:T(128)} %ref_ref.3) | copy-start | bytes 52
  2.2 17.9 %collective-permute-start = (f32[11,32,128]{2,1,0:T(8,128)S(1)}, f32[11,32,128]{2,1,0:T(8,128)S(1)}, u32[]{:S(2)}, u32[]{:S(2)}) collective-permute-start(f32[11,32,128]{2,1,0:T(8,128)S(1)} %get-tuple-element.26), channel_id=1, source_target_pairs={{16,32},{48,64},{80,96},{112,128},{144,160},{176,192},{208,224},{3... | collective-permute-start | bytes 540680 | tf_op jit(solution)/shard_map/ppermute | solution.py:721
  2.9 17.3 %collective-permute-start.1 = (f32[11,32,128]{2,1,0:T(8,128)S(1)}, f32[11,32,128]{2,1,0:T(8,128)S(1)}, u32[]{:S(2)}, u32[]{:S(2)}) collective-permute-start(f32[11,32,128]{2,1,0:T(8,128)S(1)} %get-tuple-element.27), channel_id=1, source_target_pairs={{0,16},{32,48},{64,80},{96,112},{128,144},{160,176},{192,208},{224... | collective-permute-start | bytes 540680 | tf_op jit(solution)/shard_map/ppermute | solution.py:722
  20.2 8.5 %collective-permute-start.2 = (f32[59,8,128]{2,1,0:T(8,128)S(1)}, f32[59,8,128]{2,1,0:T(8,128)S(1)}, u32[]{:S(2)}, u32[]{:S(2)}) collective-permute-start(f32[59,8,128]{2,1,0:T(8,128)S(1)} %get-tuple-element.41), channel_id=1, source_target_pairs={{1,2},{3,4},{5,6},{7,8},{9,10},{11,12},{13,14},{2,1},{4,3},{6,5},{... | collective-permute-start | bytes 725000 | tf_op jit(solution)/shard_map/ppermute | solution.py:736
  22.7 6.0 %collective-permute-start.3 = (f32[59,8,128]{2,1,0:T(8,128)S(1)}, f32[59,8,128]{2,1,0:T(8,128)S(1)}, u32[]{:S(2)}, u32[]{:S(2)}) collective-permute-start(f32[59,8,128]{2,1,0:T(8,128)S(1)} %get-tuple-element.42), channel_id=1, source_target_pairs={{0,1},{2,3},{4,5},{6,7},{8,9},{10,11},{12,13},{14,15},{1,0},{3,2},... | collective-permute-start | bytes 725000 | tf_op jit(solution)/shard_map/ppermute | solution.py:737
  22.8 0.7 copy-start
  23.4 0.7 copy-start.2
  24.1 0.7 copy-start.3

commit v6 on v5

--- a/solution.py
+++ b/solution.py
@@ -176,8 +176,8 @@
 
 
 def pick(ident, table):
-    low = jnp.where(ident == 1, table[1], table[0])
-    high = jnp.where(ident == 3, table[3], table[2])
+    low = jnp.where(ident == 1, table(1), table(0))
+    high = jnp.where(ident == 3, table(3), table(2))
     return jnp.where(ident >= 2, high, low)
 
 
@@ -230,9 +230,9 @@
 
 
 def own_kernel(
-    ref_ref,
-    grad_ref,
-    store_ref,
+    ref_hbm,
+    grad_hbm,
+    store_hbm,
     t_hbm,
     id_hbm,
     chip_hbm,
@@ -248,18 +248,30 @@
     hot_ref,
     row_ref,
     lane_ref,
+    table_ref,
     t_ref,
     id_ref,
     chip_ref,
+    ref_ref,
+    grad_ref,
+    store_ref,
     sems,
 ):
-    tables = (ref_ref, grad_ref, store_ref)
     ix = lax.axis_index("gx")
     iy = lax.axis_index("gy")
 
     copies = [
         pltpu.make_async_copy(src, dst, sems.at[k])
-        for k, (src, dst) in enumerate(((t_hbm, t_ref), (id_hbm, id_ref), (chip_hbm, chip_ref)))
+        for k, (src, dst) in enumerate(
+            (
+                (ref_hbm, ref_ref),
+                (grad_hbm, grad_ref),
+                (store_hbm, store_ref),
+                (t_hbm, t_ref),
+                (id_hbm, id_ref),
+                (chip_hbm, chip_ref),
+            )
+        )
     ]
     for copy in copies:
         copy.start()
@@ -285,6 +297,11 @@
     for copy in copies:
         copy.wait()
 
+    tables = [lambda k, ref=ref: ref[k] for ref in (ref_ref, grad_ref, store_ref)]
+    for j, table in enumerate(tables):
+        for k in range(4):
+            table_ref[4 * j + k] = jnp.full((TILE, NZ), table(k), f32)
+
     def put(q, temp, ident, chip, inside=None):
         conduct, diag, resid, e_z = cells(temp, ident, chip, tables, inside)
         tp[q, :NY, :] = temp
@@ -321,9 +338,7 @@
 
 
 def krylov_kernel(
-    ref_ref,
-    grad_ref,
-    store_ref,
+    table_ref,
     tp_in,
     cp_in,
     dp_in,
@@ -346,7 +361,7 @@
     dinv,
 ):
     del tp_in, cp_in, dp_in, rp_in, ez_in
-    tables = (ref_ref, grad_ref, store_ref)
+    tables = [lambda k, j=j: table_ref[4 * j + k] for j in range(3)]
     ix = lax.axis_index("gx")
     iy = lax.axis_index("gy")
     last_x = lax.axis_size("gx") - 1
@@ -668,7 +683,6 @@
     size_y = lax.axis_size("gy")
     temp, ident, chip = prior_kelvin_state, substance_identifier, chip_touch_indicator
     vmem = pl.BlockSpec(memory_space=pltpu.VMEM)
-    smem = pl.BlockSpec(memory_space=pltpu.SMEM)
 
     def params(mib):
         return pltpu.CompilerParams(vmem_limit_bytes=mib * MIB)
@@ -742,38 +756,42 @@
         substance_storage_coefficient,
     )
     padded = arr(PX, PY, NZ)
-    *own, hot, row, place = pl.pallas_call(
+    *own, hot, row, place, table_tiles = pl.pallas_call(
         own_kernel,
         name="own_cells",
-        in_specs=[smem] * 3 + [anywhere] * 3 + [vmem] * 3,
-        out_specs=[vmem] * 9,
+        in_specs=[anywhere] * 6 + [vmem] * 3,
+        out_specs=[vmem] * 10,
         out_shape=[padded] * 5
         + [
             arr(TILE, NZ),
             arr(size_y, NZ, TILE * NZ, dtype=bf16),
             arr(size_y, TILE, NZ, dtype=i32),
             arr(size_y, TILE, NZ, dtype=i32),
+            arr(12, TILE, NZ),
         ],
         scratch_shapes=[
             buf(NX, NY, NZ),
             buf(NX, NY, NZ, dtype=i32),
             buf(NX, NY, NZ, dtype=i32),
-            pltpu.SemaphoreType.DMA((3,)),
+            pltpu.SMEM((4,), f32),
+            pltpu.SMEM((4,), f32),
+            pltpu.SMEM((4,), f32),
+            pltpu.SemaphoreType.DMA((6,)),
         ],
         compiler_params=params(14),
-    )(*tables, *in_hbm(temp, ident, chip), xa, xb, sites)
+    )(*in_hbm(*tables, temp, ident, chip), xa, xb, sites)
 
     payload = TILE * (FIELDS + 1)
     start, _, _, _, _, w0, w1, w2, send = pl.pallas_call(
         krylov_kernel,
         name="krylov",
-        in_specs=[smem] * 3 + [vmem] * 8,
+        in_specs=[vmem] * 9,
         out_specs=[vmem] * 9,
         out_shape=[padded] * 8 + [arr(size_x, payload, NZ)],
-        input_output_aliases={3: 0, 4: 1, 5: 2, 6: 3, 7: 4},
+        input_output_aliases={1: 0, 2: 1, 3: 2, 4: 3, 5: 4},
         scratch_shapes=[buf(PX, PY, NZ)] * 3,
         compiler_params=params(24),
-    )(*tables, *own, ya, yb)
+    )(table_tiles, *own, ya, yb)
     table = lax.all_to_all(send, "gx", 0, 0)
     found = pl.pallas_call(
         lookup_kernel,

time: 75 us -> 72.5 us (0.967)
  local copies, waits for them, and re-layouts: 1.97 us -> 0 us
  waiting for transfers between devices: 0.01 us -> 1.49 us
  Pallas kernels: 15.8 us -> 14.8 us
  blocking collectives: 48.1 us -> 47.2 us
    all_to_all x1, blocking collectives: 14.6 us -> 12.2 us  [local(): got = lax.all_to_all(found, 'gy', 0, 0)]
    unnamed x8 -> x0, local copies, waits for them, and re-layouts: 1.97 us -> none
    all_to_all x1, blocking collectives: 21 us -> 22.5 us  [local(): table = lax.all_to_all(send, 'gx', 0, 0)]
    ppermute x1, waiting for transfers between devices: 0.01 us -> 1.48 us  [local(): ya = lax.ppermute(ya, 'gy', swaps(size_y, 1))]
    pallas_call x2, Pallas kernels: 7.38 us -> 6.41 us  [the longest x1 3.4 us: local(): pl.pallas_call(own_kernel, name='own_cells', in_specs=[anywhere] * 6 + [v...]
  transfers between devices with their start and end apart: 4 -> 4, of which waited for: 0 -> 1; matrix products, arithmetic and copies ran while one was open for 0% -> 0% of each run, Pallas kernels for 5% -> 5%
where the time goes in v6:
time: 72.5 us; the launch traced here: 72.1 us
  blocking collectives  47.2 us (65%)
  Pallas kernels  14.8 us (20%)
  starting transfers between devices  7.98 us (11%)
  waiting for transfers between devices  1.49 us (2%)
    all_to_all x1, blocking collectives, local(): table = lax.all_to_all(send, 'gx', 0, 0)  22.5 us
    all_to_all x1, blocking collectives, local(): sites = lax.all_to_all(sites, 'gy', 0, 0)  12.5 us
    all_to_all x1, blocking collectives, local(): got = lax.all_to_all(found, 'gy', 0, 0)  12.2 us
    pallas_call x1, Pallas kernels, local(): pl.pallas_call(lookup_kernel, name='lookup', in_specs=[vmem] * 4, out_spe...  5.12 us
    ppermute x1, starting transfers between devices, local(): xb = lax.ppermute(xb, 'gx', swaps(size_x, 0))  4.75 us
    pallas_call x1, Pallas kernels, local(): pl.pallas_call(own_kernel, name='own_cells', in_specs=[anywhere] * 6 + [v...  3.4 us
    pallas_call x1, Pallas kernels, local(): pl.pallas_call(krylov_kernel, name='krylov', in_specs=[vmem] * 9, out_spe...  3.01 us
    ppermute x1, starting transfers between devices, local(): ya = lax.ppermute(ya, 'gy', swaps(size_y, 1))  2.47 us
  transfers between devices with their start and end apart: 4, of which 1 were waited for; matrix products, arithmetic and copies ran while one was open for 0% of the time, Pallas kernels for 5%

profile of v6, /device:TPU:1, one launch (start us, length us, event | category | flops | bytes accessed | tf_op | source)
XLA Modules:
  0.0 72.1 jit_solution(9671675002887239718)
XLA Ops:
  0.6 1.6 %pack.1 = (f32[11,32,128]{2,1,0:T(8,128)S(1)}, f32[11,32,128]{2,1,0:T(8,128)S(1)}, f32[59,8,128]{2,1,0:T(8,128)S(1)}, f32[59,8,128]{2,1,0:T(8,128)S(1)}, s32[16,8,128]{2,1,0:T(8,128)S(1)}) custom-call(f32[32,32,128]{2,1,0:T(8,128)} %t_hbm.3, s32[32,32,128]{2,1,0:T(8,128)} %id_hbm.3, s32[32,32,128]{2,1,0:T(8,128)} %chip_hbm.3, s32[8,128]{1,0:T(8,128)} %bitcast.3), custom_call_target="tpu_custom_call" | custom-call | tf_op jit(solution)/shard_map/pack/pallas_call | solution.py:703
  2.2 0.7 collective-permute-start
  2.9 4.7 %collective-permute-start.1 = (f32[11,32,128]{2,1,0:T(8,128)S(1)}, f32[11,32,128]{2,1,0:T(8,128)S(1)}, u32[]{:S(2)}, u32[]{:S(2)}) collective-permute-start(f32[11,32,128]{2,1,0:T(8,128)S(1)} %get-tuple-element.28), channel_id=1, source_target_pairs={{0,16},{32,48},{64,80},{96,112},{128,144},{160,176},{192,208},{224... | collective-permute-start | bytes 540680 | tf_op jit(solution)/shard_map/ppermute | solution.py:736
  7.6 12.5 %all_to_all.15.sites_in = s32[16,8,128]{2,1,0:T(8,128)S(1)} all-to-all(s32[16,8,128]{2,1,0:T(8,128)S(1)} %get-tuple-element.31), channel_id=1, replica_groups=mesh['gx'=16,'gy'=16] {'gy'}, dimensions={0} | all-to-all | bytes 131072 | tf_op jit(solution)/shard_map/all_to_all | solution.py:733
  20.1 0.0 collective-permute-done.xa_ref
  20.1 0.0 collective-permute-done.1.xb_ref
  20.2 2.5 %collective-permute-start.2 = (f32[59,8,128]{2,1,0:T(8,128)S(1)}, f32[59,8,128]{2,1,0:T(8,128)S(1)}, u32[]{:S(2)}, u32[]{:S(2)}) collective-permute-start(f32[59,8,128]{2,1,0:T(8,128)S(1)} %get-tuple-element.43), channel_id=1, source_target_pairs={{1,2},{3,4},{5,6},{7,8},{9,10},{11,12},{13,14},{2,1},{4,3},{6,5},{... | collective-permute-start | bytes 725000 | tf_op jit(solution)/shard_map/ppermute | solution.py:750
  22.7 0.1 collective-permute-start.3
  22.8 3.4 %own_cells.1 = (f32[39,40,128]{2,1,0:T(8,128)S(1)}, f32[39,40,128]{2,1,0:T(8,128)S(1)}, f32[39,40,128]{2,1,0:T(8,128)S(1)}, f32[39,40,128]{2,1,0:T(8,128)S(1)}, ...) custom-call(f32[4]{0:T(128)} %ref_hbm.1, ...), custom_call_target="tpu_custom_call" | custom-call | tf_op jit(solution)/shard_map/own_cells/pallas_call | solution.py:759
  26.2 1.5 %collective-permute-done.2.ya_ref = f32[59,8,128]{2,1,0:T(8,128)S(1)} collective-permute-done((f32[59,8,128]{2,1,0:T(8,128)S(1)}, f32[59,8,128]{2,1,0:T(8,128)S(1)}, u32[]{:S(2)}, u32[]{:S(2)}) %collective-permute-start.2) | collective-permute-done | bytes 241696 | tf_op jit(solution)/shard_map/ppermute | solution.py:750
  27.6 0.0 collective-permute-done.3.yb_ref
  27.6 3.0 %krylov.1 = (f32[39,40,128]{2,1,0:T(8,128)S(1)}, f32[39,40,128]{2,1,0:T(8,128)S(1)}, f32[39,40,128]{2,1,0:T(8,128)S(1)}, f32[39,40,128]{2,1,0:T(8,128)S(1)}, f32...) custom-call(f32[12,8,128]{2,1,0:T(8,128)S(1)} %get-tuple-element.36., ...), custom_call_target="tpu_custom_call", output_to_operand_aliasing={{0}: (1, {}), {1}: (2, {}), {2}: (3, {}), {3}: (4, {}), {4}... | custom-call | tf_op jit(solution)/shard_map/krylov/pallas_call | solution.py:785
  30.7 22.5 %all_to_all.16.table_ref = f32[16,40,128]{2,1,0:T(8,128)S(1)} all-to-all(f32[16,40,128]{2,1,0:T(8,128)S(1)} %get-tuple-element.45), channel_id=1, replica_groups=mesh['gx'=16,'gy'=16] {'gx'}, dimensions={0} | all-to-all | bytes 655360 | tf_op jit(solution)/shard_map/all_to_all | solution.py:795
  53.2 5.1 %lookup.1 = f32[16,40,128]{2,1,0:T(8,128)S(1)} custom-call(bf16[16,128,1024]{2,1,0:T(8,128)(2,1)S(1)} %get-tuple-element.33.hot_ref, s32[16,8,128]{2,1,0:T(8,128)S(1)} %get-tuple-element.34.row_ref, s32[16,8,128]{2,1,0:T(8,128)S(1)} %get-tuple-element.35.lane_ref, f32[16,40,128]{2,1,0:T(8,128)S(1)} %all_to_all.16.table_ref), custom_call_target="tpu_custom_call" | custom-call | tf_op jit(solution)/shard_map/lookup/pallas_call | solution.py:796
  58.3 12.2 %all_to_all.17.got_ref = f32[16,40,128]{2,1,0:T(8,128)S(1)} all-to-all(f32[16,40,128]{2,1,0:T(8,128)S(1)} %lookup.1), channel_id=1, replica_groups=mesh['gx'=16,'gy'=16] {'gy'}, dimensions={0} | all-to-all | bytes 655360 | tf_op jit(solution)/shard_map/all_to_all | solution.py:805
  70.5 1.7 %finish.1 = (f32[32,32,128]{2,1,0:T(8,128)}, f32[8,128]{1,0:T(8,128)}) custom-call(f32[16,40,128]{2,1,0:T(8,128)S(1)} %all_to_all.17.got_ref, f32[8,128]{1,0:T(8,128)} %bitcast.4, f32[39,40,128]{2,1,0:T(8,128)S(1)} %get-tuple-element.46.t_ref, f32[39,40,128]{2,1,0:T(8,128)S(1)} %get-tuple-element.47.w0_ref, f32[39,40,128]{2,1,0:T(8,128)S(1)} %get-tuple-element.48.w1_ref, ...), custom_call_target="tpu_custom_call" | custom-call | tf_op jit(solution)/shard_map/finish/pallas_call | solution.py:806
  (1 shorter events, 0.0 us)
Async XLA Ops:
  2.2 17.9 %collective-permute-start = (f32[11,32,128]{2,1,0:T(8,128)S(1)}, f32[11,32,128]{2,1,0:T(8,128)S(1)}, u32[]{:S(2)}, u32[]{:S(2)}) collective-permute-start(f32[11,32,128]{2,1,0:T(8,128)S(1)} %get-tuple-element.27), channel_id=1, source_target_pairs={{16,32},{48,64},{80,96},{112,128},{144,160},{176,192},{208,224},{3... | collective-permute-start | bytes 540680 | tf_op jit(solution)/shard_map/ppermute | solution.py:735
  2.9 17.3 %collective-permute-start.1 = (f32[11,32,128]{2,1,0:T(8,128)S(1)}, f32[11,32,128]{2,1,0:T(8,128)S(1)}, u32[]{:S(2)}, u32[]{:S(2)}) collective-permute-start(f32[11,32,128]{2,1,0:T(8,128)S(1)} %get-tuple-element.28), channel_id=1, source_target_pairs={{0,16},{32,48},{64,80},{96,112},{128,144},{160,176},{192,208},{224... | collective-permute-start | bytes 540680 | tf_op jit(solution)/shard_map/ppermute | solution.py:736
  20.2 7.5 %collective-permute-start.2 = (f32[59,8,128]{2,1,0:T(8,128)S(1)}, f32[59,8,128]{2,1,0:T(8,128)S(1)}, u32[]{:S(2)}, u32[]{:S(2)}) collective-permute-start(f32[59,8,128]{2,1,0:T(8,128)S(1)} %get-tuple-element.43), channel_id=1, source_target_pairs={{1,2},{3,4},{5,6},{7,8},{9,10},{11,12},{13,14},{2,1},{4,3},{6,5},{... | collective-permute-start | bytes 725000 | tf_op jit(solution)/shard_map/ppermute | solution.py:750
  22.7 5.0 %collective-permute-start.3 = (f32[59,8,128]{2,1,0:T(8,128)S(1)}, f32[59,8,128]{2,1,0:T(8,128)S(1)}, u32[]{:S(2)}, u32[]{:S(2)}) collective-permute-start(f32[59,8,128]{2,1,0:T(8,128)S(1)} %get-tuple-element.44), channel_id=1, source_target_pairs={{0,1},{2,3},{4,5},{6,7},{8,9},{10,11},{12,13},{14,15},{1,0},{3,2},... | collective-permute-start | bytes 725000 | tf_op jit(solution)/shard_map/ppermute | solution.py:751

commit v7 on v6

--- a/solution.py
+++ b/solution.py
@@ -20,6 +20,8 @@
 PY = NY + 8
 FIELDS = 4
 TILE = 8
+HALF = 4
+BLOCK = 2 * FIELDS + 1
 PAIRS = 20
 MIB = 1024 * 1024
 f32 = jnp.float32
@@ -94,7 +96,7 @@
     ):
         copies.append(pltpu.make_async_copy(src, dst, sems.at[k]))
         copies[-1].start()
-    for copy in copies:
+    for copy in copies[:6]:
         copy.wait()
 
     def x_sides(low, high):
@@ -119,6 +121,8 @@
     def _():
         x_sides(xb, xa)
 
+    for copy in copies[6:]:
+        copy.wait()
     sub = sublane((TILE, NZ))
 
     def own(q, _):
@@ -511,33 +515,40 @@
     m5 = m5 + crossing(NX - 1, before, dinv[NX] * total)
     m5 = m5 + m5
 
-    moments = zero_tile
+    lanes = lane((HALF, NZ))
+    moments = jnp.zeros((HALF, NZ), f32)
     for k, m in enumerate((m0, m1, m2, m3, m4, m5)):
-        moments = jnp.where(sub == k, jnp.sum(m, axis=0, keepdims=True), moments)
+        m = jnp.sum(jnp.sum(m, axis=0, keepdims=True), axis=1, keepdims=True)
+        moments = jnp.where(lanes == k, jnp.broadcast_to(m, (HALF, NZ)), moments)
     fields = [surf_ref[...]] + [surface(own_rows(w), 2) for w in (w0_ref, w1_ref, w2_ref)]
+    halves = [tile[i : i + HALF] for tile in fields for i in (0, HALF)] + [moments]
     for k in range(send_ref.shape[0]):
-        for j, tile in enumerate((*fields, moments)):
-            send_ref[k, TILE * j : TILE * (j + 1), :] = tile
-
-
-def lookup_kernel(hot_ref, row_ref, lane_ref, table_ref, out_ref, parts):
+        for j, half in enumerate(halves):
+            send_ref[k, j] = half
+
+
+def lookup_kernel(hot_ref, row_ref, lane_ref, table_ref, out_ref, parts, start):
     blocks = table_ref.shape[0]
     targets = hot_ref.shape[0]
     sub = sublane((TILE, NZ))
     zero = jnp.zeros((TILE, NZ), f32)
     fields = FIELDS - 1
+
+    def tile(a, f):
+        return jnp.concatenate([table_ref[a, 2 * f], table_ref[a, 2 * f + 1]], axis=0)
+
+    for a in range(blocks):
+        start[a] = tile(a, 0)
     for f in range(fields):
-        rest = jnp.concatenate(
-            [table_ref[a, TILE * (f + 1) : TILE * (f + 2), :] for a in range(blocks)], axis=0
-        ).T
+        rest = jnp.concatenate([tile(a, f + 1) for a in range(blocks)], axis=0).T
         for k in range(2):
             part = rest.astype(bf16)
             parts[NZ * f : NZ * (f + 1), NZ * k : NZ * (k + 1)] = part
             rest = rest - part.astype(f32)
 
-    total = table_ref[0, TILE * FIELDS :, :]
+    total = table_ref[0, 2 * FIELDS]
     for a in range(1, blocks):
-        total = total + table_ref[a, TILE * FIELDS :, :]
+        total = total + table_ref[a, 2 * FIELDS]
 
     def one(b, _):
         row_of = row_ref[b]
@@ -552,7 +563,7 @@
                 rows = jnp.broadcast_to(row_of[pair + i : pair + i + 1], (TILE, NZ)) - sub
                 acc = zero
                 for a in range(blocks):
-                    got = jnp.take_along_axis(table_ref[a, 0:TILE, :], lanes[i], axis=1)
+                    got = jnp.take_along_axis(start[a], lanes[i], axis=1)
                     acc = jnp.where(rows == a * TILE, got, acc)
                 found[0] = jnp.where(
                     sub == pair + i, jnp.sum(acc, axis=0, keepdims=True), found[0]
@@ -571,11 +582,12 @@
                         sub == pair + i, jnp.sum(acc, axis=0, keepdims=True), found[f + 1]
                     )
         for f in range(FIELDS):
-            out_ref[b, TILE * f : TILE * (f + 1), :] = found[f]
-        out_ref[b, TILE * FIELDS :, :] = total
+            out_ref[b, 2 * f] = found[f][:HALF]
+            out_ref[b, 2 * f + 1] = found[f][HALF:]
+        out_ref[b, 2 * FIELDS] = total
         return 0
 
-    lax.fori_loop(0, targets, one, 0, unroll=2)
+    lax.fori_loop(0, targets, one, 0, unroll=4)
 
 
 def cg_coefficients(m):
@@ -636,8 +648,8 @@
     total = got_ref[0]
     for b in range(1, got_ref.shape[0]):
         total = total + got_ref[b]
-    sums = jnp.sum(total[TILE * FIELDS :], axis=1, keepdims=True)
-    m = [sums[k : k + 1] for k in range(6)]
+    m = [total[2 * FIELDS, 0:1, k : k + 1] for k in range(6)]
+    fields = [jnp.concatenate([total[2 * f], total[2 * f + 1]], axis=0) for f in range(FIELDS)]
     c = cg_coefficients(m)
     c_tile = [jnp.broadcast_to(e, (TILE, NZ)) for e in c]
     c_plane = [jnp.broadcast_to(e, (NY, NZ)) for e in c]
@@ -659,9 +671,9 @@
         outs.append(pltpu.make_async_copy(temp_ref.at[part], temp_hbm.at[part], out_sems.at[k]))
         outs[-1].start()
 
-    flank = total[0:TILE]
+    flank = fields[0]
     for k in range(3):
-        flank = flank + c_tile[k] * total[TILE * (k + 1) : TILE * (k + 2)]
+        flank = flank + c_tile[k] * fields[k + 1]
     soft = jnp.maximum(flank, 0.0) + jnp.log1p(jnp.exp(-jnp.abs(flank)))
     copy.wait()
     growth_ref[...] = usui_rate * pressure_ref[...] * jnp.exp(-usui_energy / (1.0 + soft))
@@ -781,13 +793,12 @@
         compiler_params=params(14),
     )(*in_hbm(*tables, temp, ident, chip), xa, xb, sites)
 
-    payload = TILE * (FIELDS + 1)
     start, _, _, _, _, w0, w1, w2, send = pl.pallas_call(
         krylov_kernel,
         name="krylov",
         in_specs=[vmem] * 9,
         out_specs=[vmem] * 9,
-        out_shape=[padded] * 8 + [arr(size_x, payload, NZ)],
+        out_shape=[padded] * 8 + [arr(size_x, BLOCK, HALF, NZ)],
         input_output_aliases={1: 0, 2: 1, 3: 2, 4: 3, 5: 4},
         scratch_shapes=[buf(PX, PY, NZ)] * 3,
         compiler_params=params(24),
@@ -798,8 +809,11 @@
         name="lookup",
         in_specs=[vmem] * 4,
         out_specs=vmem,
-        out_shape=arr(size_y, payload, NZ),
-        scratch_shapes=[buf(NZ * (FIELDS - 1), 2 * NZ, dtype=bf16)],
+        out_shape=arr(size_y, BLOCK, HALF, NZ),
+        scratch_shapes=[
+            buf(NZ * (FIELDS - 1), 2 * NZ, dtype=bf16),
+            buf(size_x, TILE, NZ),
+        ],
         compiler_params=params(20),
     )(hot, row, place, table)
     got = lax.all_to_all(found, "gy", 0, 0)

time: 72.5 us -> 70.7 us (0.975)
  blocking collectives: 47.2 us -> 46.2 us
  Pallas kernels: 14.8 us -> 14 us
    pallas_call x1, Pallas kernels: 5.12 us -> 4.28 us  [local(): pl.pallas_call(lookup_kernel, name='lookup', in_specs=[vmem] * 4, out_spe...]
where the time goes in v7:
time: 70.7 us; the launch traced here: 70.4 us
  blocking collectives  46.2 us (65%)
  Pallas kernels  14 us (20%)
  starting transfers between devices  7.98 us (11%)
  waiting for transfers between devices  1.49 us (2%)
    all_to_all x1, blocking collectives, local(): table = lax.all_to_all(send, 'gx', 0, 0)  22.1 us
    all_to_all x1, blocking collectives, local(): sites = lax.all_to_all(sites, 'gy', 0, 0)  12.5 us
    all_to_all x1, blocking collectives, local(): got = lax.all_to_all(found, 'gy', 0, 0)  11.6 us
    ppermute x1, starting transfers between devices, local(): xb = lax.ppermute(xb, 'gx', swaps(size_x, 0))  4.75 us
    pallas_call x1, Pallas kernels, local(): pl.pallas_call(lookup_kernel, name='lookup', in_specs=[vmem] * 4, out_spe...  4.28 us
    pallas_call x1, Pallas kernels, local(): pl.pallas_call(own_kernel, name='own_cells', in_specs=[anywhere] * 6 + [v...  3.4 us
    pallas_call x1, Pallas kernels, local(): pl.pallas_call(krylov_kernel, name='krylov', in_specs=[vmem] * 9, out_spe...  3.1 us
    ppermute x1, starting transfers between devices, local(): ya = lax.ppermute(ya, 'gy', swaps(size_y, 1))  2.47 us
  transfers between devices with their start and end apart: 4, of which 1 were waited for; matrix products, arithmetic and copies ran while one was open for 0% of the time, Pallas kernels for 5%

profile of v7, /device:TPU:1, one launch (start us, length us, event | category | flops | bytes accessed | tf_op | source)
XLA Modules:
  0.0 70.4 jit_solution(4567788456500620868)
XLA Ops:
  0.6 1.5 %pack.1 = (f32[11,32,128]{2,1,0:T(8,128)S(1)}, f32[11,32,128]{2,1,0:T(8,128)S(1)}, f32[59,8,128]{2,1,0:T(8,128)S(1)}, f32[59,8,128]{2,1,0:T(8,128)S(1)}, s32[16,8,128]{2,1,0:T(8,128)S(1)}) custom-call(f32[32,32,128]{2,1,0:T(8,128)} %t_hbm.3, s32[32,32,128]{2,1,0:T(8,128)} %id_hbm.3, s32[32,32,128]{2,1,0:T(8,128)} %chip_hbm.3, s32[8,128]{1,0:T(8,128)} %bitcast.3), custom_call_target="tpu_custom_call" | custom-call | tf_op jit(solution)/shard_map/pack/pallas_call | solution.py:715
  2.2 0.7 collective-permute-start
  2.9 4.7 %collective-permute-start.1 = (f32[11,32,128]{2,1,0:T(8,128)S(1)}, f32[11,32,128]{2,1,0:T(8,128)S(1)}, u32[]{:S(2)}, u32[]{:S(2)}) collective-permute-start(f32[11,32,128]{2,1,0:T(8,128)S(1)} %get-tuple-element.28), channel_id=1, source_target_pairs={{0,16},{32,48},{64,80},{96,112},{128,144},{160,176},{192,208},{224... | collective-permute-start | bytes 540680 | tf_op jit(solution)/shard_map/ppermute | solution.py:748
  7.6 12.5 %all_to_all.15.sites_in = s32[16,8,128]{2,1,0:T(8,128)S(1)} all-to-all(s32[16,8,128]{2,1,0:T(8,128)S(1)} %get-tuple-element.31), channel_id=1, replica_groups=mesh['gx'=16,'gy'=16] {'gy'}, dimensions={0} | all-to-all | bytes 131072 | tf_op jit(solution)/shard_map/all_to_all | solution.py:745
  20.1 0.0 collective-permute-done.xa_ref
  20.1 0.0 collective-permute-done.1.xb_ref
  20.1 2.5 %collective-permute-start.2 = (f32[59,8,128]{2,1,0:T(8,128)S(1)}, f32[59,8,128]{2,1,0:T(8,128)S(1)}, u32[]{:S(2)}, u32[]{:S(2)}) collective-permute-start(f32[59,8,128]{2,1,0:T(8,128)S(1)} %get-tuple-element.43), channel_id=1, source_target_pairs={{1,2},{3,4},{5,6},{7,8},{9,10},{11,12},{13,14},{2,1},{4,3},{6,5},{... | collective-permute-start | bytes 725000 | tf_op jit(solution)/shard_map/ppermute | solution.py:762
  22.6 0.1 collective-permute-start.3
  22.7 3.4 %own_cells.1 = (f32[39,40,128]{2,1,0:T(8,128)S(1)}, f32[39,40,128]{2,1,0:T(8,128)S(1)}, f32[39,40,128]{2,1,0:T(8,128)S(1)}, f32[39,40,128]{2,1,0:T(8,128)S(1)}, ...) custom-call(f32[4]{0:T(128)} %ref_hbm.1, ...), custom_call_target="tpu_custom_call" | custom-call | tf_op jit(solution)/shard_map/own_cells/pallas_call | solution.py:771
  26.1 1.5 %collective-permute-done.2.ya_ref = f32[59,8,128]{2,1,0:T(8,128)S(1)} collective-permute-done((f32[59,8,128]{2,1,0:T(8,128)S(1)}, f32[59,8,128]{2,1,0:T(8,128)S(1)}, u32[]{:S(2)}, u32[]{:S(2)}) %collective-permute-start.2) | collective-permute-done | bytes 241696 | tf_op jit(solution)/shard_map/ppermute | solution.py:762
  27.6 0.0 collective-permute-done.3.yb_ref
  27.6 3.1 %krylov.1 = (f32[39,40,128]{2,1,0:T(8,128)S(1)}, f32[39,40,128]{2,1,0:T(8,128)S(1)}, f32[39,40,128]{2,1,0:T(8,128)S(1)}, f32[39,40,128]{2,1,0:T(8,128)S(1)}, f32...) custom-call(f32[12,8,128]{2,1,0:T(8,128)S(1)} %get-tuple-element.36., ...), custom_call_target="tpu_custom_call", output_to_operand_aliasing={{0}: (1, {}), {1}: (2, {}), {2}: (3, {}), {3}: (4, {}), {4}... | custom-call | tf_op jit(solution)/shard_map/krylov/pallas_call | solution.py:796
  30.7 22.1 %all_to_all.16.table_ref = f32[16,9,4,128]{3,2,1,0:T(4,128)S(1)} all-to-all(f32[16,9,4,128]{3,2,1,0:T(4,128)S(1)} %get-tuple-element.45), channel_id=1, replica_groups=mesh['gx'=16,'gy'=16] {'gx'}, dimensions={0} | all-to-all | bytes 589824 | tf_op jit(solution)/shard_map/all_to_all | solution.py:806
  52.8 4.3 %lookup.1 = f32[16,9,4,128]{3,2,1,0:T(4,128)S(1)} custom-call(bf16[16,128,1024]{2,1,0:T(8,128)(2,1)S(1)} %get-tuple-element.33.hot_ref, s32[16,8,128]{2,1,0:T(8,128)S(1)} %get-tuple-element.34.row_ref, s32[16,8,128]{2,1,0:T(8,128)S(1)} %get-tuple-element.35.lane_ref, f32[16,9,4,128]{3,2,1,0:T(4,128)S(1)} %all_to_all.16.table_ref), custom_call_target="tpu_custom_call" | custom-call | tf_op jit(solution)/shard_map/lookup/pallas_call | solution.py:807
  57.1 11.6 %all_to_all.17.got_ref = f32[16,9,4,128]{3,2,1,0:T(4,128)S(1)} all-to-all(f32[16,9,4,128]{3,2,1,0:T(4,128)S(1)} %lookup.1), channel_id=1, replica_groups=mesh['gx'=16,'gy'=16] {'gy'}, dimensions={0} | all-to-all | bytes 589824 | tf_op jit(solution)/shard_map/all_to_all | solution.py:819
  68.7 1.7 %finish.1 = (f32[32,32,128]{2,1,0:T(8,128)}, f32[8,128]{1,0:T(8,128)}) custom-call(f32[16,9,4,128]{3,2,1,0:T(4,128)S(1)} %all_to_all.17.got_ref, f32[8,128]{1,0:T(8,128)} %bitcast.4, f32[39,40,128]{2,1,0:T(8,128)S(1)} %get-tuple-element.46.t_ref, f32[39,40,128]{2,1,0:T(8,128)S(1)} %get-tuple-element.47.w0_ref, f32[39,40,128]{2,1,0:T(8,128)S(1)} %get-tuple-element.48.w1_ref, ...), custom_call_target="tpu_custom_call" | custom-call | tf_op jit(solution)/shard_map/finish/pallas_call | solution.py:820
  (1 shorter events, 0.0 us)
Async XLA Ops:
  2.2 17.9 %collective-permute-start = (f32[11,32,128]{2,1,0:T(8,128)S(1)}, f32[11,32,128]{2,1,0:T(8,128)S(1)}, u32[]{:S(2)}, u32[]{:S(2)}) collective-permute-start(f32[11,32,128]{2,1,0:T(8,128)S(1)} %get-tuple-element.27), channel_id=1, source_target_pairs={{16,32},{48,64},{80,96},{112,128},{144,160},{176,192},{208,224},{3... | collective-permute-start | bytes 540680 | tf_op jit(solution)/shard_map/ppermute | solution.py:747
  2.9 17.3 %collective-permute-start.1 = (f32[11,32,128]{2,1,0:T(8,128)S(1)}, f32[11,32,128]{2,1,0:T(8,128)S(1)}, u32[]{:S(2)}, u32[]{:S(2)}) collective-permute-start(f32[11,32,128]{2,1,0:T(8,128)S(1)} %get-tuple-element.28), channel_id=1, source_target_pairs={{0,16},{32,48},{64,80},{96,112},{128,144},{160,176},{192,208},{224... | collective-permute-start | bytes 540680 | tf_op jit(solution)/shard_map/ppermute | solution.py:748
  20.1 7.5 %collective-permute-start.2 = (f32[59,8,128]{2,1,0:T(8,128)S(1)}, f32[59,8,128]{2,1,0:T(8,128)S(1)}, u32[]{:S(2)}, u32[]{:S(2)}) collective-permute-start(f32[59,8,128]{2,1,0:T(8,128)S(1)} %get-tuple-element.43), channel_id=1, source_target_pairs={{1,2},{3,4},{5,6},{7,8},{9,10},{11,12},{13,14},{2,1},{4,3},{6,5},{... | collective-permute-start | bytes 725000 | tf_op jit(solution)/shard_map/ppermute | solution.py:762
  22.6 5.0 %collective-permute-start.3 = (f32[59,8,128]{2,1,0:T(8,128)S(1)}, f32[59,8,128]{2,1,0:T(8,128)S(1)}, u32[]{:S(2)}, u32[]{:S(2)}) collective-permute-start(f32[59,8,128]{2,1,0:T(8,128)S(1)} %get-tuple-element.44), channel_id=1, source_target_pairs={{0,1},{2,3},{4,5},{6,7},{8,9},{10,11},{12,13},{14,15},{1,0},{3,2},... | collective-permute-start | bytes 725000 | tf_op jit(solution)/shard_map/ppermute | solution.py:763

commit v8 on v7

--- a/solution.py
+++ b/solution.py
@@ -60,6 +60,7 @@
     xb,
     ya,
     yb,
+    yc,
     sites,
     t_a,
     t_b,
@@ -137,14 +138,13 @@
         tile = c_a[j].astype(f32)
         if j + PAIRS < NX:
             tile = jnp.where(sub < 4, tile, pltpu.roll(c_a[j + PAIRS].astype(f32), 4, 0))
-        ya[PX + j] = tile
-        yb[PX + j] = tile
+        yc[j] = tile
     for k in range(sites.shape[0]):
         sites[k] = site_ref[...]
 
 
-def corner_kernel(ya_in, yb_in, xa_ref, xb_ref, sites_in, ya, yb, sites_out):
-    del ya_in, yb_in, sites_in, sites_out
+def corner_kernel(ya_in, yb_in, yc_in, xa_ref, xb_ref, sites_in, ya, yb, yc, sites_out):
+    del ya_in, yb_in, yc_in, sites_in, sites_out
     even_x = lax.rem(lax.axis_index("gx"), 2) == 0
     even_y = lax.rem(lax.axis_index("gy"), 2) == 0
     sub = sublane((TILE, NZ))
@@ -173,10 +173,8 @@
         ya[q] = jnp.where(even_y, low, high)
         yb[q] = jnp.where(even_y, high, low)
         if chip is not None:
-            place = PX + q - PAIRS
-            tile = jnp.where(sub < 4, ya[place], pltpu.roll(side(chip, first), 4, 0))
-            ya[place] = tile
-            yb[place] = tile
+            place = q - PAIRS
+            yc[place] = jnp.where(sub < 4, yc[place], pltpu.roll(side(chip, first), 4, 0))
 
 
 def pick(ident, table):
@@ -351,6 +349,8 @@
     surf_ref,
     ya_ref,
     yb_ref,
+    yca_ref,
+    ycb_ref,
     tp,
     cp,
     dp,
@@ -386,6 +386,9 @@
     def low_row(q):
         return jnp.where(even_y, ya_ref[q], yb_ref[q])
 
+    def chip_row(j):
+        return jnp.where(even_y, ycb_ref[j], yca_ref[j])
+
     def put_halo(q, chip_high, plane_in):
         high = high_row(q)
         low = low_row(q)
@@ -400,11 +403,11 @@
         ez[q, NY:, :] = e_z
 
     def own_halo_first(q, _):
-        put_halo(q, high_row(PX + q), one)
+        put_halo(q, chip_row(q), one)
         return 0
 
     def own_halo_second(q, _):
-        put_halo(q, pltpu.roll(high_row(PX + q - PAIRS), 4, 0), one)
+        put_halo(q, pltpu.roll(chip_row(q - PAIRS), 4, 0), one)
         return 0
 
     lax.fori_loop(0, PAIRS, own_halo_first, 0, unroll=20)
@@ -412,7 +415,7 @@
 
     zero_tile = jnp.zeros((TILE, NZ), f32)
     for q in range(NX, PX):
-        put_halo(q, pltpu.roll(high_row(PX + q - PAIRS), 4, 0), high_x if q < NX + HIGH else low_x)
+        put_halo(q, pltpu.roll(chip_row(q - PAIRS), 4, 0), high_x if q < NX + HIGH else low_x)
 
     subs = sublane((PY, NZ))
     rows_in = jnp.where(subs < NY, 1.0, jnp.where(subs < NY + 4, high_y, low_y)).astype(f32)
@@ -712,16 +715,17 @@
         return [pltpu.with_memory_space_constraint(a, pltpu.HBM) for a in arrays]
 
     i32 = jnp.int32
-    xa, xb, ya, yb, sites = pl.pallas_call(
+    xa, xb, ya, yb, yc, sites = pl.pallas_call(
         pack_kernel,
         name="pack",
         in_specs=[anywhere] * 4,
-        out_specs=[vmem] * 5,
+        out_specs=[vmem] * 6,
         out_shape=[
             arr(11, NY, NZ),
             arr(11, NY, NZ),
-            arr(PX + PAIRS, TILE, NZ),
-            arr(PX + PAIRS, TILE, NZ),
+            arr(PX, TILE, NZ),
+            arr(PX, TILE, NZ),
+            arr(PAIRS, TILE, NZ),
             arr(size_y, TILE, NZ, dtype=i32),
         ],
         scratch_shapes=[
@@ -746,21 +750,24 @@
 
     xa = lax.ppermute(xa, "gx", swaps(size_x, 1))
     xb = lax.ppermute(xb, "gx", swaps(size_x, 0))
-    ya, yb, sites = pl.pallas_call(
+    ya, yb, yc, sites = pl.pallas_call(
         corner_kernel,
         name="corners",
-        in_specs=[vmem] * 5,
-        out_specs=[vmem] * 3,
+        in_specs=[vmem] * 6,
+        out_specs=[vmem] * 4,
         out_shape=[
-            arr(PX + PAIRS, TILE, NZ),
-            arr(PX + PAIRS, TILE, NZ),
+            arr(PX, TILE, NZ),
+            arr(PX, TILE, NZ),
+            arr(PAIRS, TILE, NZ),
             arr(size_y, TILE, NZ, dtype=i32),
         ],
-        input_output_aliases={0: 0, 1: 1, 4: 2},
+        input_output_aliases={0: 0, 1: 1, 2: 2, 5: 3},
         compiler_params=params(8),
-    )(ya, yb, xa, xb, sites)
+    )(ya, yb, yc, xa, xb, sites)
     ya = lax.ppermute(ya, "gy", swaps(size_y, 1))
+    yca = lax.ppermute(yc, "gy", swaps(size_y, 1))
     yb = lax.ppermute(yb, "gy", swaps(size_y, 0))
+    ycb = lax.ppermute(yc, "gy", swaps(size_y, 0))
 
     tables = (
         substance_reference_diffusivity,
@@ -796,13 +803,13 @@
     start, _, _, _, _, w0, w1, w2, send = pl.pallas_call(
         krylov_kernel,
         name="krylov",
-        in_specs=[vmem] * 9,
+        in_specs=[vmem] * 11,
         out_specs=[vmem] * 9,
         out_shape=[padded] * 8 + [arr(size_x, BLOCK, HALF, NZ)],
         input_output_aliases={1: 0, 2: 1, 3: 2, 4: 3, 5: 4},
         scratch_shapes=[buf(PX, PY, NZ)] * 3,
         compiler_params=params(24),
-    )(table_tiles, *own, ya, yb)
+    )(table_tiles, *own, ya, yb, yca, ycb)
     table = lax.all_to_all(send, "gx", 0, 0)
     found = pl.pallas_call(
         lookup_kernel,

time: 70.7 us -> 73.2 us (1.035)
  starting transfers between devices: 7.98 us -> 11.6 us
  waiting for transfers between devices: 1.49 us -> 0.02 us
    ppermute x0 -> x2, starting transfers between devices: none -> 3.57 us  [the longest x1 3.08 us: local(): yca = lax.ppermute(yc, 'gy', swaps(size_y, 1))]
    ppermute x1, waiting for transfers between devices: 1.48 us -> 0.01 us  [local(): ya = lax.ppermute(ya, 'gy', swaps(size_y, 1))]
    all_to_all x1, blocking collectives: 11.6 us -> 12.9 us  [local(): got = lax.all_to_all(found, 'gy', 0, 0)]
    all_to_all x1, blocking collectives: 22.1 us -> 21.2 us  [local(): table = lax.all_to_all(send, 'gx', 0, 0)]
  transfers between devices with their start and end apart: 4 -> 6, of which waited for: 1 -> 0; matrix products, arithmetic and copies ran while one was open for 0% -> 0% of each run, Pallas kernels for 5% -> 5%
where the time goes in v8:
time: 73.2 us; the launch traced here: 72.9 us
  blocking collectives  46.5 us (64%)
  Pallas kernels  14 us (19%)
  starting transfers between devices  11.6 us (16%)
    all_to_all x1, blocking collectives, local(): table = lax.all_to_all(send, 'gx', 0, 0)  21.2 us
    all_to_all x1, blocking collectives, local(): got = lax.all_to_all(found, 'gy', 0, 0)  12.9 us
    all_to_all x1, blocking collectives, local(): sites = lax.all_to_all(sites, 'gy', 0, 0)  12.5 us
    ppermute x1, starting transfers between devices, local(): xb = lax.ppermute(xb, 'gx', swaps(size_x, 0))  4.75 us
    pallas_call x1, Pallas kernels, local(): pl.pallas_call(lookup_kernel, name='lookup', in_specs=[vmem] * 4, out_spe...  4.28 us
    pallas_call x1, Pallas kernels, local(): pl.pallas_call(own_kernel, name='own_cells', in_specs=[anywhere] * 6 + [v...  3.4 us
    pallas_call x1, Pallas kernels, local(): pl.pallas_call(krylov_kernel, name='krylov', in_specs=[vmem] * 11, out_sp...  3.11 us
    ppermute x1, starting transfers between devices, local(): yca = lax.ppermute(yc, 'gy', swaps(size_y, 1))  3.08 us
  transfers between devices with their start and end apart: 6, of which 0 were waited for; matrix products, arithmetic and copies ran while one was open for 0% of the time, Pallas kernels for 5%

profile of v8, /device:TPU:1, one launch (start us, length us, event | category | flops | bytes accessed | tf_op | source)
XLA Modules:
  0.0 72.9 jit_solution(18069682114768915197)
XLA Ops:
  0.6 1.5 %pack.1 = (f32[11,32,128]{2,1,0:T(8,128)S(1)}, f32[11,32,128]{2,1,0:T(8,128)S(1)}, f32[39,8,128]{2,1,0:T(8,128)S(1)}, f32[39,8,128]{2,1,0:T(8,128)S(1)}, f32[20,...) custom-call(f32[32,32,128]{2,1,0:T(8,128)} %t_hbm.3, s32[32,32,128]{2,1,0:T(8,128)} %id_hbm.3, s32[32,32,128]{2,1,0:T(8,128)} %chip_hbm.3, ...), custom_call_target="tpu_custom_call" | custom-call | tf_op jit(solution)/shard_map/pack/pallas_call | solution.py:718
  2.2 0.7 collective-permute-start
  2.8 4.7 %collective-permute-start.1 = (f32[11,32,128]{2,1,0:T(8,128)S(1)}, f32[11,32,128]{2,1,0:T(8,128)S(1)}, u32[]{:S(2)}, u32[]{:S(2)}) collective-permute-start(f32[11,32,128]{2,1,0:T(8,128)S(1)} %get-tuple-element.30), channel_id=1, source_target_pairs={{0,16},{32,48},{64,80},{96,112},{128,144},{160,176},{192,208},{224... | collective-permute-start | bytes 540680 | tf_op jit(solution)/shard_map/ppermute | solution.py:752
  7.6 12.5 %all_to_all.15.sites_in = s32[16,8,128]{2,1,0:T(8,128)S(1)} all-to-all(s32[16,8,128]{2,1,0:T(8,128)S(1)} %get-tuple-element.34), channel_id=1, replica_groups=mesh['gx'=16,'gy'=16] {'gy'}, dimensions={0} | all-to-all | bytes 131072 | tf_op jit(solution)/shard_map/all_to_all | solution.py:749
  20.1 0.0 collective-permute-done.xa_ref
  20.1 0.0 collective-permute-done.1.xb_ref
  20.1 2.5 %collective-permute-start.2 = (f32[39,8,128]{2,1,0:T(8,128)S(1)}, f32[39,8,128]{2,1,0:T(8,128)S(1)}, u32[]{:S(2)}, u32[]{:S(2)}) collective-permute-start(f32[39,8,128]{2,1,0:T(8,128)S(1)} %get-tuple-element.46), channel_id=1, source_target_pairs={{1,2},{3,4},{5,6},{7,8},{9,10},{11,12},{13,14},{2,1},{4,3},{6,5},{... | collective-permute-start | bytes 479240 | tf_op jit(solution)/shard_map/ppermute | solution.py:767
  22.6 0.1 collective-permute-start.3
  22.7 0.5 collective-permute-start.5
  23.2 3.1 %collective-permute-start.4 = (f32[20,8,128]{2,1,0:T(8,128)S(1)}, f32[20,8,128]{2,1,0:T(8,128)S(1)}, u32[]{:S(2)}, u32[]{:S(2)}) collective-permute-start(f32[20,8,128]{2,1,0:T(8,128)S(1)} %get-tuple-element.48), channel_id=1, source_target_pairs={{1,2},{3,4},{5,6},{7,8},{9,10},{11,12},{13,14},{2,1},{4,3},{6,5},{... | collective-permute-start | bytes 245768 | tf_op jit(solution)/shard_map/ppermute | solution.py:768
  26.3 3.4 %own_cells.1 = (f32[39,40,128]{2,1,0:T(8,128)S(1)}, f32[39,40,128]{2,1,0:T(8,128)S(1)}, f32[39,40,128]{2,1,0:T(8,128)S(1)}, f32[39,40,128]{2,1,0:T(8,128)S(1)}, ...) custom-call(f32[4]{0:T(128)} %ref_hbm.1, ...), custom_call_target="tpu_custom_call" | custom-call | tf_op jit(solution)/shard_map/own_cells/pallas_call | solution.py:778
  29.7 0.0 collective-permute-done.5.ycb_ref
  29.7 0.0 collective-permute-done.4.yca_ref
  29.7 0.0 collective-permute-done.2.ya_ref
  29.7 0.0 collective-permute-done.3.yb_ref
  29.8 3.1 %krylov.1 = (f32[39,40,128]{2,1,0:T(8,128)S(1)}, f32[39,40,128]{2,1,0:T(8,128)S(1)}, f32[39,40,128]{2,1,0:T(8,128)S(1)}, f32[39,40,128]{2,1,0:T(8,128)S(1)}, f32...) custom-call(f32[12,8,128]{2,1,0:T(8,128)S(1)} %get-tuple-element.39., ...), custom_call_target="tpu_custom_call", output_to_operand_aliasing={{0}: (1, {}), {1}: (2, {}), {2}: (3, {}), {3}: (4, {}), {4}... | custom-call | tf_op jit(solution)/shard_map/krylov/pallas_call | solution.py:803
  32.9 21.2 %all_to_all.16.table_ref = f32[16,9,4,128]{3,2,1,0:T(4,128)S(1)} all-to-all(f32[16,9,4,128]{3,2,1,0:T(4,128)S(1)} %get-tuple-element.49), channel_id=1, replica_groups=mesh['gx'=16,'gy'=16] {'gx'}, dimensions={0} | all-to-all | bytes 589824 | tf_op jit(solution)/shard_map/all_to_all | solution.py:813
  54.0 4.3 %lookup.1 = f32[16,9,4,128]{3,2,1,0:T(4,128)S(1)} custom-call(bf16[16,128,1024]{2,1,0:T(8,128)(2,1)S(1)} %get-tuple-element.36.hot_ref, s32[16,8,128]{2,1,0:T(8,128)S(1)} %get-tuple-element.37.row_ref, s32[16,8,128]{2,1,0:T(8,128)S(1)} %get-tuple-element.38.lane_ref, f32[16,9,4,128]{3,2,1,0:T(4,128)S(1)} %all_to_all.16.table_ref), custom_call_target="tpu_custom_call" | custom-call | tf_op jit(solution)/shard_map/lookup/pallas_call | solution.py:814
  58.3 12.9 %all_to_all.17.got_ref = f32[16,9,4,128]{3,2,1,0:T(4,128)S(1)} all-to-all(f32[16,9,4,128]{3,2,1,0:T(4,128)S(1)} %lookup.1), channel_id=1, replica_groups=mesh['gx'=16,'gy'=16] {'gy'}, dimensions={0} | all-to-all | bytes 589824 | tf_op jit(solution)/shard_map/all_to_all | solution.py:826
  71.2 1.7 %finish.1 = (f32[32,32,128]{2,1,0:T(8,128)}, f32[8,128]{1,0:T(8,128)}) custom-call(f32[16,9,4,128]{3,2,1,0:T(4,128)S(1)} %all_to_all.17.got_ref, f32[8,128]{1,0:T(8,128)} %bitcast.4, f32[39,40,128]{2,1,0:T(8,128)S(1)} %get-tuple-element.50.t_ref, f32[39,40,128]{2,1,0:T(8,128)S(1)} %get-tuple-element.51.w0_ref, f32[39,40,128]{2,1,0:T(8,128)S(1)} %get-tuple-element.52.w1_ref, ...), custom_call_target="tpu_custom_call" | custom-call | tf_op jit(solution)/shard_map/finish/pallas_call | solution.py:827
  (1 shorter events, 0.0 us)
Async XLA Ops:
  2.2 17.9 %collective-permute-start = (f32[11,32,128]{2,1,0:T(8,128)S(1)}, f32[11,32,128]{2,1,0:T(8,128)S(1)}, u32[]{:S(2)}, u32[]{:S(2)}) collective-permute-start(f32[11,32,128]{2,1,0:T(8,128)S(1)} %get-tuple-element.29), channel_id=1, source_target_pairs={{16,32},{48,64},{80,96},{112,128},{144,160},{176,192},{208,224},{3... | collective-permute-start | bytes 540680 | tf_op jit(solution)/shard_map/ppermute | solution.py:751
  2.8 17.3 %collective-permute-start.1 = (f32[11,32,128]{2,1,0:T(8,128)S(1)}, f32[11,32,128]{2,1,0:T(8,128)S(1)}, u32[]{:S(2)}, u32[]{:S(2)}) collective-permute-start(f32[11,32,128]{2,1,0:T(8,128)S(1)} %get-tuple-element.30), channel_id=1, source_target_pairs={{0,16},{32,48},{64,80},{96,112},{128,144},{160,176},{192,208},{224... | collective-permute-start | bytes 540680 | tf_op jit(solution)/shard_map/ppermute | solution.py:752
  20.1 9.6 %collective-permute-start.2 = (f32[39,8,128]{2,1,0:T(8,128)S(1)}, f32[39,8,128]{2,1,0:T(8,128)S(1)}, u32[]{:S(2)}, u32[]{:S(2)}) collective-permute-start(f32[39,8,128]{2,1,0:T(8,128)S(1)} %get-tuple-element.46), channel_id=1, source_target_pairs={{1,2},{3,4},{5,6},{7,8},{9,10},{11,12},{13,14},{2,1},{4,3},{6,5},{... | collective-permute-start | bytes 479240 | tf_op jit(solution)/shard_map/ppermute | solution.py:767
  22.6 7.1 %collective-permute-start.3 = (f32[39,8,128]{2,1,0:T(8,128)S(1)}, f32[39,8,128]{2,1,0:T(8,128)S(1)}, u32[]{:S(2)}, u32[]{:S(2)}) collective-permute-start(f32[39,8,128]{2,1,0:T(8,128)S(1)} %get-tuple-element.47), channel_id=1, source_target_pairs={{0,1},{2,3},{4,5},{6,7},{8,9},{10,11},{12,13},{14,15},{1,0},{3,2},... | collective-permute-start | bytes 479240 | tf_op jit(solution)/shard_map/ppermute | solution.py:769
  22.7 7.0 %collective-permute-start.5 = (f32[20,8,128]{2,1,0:T(8,128)S(1)}, f32[20,8,128]{2,1,0:T(8,128)S(1)}, u32[]{:S(2)}, u32[]{:S(2)}) collective-permute-start(f32[20,8,128]{2,1,0:T(8,128)S(1)} %get-tuple-element.48), channel_id=1, source_target_pairs={{0,1},{2,3},{4,5},{6,7},{8,9},{10,11},{12,13},{14,15},{1,0},{3,2},... | collective-permute-start | bytes 245768 | tf_op jit(solution)/shard_map/ppermute | solution.py:770
  23.2 6.5 %collective-permute-start.4 = (f32[20,8,128]{2,1,0:T(8,128)S(1)}, f32[20,8,128]{2,1,0:T(8,128)S(1)}, u32[]{:S(2)}, u32[]{:S(2)}) collective-permute-start(f32[20,8,128]{2,1,0:T(8,128)S(1)} %get-tuple-element.48), channel_id=1, source_target_pairs={{1,2},{3,4},{5,6},{7,8},{9,10},{11,12},{13,14},{2,1},{4,3},{6,5},{... | collective-permute-start | bytes 245768 | tf_op jit(solution)/shard_map/ppermute | solution.py:768

commit v9 on v7

--- a/solution.py
+++ b/solution.py
@@ -20,8 +20,9 @@
 PY = NY + 8
 FIELDS = 4
 TILE = 8
-HALF = 4
-BLOCK = 2 * FIELDS + 1
+PART = 2
+PARTS = TILE // PART
+BLOCK = PARTS * FIELDS + 1
 PAIRS = 20
 MIB = 1024 * 1024
 f32 = jnp.float32
@@ -515,16 +516,16 @@
     m5 = m5 + crossing(NX - 1, before, dinv[NX] * total)
     m5 = m5 + m5
 
-    lanes = lane((HALF, NZ))
-    moments = jnp.zeros((HALF, NZ), f32)
+    lanes = lane((PART, NZ))
+    moments = jnp.zeros((PART, NZ), f32)
     for k, m in enumerate((m0, m1, m2, m3, m4, m5)):
         m = jnp.sum(jnp.sum(m, axis=0, keepdims=True), axis=1, keepdims=True)
-        moments = jnp.where(lanes == k, jnp.broadcast_to(m, (HALF, NZ)), moments)
+        moments = jnp.where(lanes == k, jnp.broadcast_to(m, (PART, NZ)), moments)
     fields = [surf_ref[...]] + [surface(own_rows(w), 2) for w in (w0_ref, w1_ref, w2_ref)]
-    halves = [tile[i : i + HALF] for tile in fields for i in (0, HALF)] + [moments]
+    pieces = [tile[i : i + PART] for tile in fields for i in range(0, TILE, PART)] + [moments]
     for k in range(send_ref.shape[0]):
-        for j, half in enumerate(halves):
-            send_ref[k, j] = half
+        for j, piece in enumerate(pieces):
+            send_ref[k, j] = piece
 
 
 def lookup_kernel(hot_ref, row_ref, lane_ref, table_ref, out_ref, parts, start):
@@ -535,7 +536,7 @@
     fields = FIELDS - 1
 
     def tile(a, f):
-        return jnp.concatenate([table_ref[a, 2 * f], table_ref[a, 2 * f + 1]], axis=0)
+        return jnp.concatenate([table_ref[a, PARTS * f + i] for i in range(PARTS)], axis=0)
 
     for a in range(blocks):
         start[a] = tile(a, 0)
@@ -546,9 +547,9 @@
             parts[NZ * f : NZ * (f + 1), NZ * k : NZ * (k + 1)] = part
             rest = rest - part.astype(f32)
 
-    total = table_ref[0, 2 * FIELDS]
+    total = table_ref[0, PARTS * FIELDS]
     for a in range(1, blocks):
-        total = total + table_ref[a, 2 * FIELDS]
+        total = total + table_ref[a, PARTS * FIELDS]
 
     def one(b, _):
         row_of = row_ref[b]
@@ -582,12 +583,12 @@
                         sub == pair + i, jnp.sum(acc, axis=0, keepdims=True), found[f + 1]
                     )
         for f in range(FIELDS):
-            out_ref[b, 2 * f] = found[f][:HALF]
-            out_ref[b, 2 * f + 1] = found[f][HALF:]
-        out_ref[b, 2 * FIELDS] = total
+            for i in range(PARTS):
+                out_ref[b, PARTS * f + i] = found[f][PART * i : PART * (i + 1)]
+        out_ref[b, PARTS * FIELDS] = total
         return 0
 
-    lax.fori_loop(0, targets, one, 0, unroll=4)
+    lax.fori_loop(0, targets, one, 0, unroll=8)
 
 
 def cg_coefficients(m):
@@ -648,8 +649,11 @@
     total = got_ref[0]
     for b in range(1, got_ref.shape[0]):
         total = total + got_ref[b]
-    m = [total[2 * FIELDS, 0:1, k : k + 1] for k in range(6)]
-    fields = [jnp.concatenate([total[2 * f], total[2 * f + 1]], axis=0) for f in range(FIELDS)]
+    m = [total[PARTS * FIELDS, 0:1, k : k + 1] for k in range(6)]
+    fields = [
+        jnp.concatenate([total[PARTS * f + i] for i in range(PARTS)], axis=0)
+        for f in range(FIELDS)
+    ]
     c = cg_coefficients(m)
     c_tile = [jnp.broadcast_to(e, (TILE, NZ)) for e in c]
     c_plane = [jnp.broadcast_to(e, (NY, NZ)) for e in c]
@@ -798,7 +802,7 @@
         name="krylov",
         in_specs=[vmem] * 9,
         out_specs=[vmem] * 9,
-        out_shape=[padded] * 8 + [arr(size_x, BLOCK, HALF, NZ)],
+        out_shape=[padded] * 8 + [arr(size_x, BLOCK, PART, NZ)],
         input_output_aliases={1: 0, 2: 1, 3: 2, 4: 3, 5: 4},
         scratch_shapes=[buf(PX, PY, NZ)] * 3,
         compiler_params=params(24),
@@ -809,7 +813,7 @@
         name="lookup",
         in_specs=[vmem] * 4,
         out_specs=vmem,
-        out_shape=arr(size_y, BLOCK, HALF, NZ),
+        out_shape=arr(size_y, BLOCK, PART, NZ),
         scratch_shapes=[
             buf(NZ * (FIELDS - 1), 2 * NZ, dtype=bf16),
             buf(size_x, TILE, NZ),

time: 70.7 us -> 70 us (0.990)
  no operation moved by 1% of the time
where the time goes in v9:
time: 70 us; the launch traced here: 69.7 us
  blocking collectives  45.8 us (65%)
  Pallas kernels  13.7 us (20%)
  starting transfers between devices  7.98 us (11%)
  waiting for transfers between devices  1.49 us (2%)
    all_to_all x1, blocking collectives, local(): table = lax.all_to_all(send, 'gx', 0, 0)  22 us
    all_to_all x1, blocking collectives, local(): sites = lax.all_to_all(sites, 'gy', 0, 0)  12.5 us
    all_to_all x1, blocking collectives, local(): got = lax.all_to_all(found, 'gy', 0, 0)  11.4 us
    ppermute x1, starting transfers between devices, local(): xb = lax.ppermute(xb, 'gx', swaps(size_x, 0))  4.75 us
    pallas_call x1, Pallas kernels, local(): pl.pallas_call(lookup_kernel, name='lookup', in_specs=[vmem] * 4, out_spe...  3.88 us
    pallas_call x1, Pallas kernels, local(): pl.pallas_call(own_kernel, name='own_cells', in_specs=[anywhere] * 6 + [v...  3.4 us
    pallas_call x1, Pallas kernels, local(): pl.pallas_call(krylov_kernel, name='krylov', in_specs=[vmem] * 9, out_spe...  3.11 us
    ppermute x1, starting transfers between devices, local(): ya = lax.ppermute(ya, 'gy', swaps(size_y, 1))  2.47 us
  transfers between devices with their start and end apart: 4, of which 1 were waited for; matrix products, arithmetic and copies ran while one was open for 0% of the time, Pallas kernels for 5%

profile of v9, /device:TPU:1, one launch (start us, length us, event | category | flops | bytes accessed | tf_op | source)
XLA Modules:
  0.0 69.7 jit_solution(8074098977820721861)
XLA Ops:
  0.6 1.5 %pack.1 = (f32[11,32,128]{2,1,0:T(8,128)S(1)}, f32[11,32,128]{2,1,0:T(8,128)S(1)}, f32[59,8,128]{2,1,0:T(8,128)S(1)}, f32[59,8,128]{2,1,0:T(8,128)S(1)}, s32[16,8,128]{2,1,0:T(8,128)S(1)}) custom-call(f32[32,32,128]{2,1,0:T(8,128)} %t_hbm.3, s32[32,32,128]{2,1,0:T(8,128)} %id_hbm.3, s32[32,32,128]{2,1,0:T(8,128)} %chip_hbm.3, s32[8,128]{1,0:T(8,128)} %bitcast.3), custom_call_target="tpu_custom_call" | custom-call | tf_op jit(solution)/shard_map/pack/pallas_call | solution.py:719
  2.2 0.7 collective-permute-start
  2.9 4.7 %collective-permute-start.1 = (f32[11,32,128]{2,1,0:T(8,128)S(1)}, f32[11,32,128]{2,1,0:T(8,128)S(1)}, u32[]{:S(2)}, u32[]{:S(2)}) collective-permute-start(f32[11,32,128]{2,1,0:T(8,128)S(1)} %get-tuple-element.28), channel_id=1, source_target_pairs={{0,16},{32,48},{64,80},{96,112},{128,144},{160,176},{192,208},{224... | collective-permute-start | bytes 540680 | tf_op jit(solution)/shard_map/ppermute | solution.py:752
  7.6 12.5 %all_to_all.15.sites_in = s32[16,8,128]{2,1,0:T(8,128)S(1)} all-to-all(s32[16,8,128]{2,1,0:T(8,128)S(1)} %get-tuple-element.31), channel_id=1, replica_groups=mesh['gx'=16,'gy'=16] {'gy'}, dimensions={0} | all-to-all | bytes 131072 | tf_op jit(solution)/shard_map/all_to_all | solution.py:749
  20.1 0.0 collective-permute-done.xa_ref
  20.1 0.0 collective-permute-done.1.xb_ref
  20.1 2.5 %collective-permute-start.2 = (f32[59,8,128]{2,1,0:T(8,128)S(1)}, f32[59,8,128]{2,1,0:T(8,128)S(1)}, u32[]{:S(2)}, u32[]{:S(2)}) collective-permute-start(f32[59,8,128]{2,1,0:T(8,128)S(1)} %get-tuple-element.43), channel_id=1, source_target_pairs={{1,2},{3,4},{5,6},{7,8},{9,10},{11,12},{13,14},{2,1},{4,3},{6,5},{... | collective-permute-start | bytes 725000 | tf_op jit(solution)/shard_map/ppermute | solution.py:766
  22.6 0.1 collective-permute-start.3
  22.7 3.4 %own_cells.1 = (f32[39,40,128]{2,1,0:T(8,128)S(1)}, f32[39,40,128]{2,1,0:T(8,128)S(1)}, f32[39,40,128]{2,1,0:T(8,128)S(1)}, f32[39,40,128]{2,1,0:T(8,128)S(1)}, ...) custom-call(f32[4]{0:T(128)} %ref_hbm.1, ...), custom_call_target="tpu_custom_call" | custom-call | tf_op jit(solution)/shard_map/own_cells/pallas_call | solution.py:775
  26.1 1.5 %collective-permute-done.2.ya_ref = f32[59,8,128]{2,1,0:T(8,128)S(1)} collective-permute-done((f32[59,8,128]{2,1,0:T(8,128)S(1)}, f32[59,8,128]{2,1,0:T(8,128)S(1)}, u32[]{:S(2)}, u32[]{:S(2)}) %collective-permute-start.2) | collective-permute-done | bytes 241696 | tf_op jit(solution)/shard_map/ppermute | solution.py:766
  27.6 0.0 collective-permute-done.3.yb_ref
  27.6 3.1 %krylov.1 = (f32[39,40,128]{2,1,0:T(8,128)S(1)}, f32[39,40,128]{2,1,0:T(8,128)S(1)}, f32[39,40,128]{2,1,0:T(8,128)S(1)}, f32[39,40,128]{2,1,0:T(8,128)S(1)}, f32...) custom-call(f32[12,8,128]{2,1,0:T(8,128)S(1)} %get-tuple-element.36., ...), custom_call_target="tpu_custom_call", output_to_operand_aliasing={{0}: (1, {}), {1}: (2, {}), {2}: (3, {}), {3}: (4, {}), {4}... | custom-call | tf_op jit(solution)/shard_map/krylov/pallas_call | solution.py:800
  30.7 22.0 %all_to_all.16.table_ref = f32[16,17,2,128]{3,2,1,0:T(2,128)S(1)} all-to-all(f32[16,17,2,128]{3,2,1,0:T(2,128)S(1)} %get-tuple-element.45), channel_id=1, replica_groups=mesh['gx'=16,'gy'=16] {'gx'}, dimensions={0} | all-to-all | bytes 557056 | tf_op jit(solution)/shard_map/all_to_all | solution.py:810
  52.7 3.9 %lookup.1 = f32[16,17,2,128]{3,2,1,0:T(2,128)S(1)} custom-call(bf16[16,128,1024]{2,1,0:T(8,128)(2,1)S(1)} %get-tuple-element.33.hot_ref, s32[16,8,128]{2,1,0:T(8,128)S(1)} %get-tuple-element.34.row_ref, s32[16,8,128]{2,1,0:T(8,128)S(1)} %get-tuple-element.35.lane_ref, f32[16,17,2,128]{3,2,1,0:T(2,128)S(1)} %all_to_all.16.table_ref), custom_call_target="tpu_custom_call" | custom-call | tf_op jit(solution)/shard_map/lookup/pallas_call | solution.py:811
  56.6 11.4 %all_to_all.17.got_ref = f32[16,17,2,128]{3,2,1,0:T(2,128)S(1)} all-to-all(f32[16,17,2,128]{3,2,1,0:T(2,128)S(1)} %lookup.1), channel_id=1, replica_groups=mesh['gx'=16,'gy'=16] {'gy'}, dimensions={0} | all-to-all | bytes 557056 | tf_op jit(solution)/shard_map/all_to_all | solution.py:823
  68.0 1.7 %finish.1 = (f32[32,32,128]{2,1,0:T(8,128)}, f32[8,128]{1,0:T(8,128)}) custom-call(f32[16,17,2,128]{3,2,1,0:T(2,128)S(1)} %all_to_all.17.got_ref, f32[8,128]{1,0:T(8,128)} %bitcast.4, f32[39,40,128]{2,1,0:T(8,128)S(1)} %get-tuple-element.46.t_ref, f32[39,40,128]{2,1,0:T(8,128)S(1)} %get-tuple-element.47.w0_ref, f32[39,40,128]{2,1,0:T(8,128)S(1)} %get-tuple-element.48.w1_ref, ...), custom_call_target="tpu_custom_call" | custom-call | tf_op jit(solution)/shard_map/finish/pallas_call | solution.py:824
  (1 shorter events, 0.0 us)
Async XLA Ops:
  2.2 17.9 %collective-permute-start = (f32[11,32,128]{2,1,0:T(8,128)S(1)}, f32[11,32,128]{2,1,0:T(8,128)S(1)}, u32[]{:S(2)}, u32[]{:S(2)}) collective-permute-start(f32[11,32,128]{2,1,0:T(8,128)S(1)} %get-tuple-element.27), channel_id=1, source_target_pairs={{16,32},{48,64},{80,96},{112,128},{144,160},{176,192},{208,224},{3... | collective-permute-start | bytes 540680 | tf_op jit(solution)/shard_map/ppermute | solution.py:751
  2.9 17.3 %collective-permute-start.1 = (f32[11,32,128]{2,1,0:T(8,128)S(1)}, f32[11,32,128]{2,1,0:T(8,128)S(1)}, u32[]{:S(2)}, u32[]{:S(2)}) collective-permute-start(f32[11,32,128]{2,1,0:T(8,128)S(1)} %get-tuple-element.28), channel_id=1, source_target_pairs={{0,16},{32,48},{64,80},{96,112},{128,144},{160,176},{192,208},{224... | collective-permute-start | bytes 540680 | tf_op jit(solution)/shard_map/ppermute | solution.py:752
  20.1 7.5 %collective-permute-start.2 = (f32[59,8,128]{2,1,0:T(8,128)S(1)}, f32[59,8,128]{2,1,0:T(8,128)S(1)}, u32[]{:S(2)}, u32[]{:S(2)}) collective-permute-start(f32[59,8,128]{2,1,0:T(8,128)S(1)} %get-tuple-element.43), channel_id=1, source_target_pairs={{1,2},{3,4},{5,6},{7,8},{9,10},{11,12},{13,14},{2,1},{4,3},{6,5},{... | collective-permute-start | bytes 725000 | tf_op jit(solution)/shard_map/ppermute | solution.py:766
  22.6 5.0 %collective-permute-start.3 = (f32[59,8,128]{2,1,0:T(8,128)S(1)}, f32[59,8,128]{2,1,0:T(8,128)S(1)}, u32[]{:S(2)}, u32[]{:S(2)}) collective-permute-start(f32[59,8,128]{2,1,0:T(8,128)S(1)} %get-tuple-element.44), channel_id=1, source_target_pairs={{0,1},{2,3},{4,5},{6,7},{8,9},{10,11},{12,13},{14,15},{1,0},{3,2},... | collective-permute-start | bytes 725000 | tf_op jit(solution)/shard_map/ppermute | solution.py:767

commit v10 on v9

--- a/solution.py
+++ b/solution.py
@@ -484,7 +484,7 @@
             mb = mb + fold(total[:NY] * new[:NY])
             return g, ma, mb
 
-        carry, ma, mb = lax.fori_loop(0, NX, step, (carry, zero_tile, zero_tile), unroll=8)
+        carry, ma, mb = lax.fori_loop(0, NX, step, (carry, zero_tile, zero_tile), unroll=16)
         for q, nxt in epilogue:
             total, _, carry = neighbours(src, q, nxt, carry)
             dst[q] = dinv[q] * total
@@ -588,7 +588,7 @@
         out_ref[b, PARTS * FIELDS] = total
         return 0
 
-    lax.fori_loop(0, targets, one, 0, unroll=8)
+    lax.fori_loop(0, targets, one, 0, unroll=16)
 
 
 def cg_coefficients(m):

time: 70 us -> 69.8 us (level)
  no operation moved by 1% of the time
where the time goes in v10:
time: 69.8 us; the launch traced here: 69.4 us
  blocking collectives  45.8 us (66%)
  Pallas kernels  13.4 us (19%)
  starting transfers between devices  7.98 us (11%)
  waiting for transfers between devices  1.49 us (2%)
    all_to_all x1, blocking collectives, local(): table = lax.all_to_all(send, 'gx', 0, 0)  22 us
    all_to_all x1, blocking collectives, local(): sites = lax.all_to_all(sites, 'gy', 0, 0)  12.5 us
    all_to_all x1, blocking collectives, local(): got = lax.all_to_all(found, 'gy', 0, 0)  11.4 us
    ppermute x1, starting transfers between devices, local(): xb = lax.ppermute(xb, 'gx', swaps(size_x, 0))  4.75 us
    pallas_call x1, Pallas kernels, local(): pl.pallas_call(lookup_kernel, name='lookup', in_specs=[vmem] * 4, out_spe...  3.78 us
    pallas_call x1, Pallas kernels, local(): pl.pallas_call(own_kernel, name='own_cells', in_specs=[anywhere] * 6 + [v...  3.4 us
    pallas_call x1, Pallas kernels, local(): pl.pallas_call(krylov_kernel, name='krylov', in_specs=[vmem] * 9, out_spe...  3 us
    ppermute x1, starting transfers between devices, local(): ya = lax.ppermute(ya, 'gy', swaps(size_y, 1))  2.47 us
  transfers between devices with their start and end apart: 4, of which 1 were waited for; matrix products, arithmetic and copies ran while one was open for 0% of the time, Pallas kernels for 5%

profile of v10, /device:TPU:1, one launch (start us, length us, event | category | flops | bytes accessed | tf_op | source)
XLA Modules:
  0.0 69.4 jit_solution(10987457075065840187)
XLA Ops:
  0.6 1.5 %pack.1 = (f32[11,32,128]{2,1,0:T(8,128)S(1)}, f32[11,32,128]{2,1,0:T(8,128)S(1)}, f32[59,8,128]{2,1,0:T(8,128)S(1)}, f32[59,8,128]{2,1,0:T(8,128)S(1)}, s32[16,8,128]{2,1,0:T(8,128)S(1)}) custom-call(f32[32,32,128]{2,1,0:T(8,128)} %t_hbm.3, s32[32,32,128]{2,1,0:T(8,128)} %id_hbm.3, s32[32,32,128]{2,1,0:T(8,128)} %chip_hbm.3, s32[8,128]{1,0:T(8,128)} %bitcast.3), custom_call_target="tpu_custom_call" | custom-call | tf_op jit(solution)/shard_map/pack/pallas_call | solution.py:719
  2.2 0.7 collective-permute-start
  2.9 4.7 %collective-permute-start.1 = (f32[11,32,128]{2,1,0:T(8,128)S(1)}, f32[11,32,128]{2,1,0:T(8,128)S(1)}, u32[]{:S(2)}, u32[]{:S(2)}) collective-permute-start(f32[11,32,128]{2,1,0:T(8,128)S(1)} %get-tuple-element.28), channel_id=1, source_target_pairs={{0,16},{32,48},{64,80},{96,112},{128,144},{160,176},{192,208},{224... | collective-permute-start | bytes 540680 | tf_op jit(solution)/shard_map/ppermute | solution.py:752
  7.6 12.5 %all_to_all.15.sites_in = s32[16,8,128]{2,1,0:T(8,128)S(1)} all-to-all(s32[16,8,128]{2,1,0:T(8,128)S(1)} %get-tuple-element.31), channel_id=1, replica_groups=mesh['gx'=16,'gy'=16] {'gy'}, dimensions={0} | all-to-all | bytes 131072 | tf_op jit(solution)/shard_map/all_to_all | solution.py:749
  20.1 0.0 collective-permute-done.xa_ref
  20.1 0.0 collective-permute-done.1.xb_ref
  20.1 2.5 %collective-permute-start.2 = (f32[59,8,128]{2,1,0:T(8,128)S(1)}, f32[59,8,128]{2,1,0:T(8,128)S(1)}, u32[]{:S(2)}, u32[]{:S(2)}) collective-permute-start(f32[59,8,128]{2,1,0:T(8,128)S(1)} %get-tuple-element.43), channel_id=1, source_target_pairs={{1,2},{3,4},{5,6},{7,8},{9,10},{11,12},{13,14},{2,1},{4,3},{6,5},{... | collective-permute-start | bytes 725000 | tf_op jit(solution)/shard_map/ppermute | solution.py:766
  22.6 0.1 collective-permute-start.3
  22.7 3.4 %own_cells.1 = (f32[39,40,128]{2,1,0:T(8,128)S(1)}, f32[39,40,128]{2,1,0:T(8,128)S(1)}, f32[39,40,128]{2,1,0:T(8,128)S(1)}, f32[39,40,128]{2,1,0:T(8,128)S(1)}, ...) custom-call(f32[4]{0:T(128)} %ref_hbm.1, ...), custom_call_target="tpu_custom_call" | custom-call | tf_op jit(solution)/shard_map/own_cells/pallas_call | solution.py:775
  26.1 1.5 %collective-permute-done.2.ya_ref = f32[59,8,128]{2,1,0:T(8,128)S(1)} collective-permute-done((f32[59,8,128]{2,1,0:T(8,128)S(1)}, f32[59,8,128]{2,1,0:T(8,128)S(1)}, u32[]{:S(2)}, u32[]{:S(2)}) %collective-permute-start.2) | collective-permute-done | bytes 241696 | tf_op jit(solution)/shard_map/ppermute | solution.py:766
  27.6 0.0 collective-permute-done.3.yb_ref
  27.6 3.0 %krylov.1 = (f32[39,40,128]{2,1,0:T(8,128)S(1)}, f32[39,40,128]{2,1,0:T(8,128)S(1)}, f32[39,40,128]{2,1,0:T(8,128)S(1)}, f32[39,40,128]{2,1,0:T(8,128)S(1)}, f32...) custom-call(f32[12,8,128]{2,1,0:T(8,128)S(1)} %get-tuple-element.36., ...), custom_call_target="tpu_custom_call", output_to_operand_aliasing={{0}: (1, {}), {1}: (2, {}), {2}: (3, {}), {3}: (4, {}), {4}... | custom-call | tf_op jit(solution)/shard_map/krylov/pallas_call | solution.py:800
  30.6 22.0 %all_to_all.16.table_ref = f32[16,17,2,128]{3,2,1,0:T(2,128)S(1)} all-to-all(f32[16,17,2,128]{3,2,1,0:T(2,128)S(1)} %get-tuple-element.45), channel_id=1, replica_groups=mesh['gx'=16,'gy'=16] {'gx'}, dimensions={0} | all-to-all | bytes 557056 | tf_op jit(solution)/shard_map/all_to_all | solution.py:810
  52.6 3.8 %lookup.1 = f32[16,17,2,128]{3,2,1,0:T(2,128)S(1)} custom-call(bf16[16,128,1024]{2,1,0:T(8,128)(2,1)S(1)} %get-tuple-element.33.hot_ref, s32[16,8,128]{2,1,0:T(8,128)S(1)} %get-tuple-element.34.row_ref, s32[16,8,128]{2,1,0:T(8,128)S(1)} %get-tuple-element.35.lane_ref, f32[16,17,2,128]{3,2,1,0:T(2,128)S(1)} %all_to_all.16.table_ref), custom_call_target="tpu_custom_call" | custom-call | tf_op jit(solution)/shard_map/lookup/pallas_call | solution.py:811
  56.4 11.4 %all_to_all.17.got_ref = f32[16,17,2,128]{3,2,1,0:T(2,128)S(1)} all-to-all(f32[16,17,2,128]{3,2,1,0:T(2,128)S(1)} %lookup.1), channel_id=1, replica_groups=mesh['gx'=16,'gy'=16] {'gy'}, dimensions={0} | all-to-all | bytes 557056 | tf_op jit(solution)/shard_map/all_to_all | solution.py:823
  67.8 1.7 %finish.1 = (f32[32,32,128]{2,1,0:T(8,128)}, f32[8,128]{1,0:T(8,128)}) custom-call(f32[16,17,2,128]{3,2,1,0:T(2,128)S(1)} %all_to_all.17.got_ref, f32[8,128]{1,0:T(8,128)} %bitcast.4, f32[39,40,128]{2,1,0:T(8,128)S(1)} %get-tuple-element.46.t_ref, f32[39,40,128]{2,1,0:T(8,128)S(1)} %get-tuple-element.47.w0_ref, f32[39,40,128]{2,1,0:T(8,128)S(1)} %get-tuple-element.48.w1_ref, ...), custom_call_target="tpu_custom_call" | custom-call | tf_op jit(solution)/shard_map/finish/pallas_call | solution.py:824
  (1 shorter events, 0.0 us)
Async XLA Ops:
  2.2 17.9 %collective-permute-start = (f32[11,32,128]{2,1,0:T(8,128)S(1)}, f32[11,32,128]{2,1,0:T(8,128)S(1)}, u32[]{:S(2)}, u32[]{:S(2)}) collective-permute-start(f32[11,32,128]{2,1,0:T(8,128)S(1)} %get-tuple-element.27), channel_id=1, source_target_pairs={{16,32},{48,64},{80,96},{112,128},{144,160},{176,192},{208,224},{3... | collective-permute-start | bytes 540680 | tf_op jit(solution)/shard_map/ppermute | solution.py:751
  2.9 17.3 %collective-permute-start.1 = (f32[11,32,128]{2,1,0:T(8,128)S(1)}, f32[11,32,128]{2,1,0:T(8,128)S(1)}, u32[]{:S(2)}, u32[]{:S(2)}) collective-permute-start(f32[11,32,128]{2,1,0:T(8,128)S(1)} %get-tuple-element.28), channel_id=1, source_target_pairs={{0,16},{32,48},{64,80},{96,112},{128,144},{160,176},{192,208},{224... | collective-permute-start | bytes 540680 | tf_op jit(solution)/shard_map/ppermute | solution.py:752
  20.1 7.5 %collective-permute-start.2 = (f32[59,8,128]{2,1,0:T(8,128)S(1)}, f32[59,8,128]{2,1,0:T(8,128)S(1)}, u32[]{:S(2)}, u32[]{:S(2)}) collective-permute-start(f32[59,8,128]{2,1,0:T(8,128)S(1)} %get-tuple-element.43), channel_id=1, source_target_pairs={{1,2},{3,4},{5,6},{7,8},{9,10},{11,12},{13,14},{2,1},{4,3},{6,5},{... | collective-permute-start | bytes 725000 | tf_op jit(solution)/shard_map/ppermute | solution.py:766
  22.6 5.0 %collective-permute-start.3 = (f32[59,8,128]{2,1,0:T(8,128)S(1)}, f32[59,8,128]{2,1,0:T(8,128)S(1)}, u32[]{:S(2)}, u32[]{:S(2)}) collective-permute-start(f32[59,8,128]{2,1,0:T(8,128)S(1)} %get-tuple-element.44), channel_id=1, source_target_pairs={{0,1},{2,3},{4,5},{6,7},{8,9},{10,11},{12,13},{14,15},{1,0},{3,2},... | collective-permute-start | bytes 725000 | tf_op jit(solution)/shard_map/ppermute | solution.py:767

commit v11 on v9

--- a/solution.py
+++ b/solution.py
@@ -20,7 +20,7 @@
 PY = NY + 8
 FIELDS = 4
 TILE = 8
-PART = 2
+PART = 1
 PARTS = TILE // PART
 BLOCK = PARTS * FIELDS + 1
 PAIRS = 20
@@ -594,15 +594,22 @@
 def cg_coefficients(m):
     a = [m[j] - m[j + 1] for j in range(5)]
 
+    def product(*factors):
+        out = None
+        for e in factors:
+            if e is None:
+                return None
+            out = e if out is None else out * e
+        return out
+
     def quadratic(v, h):
-        total = None
-        for i in range(3):
-            for j in range(3):
-                if v[i] is None or v[j] is None:
-                    continue
-                term = v[i] * v[j] * h[i + j]
-                total = term if total is None else total + term
-        return total
+        v0, v1, v2 = v
+        twice = None if v0 is None else v0 + v0
+        cross = None if v1 is None else v1 + v1
+        left = add(product(v0, v0, h[0]), product(twice, v1, h[1]))
+        middle = product(add(product(twice, v2), product(v1, v1)), h[2])
+        right = add(product(cross, v2, h[3]), product(v2, v2, h[4]))
+        return add(add(left, middle), right)
 
     def add(u, v):
         return v if u is None else u if v is None else u + v

time: 70 us -> 69.9 us (level)
  no operation moved by 1% of the time
where the time goes in v11:
time: 69.9 us; the launch traced here: 69.6 us
  blocking collectives  45.7 us (65%)
  Pallas kernels  13.8 us (20%)
  starting transfers between devices  7.98 us (11%)
  waiting for transfers between devices  1.49 us (2%)
    all_to_all x1, blocking collectives, local(): table = lax.all_to_all(send, 'gx', 0, 0)  21.9 us
    all_to_all x1, blocking collectives, local(): sites = lax.all_to_all(sites, 'gy', 0, 0)  12.5 us
    all_to_all x1, blocking collectives, local(): got = lax.all_to_all(found, 'gy', 0, 0)  11.3 us
    ppermute x1, starting transfers between devices, local(): xb = lax.ppermute(xb, 'gx', swaps(size_x, 0))  4.75 us
    pallas_call x1, Pallas kernels, local(): pl.pallas_call(lookup_kernel, name='lookup', in_specs=[vmem] * 4, out_spe...  3.95 us
    pallas_call x1, Pallas kernels, local(): pl.pallas_call(own_kernel, name='own_cells', in_specs=[anywhere] * 6 + [v...  3.4 us
    pallas_call x1, Pallas kernels, local(): pl.pallas_call(krylov_kernel, name='krylov', in_specs=[vmem] * 9, out_spe...  3.14 us
    ppermute x1, starting transfers between devices, local(): ya = lax.ppermute(ya, 'gy', swaps(size_y, 1))  2.47 us
  transfers between devices with their start and end apart: 4, of which 1 were waited for; matrix products, arithmetic and copies ran while one was open for 0% of the time, Pallas kernels for 5%

profile of v11, /device:TPU:1, one launch (start us, length us, event | category | flops | bytes accessed | tf_op | source)
XLA Modules:
  0.0 69.6 jit_solution(554746990936542093)
XLA Ops:
  0.6 1.5 %pack.1 = (f32[11,32,128]{2,1,0:T(8,128)S(1)}, f32[11,32,128]{2,1,0:T(8,128)S(1)}, f32[59,8,128]{2,1,0:T(8,128)S(1)}, f32[59,8,128]{2,1,0:T(8,128)S(1)}, s32[16,8,128]{2,1,0:T(8,128)S(1)}) custom-call(f32[32,32,128]{2,1,0:T(8,128)} %t_hbm.3, s32[32,32,128]{2,1,0:T(8,128)} %id_hbm.3, s32[32,32,128]{2,1,0:T(8,128)} %chip_hbm.3, s32[8,128]{1,0:T(8,128)} %bitcast.3), custom_call_target="tpu_custom_call" | custom-call | tf_op jit(solution)/shard_map/pack/pallas_call | solution.py:726
  2.2 0.7 collective-permute-start
  2.9 4.7 %collective-permute-start.1 = (f32[11,32,128]{2,1,0:T(8,128)S(1)}, f32[11,32,128]{2,1,0:T(8,128)S(1)}, u32[]{:S(2)}, u32[]{:S(2)}) collective-permute-start(f32[11,32,128]{2,1,0:T(8,128)S(1)} %get-tuple-element.28), channel_id=1, source_target_pairs={{0,16},{32,48},{64,80},{96,112},{128,144},{160,176},{192,208},{224... | collective-permute-start | bytes 540680 | tf_op jit(solution)/shard_map/ppermute | solution.py:759
  7.6 12.5 %all_to_all.15.sites_in = s32[16,8,128]{2,1,0:T(8,128)S(1)} all-to-all(s32[16,8,128]{2,1,0:T(8,128)S(1)} %get-tuple-element.31), channel_id=1, replica_groups=mesh['gx'=16,'gy'=16] {'gy'}, dimensions={0} | all-to-all | bytes 131072 | tf_op jit(solution)/shard_map/all_to_all | solution.py:756
  20.1 0.0 collective-permute-done.xa_ref
  20.1 0.0 collective-permute-done.1.xb_ref
  20.1 2.5 %collective-permute-start.2 = (f32[59,8,128]{2,1,0:T(8,128)S(1)}, f32[59,8,128]{2,1,0:T(8,128)S(1)}, u32[]{:S(2)}, u32[]{:S(2)}) collective-permute-start(f32[59,8,128]{2,1,0:T(8,128)S(1)} %get-tuple-element.43), channel_id=1, source_target_pairs={{1,2},{3,4},{5,6},{7,8},{9,10},{11,12},{13,14},{2,1},{4,3},{6,5},{... | collective-permute-start | bytes 725000 | tf_op jit(solution)/shard_map/ppermute | solution.py:773
  22.6 0.1 collective-permute-start.3
  22.7 3.4 %own_cells.1 = (f32[39,40,128]{2,1,0:T(8,128)S(1)}, f32[39,40,128]{2,1,0:T(8,128)S(1)}, f32[39,40,128]{2,1,0:T(8,128)S(1)}, f32[39,40,128]{2,1,0:T(8,128)S(1)}, ...) custom-call(f32[4]{0:T(128)} %ref_hbm.1, ...), custom_call_target="tpu_custom_call" | custom-call | tf_op jit(solution)/shard_map/own_cells/pallas_call | solution.py:782
  26.1 1.5 %collective-permute-done.2.ya_ref = f32[59,8,128]{2,1,0:T(8,128)S(1)} collective-permute-done((f32[59,8,128]{2,1,0:T(8,128)S(1)}, f32[59,8,128]{2,1,0:T(8,128)S(1)}, u32[]{:S(2)}, u32[]{:S(2)}) %collective-permute-start.2) | collective-permute-done | bytes 241696 | tf_op jit(solution)/shard_map/ppermute | solution.py:773
  27.6 0.0 collective-permute-done.3.yb_ref
  27.6 3.1 %krylov.1 = (f32[39,40,128]{2,1,0:T(8,128)S(1)}, f32[39,40,128]{2,1,0:T(8,128)S(1)}, f32[39,40,128]{2,1,0:T(8,128)S(1)}, f32[39,40,128]{2,1,0:T(8,128)S(1)}, f32...) custom-call(f32[12,8,128]{2,1,0:T(8,128)S(1)} %get-tuple-element.36., ...), custom_call_target="tpu_custom_call", output_to_operand_aliasing={{0}: (1, {}), {1}: (2, {}), {2}: (3, {}), {3}: (4, {}), {4}... | custom-call | tf_op jit(solution)/shard_map/krylov/pallas_call | solution.py:807
  30.8 21.9 %all_to_all.16.table_ref = f32[16,33,1,128]{3,2,1,0:T(1,128)S(1)} all-to-all(f32[16,33,1,128]{3,2,1,0:T(1,128)S(1)} %get-tuple-element.45), channel_id=1, replica_groups=mesh['gx'=16,'gy'=16] {'gx'}, dimensions={0} | all-to-all | bytes 540672 | tf_op jit(solution)/shard_map/all_to_all | solution.py:817
  52.7 4.0 %lookup.1 = f32[16,33,1,128]{3,2,1,0:T(1,128)S(1)} custom-call(bf16[16,128,1024]{2,1,0:T(8,128)(2,1)S(1)} %get-tuple-element.33.hot_ref, s32[16,8,128]{2,1,0:T(8,128)S(1)} %get-tuple-element.34.row_ref, s32[16,8,128]{2,1,0:T(8,128)S(1)} %get-tuple-element.35.lane_ref, f32[16,33,1,128]{3,2,1,0:T(1,128)S(1)} %all_to_all.16.table_ref), custom_call_target="tpu_custom_call" | custom-call | tf_op jit(solution)/shard_map/lookup/pallas_call | solution.py:818
  56.6 11.3 %all_to_all.17.got_ref = f32[16,33,1,128]{3,2,1,0:T(1,128)S(1)} all-to-all(f32[16,33,1,128]{3,2,1,0:T(1,128)S(1)} %lookup.1), channel_id=1, replica_groups=mesh['gx'=16,'gy'=16] {'gy'}, dimensions={0} | all-to-all | bytes 540672 | tf_op jit(solution)/shard_map/all_to_all | solution.py:830
  67.9 1.7 %finish.1 = (f32[32,32,128]{2,1,0:T(8,128)}, f32[8,128]{1,0:T(8,128)}) custom-call(f32[16,33,1,128]{3,2,1,0:T(1,128)S(1)} %all_to_all.17.got_ref, f32[8,128]{1,0:T(8,128)} %bitcast.4, f32[39,40,128]{2,1,0:T(8,128)S(1)} %get-tuple-element.46.t_ref, f32[39,40,128]{2,1,0:T(8,128)S(1)} %get-tuple-element.47.w0_ref, f32[39,40,128]{2,1,0:T(8,128)S(1)} %get-tuple-element.48.w1_ref, ...), custom_call_target="tpu_custom_call" | custom-call | tf_op jit(solution)/shard_map/finish/pallas_call | solution.py:831
  (1 shorter events, 0.0 us)
Async XLA Ops:
  2.2 17.9 %collective-permute-start = (f32[11,32,128]{2,1,0:T(8,128)S(1)}, f32[11,32,128]{2,1,0:T(8,128)S(1)}, u32[]{:S(2)}, u32[]{:S(2)}) collective-permute-start(f32[11,32,128]{2,1,0:T(8,128)S(1)} %get-tuple-element.27), channel_id=1, source_target_pairs={{16,32},{48,64},{80,96},{112,128},{144,160},{176,192},{208,224},{3... | collective-permute-start | bytes 540680 | tf_op jit(solution)/shard_map/ppermute | solution.py:758
  2.9 17.3 %collective-permute-start.1 = (f32[11,32,128]{2,1,0:T(8,128)S(1)}, f32[11,32,128]{2,1,0:T(8,128)S(1)}, u32[]{:S(2)}, u32[]{:S(2)}) collective-permute-start(f32[11,32,128]{2,1,0:T(8,128)S(1)} %get-tuple-element.28), channel_id=1, source_target_pairs={{0,16},{32,48},{64,80},{96,112},{128,144},{160,176},{192,208},{224... | collective-permute-start | bytes 540680 | tf_op jit(solution)/shard_map/ppermute | solution.py:759
  20.1 7.5 %collective-permute-start.2 = (f32[59,8,128]{2,1,0:T(8,128)S(1)}, f32[59,8,128]{2,1,0:T(8,128)S(1)}, u32[]{:S(2)}, u32[]{:S(2)}) collective-permute-start(f32[59,8,128]{2,1,0:T(8,128)S(1)} %get-tuple-element.43), channel_id=1, source_target_pairs={{1,2},{3,4},{5,6},{7,8},{9,10},{11,12},{13,14},{2,1},{4,3},{6,5},{... | collective-permute-start | bytes 725000 | tf_op jit(solution)/shard_map/ppermute | solution.py:773
  22.6 5.0 %collective-permute-start.3 = (f32[59,8,128]{2,1,0:T(8,128)S(1)}, f32[59,8,128]{2,1,0:T(8,128)S(1)}, u32[]{:S(2)}, u32[]{:S(2)}) collective-permute-start(f32[59,8,128]{2,1,0:T(8,128)S(1)} %get-tuple-element.44), channel_id=1, source_target_pairs={{0,1},{2,3},{4,5},{6,7},{8,9},{10,11},{12,13},{14,15},{1,0},{3,2},... | collective-permute-start | bytes 725000 | tf_op jit(solution)/shard_map/ppermute | solution.py:774
